TPU v7x, 32 devices: a whole 2x2x4 slice. The times are simulated.
32 devices in a mesh: kv: 2 (over y), ex: 16 (over z, x, core).
Axes of the slice: x: 2, y: 2, z: 4, core: 2. Of those that a mesh axis runs over, the one named last changes fastest.
Arguments:
- x_tokens: bfloat16 [16, 576, 2048], P('ex'), may hold values from -6 to 6
- attn_gain: float32 [2048], replicated, may hold values from 0.1 to 1.9
- w_qkv: bfloat16 [2048, 3, 2048], P(None, None, 'kv'), may hold values from -1 to 1
- w_out: bfloat16 [2048, 2048], P('kv'), may hold values from -0.125 to 0.125
- cache: bfloat16 [32, 2, 512, 2048], P('ex', None, None, 'kv'), may hold values from -6 to 6
- cache_len: int32 [32], P('ex'), may hold values from 1 to 512, 8192 in all
- moe_gain: float32 [2048], replicated, may hold values from 0.1 to 1.9
- w_trainer: float32 [16, 3, 2048, 1024], P(None, None, 'ex', 'kv'), may hold values from -0.125 to 0.125
- expert_ids: int32 [16, 576, 8], P('ex', 'kv'), may hold values from 0 to 15, all different within a row; in each aligned block of 288 rows (0 to 287, 288 to 575, ..., all dimensions but the last counted through in order) at most 230 rows name the same one
- route_probs: float32 [16, 576, 8], P('ex', 'kv'), may hold values from 0.05 to 1
Outputs:
- layer_out: bfloat16 [16, 576, 2048], P('ex', 'kv')
Inputs may be any that keep to these rules, and one draw needn't show every extreme that they name: `expert_ids`: in each aligned block of 288 tokens, no expert is named by more than 230 of them; each token names 8 different experts.
All inputs are finite; a program needn't handle non-finite values. No bound on the sum of `cache_len` on one device may be relied on, other than what follows from the above.
Results may differ from a plain program's by a relative error of at most 0.0055.
Values may be sent and summed in bfloat16 or wider, within the bound.
No kernel may reach another device: no remote copies, remote signals or barrier semaphores. Data moves between devices by JAX's collectives and lax.ppermute only.
A program may use at most 192 MiB of HBM per device.

v0:
```python
import functools
import math

import jax
import jax.numpy as jnp
from jax import lax
from jax.experimental import pallas as pl
from jax.experimental.pallas import tpu as pltpu
from jax.sharding import PartitionSpec as P

HD = 128
TOPK = 8
PLEN = 512
REQ_DEV = 2
QB = 32
CMAX = 512


def rms_scale(rows, gain):
    values = rows.astype(jnp.float32)
    scale = lax.rsqrt(jnp.mean(values * values, axis=-1, keepdims=True) + 1e-06)
    return values * scale * gain


def attention_kernel(scale, len_ref, x_ref, gain_ref, w_ref, cache_ref, w_out_ref, out_ref, normed):
    @pl.when(pl.program_id(0) == 0)
    def _():
        normed[...] = rms_scale(x_ref[...], gain_ref[...]).astype(jnp.bfloat16)
        out_ref[...] = jnp.zeros_like(out_ref)

    rows = normed[...]
    query, keys, values = (
        jnp.dot(rows, w_ref[j], preferred_element_type=jnp.float32).astype(jnp.bfloat16)
        for j in range(3)
    )

    def scores_of(q, k):
        return scale * lax.dot_general(
            q, k, (((1,), (1,)), ((), ())), preferred_element_type=jnp.float32
        )

    def mix(weights, v):
        return jnp.dot(weights.astype(jnp.bfloat16), v, preferred_element_type=jnp.float32)

    heads = []
    for head in range(query.shape[1] // HD):
        cut = slice(head * HD, (head + 1) * HD)
        q, k, v = query[:, cut], keys[:, cut], values[:, cut]
        scores = scores_of(q[:PLEN], k[:PLEN])
        weights = jnp.exp(scores - jnp.max(scores, axis=-1, keepdims=True))
        total = jnp.sum(weights, axis=-1, keepdims=True)
        outs = [(mix(weights, v[:PLEN]) / total).astype(jnp.bfloat16)]
        for request in range(REQ_DEV):
            own = slice(PLEN + request * QB, PLEN + (request + 1) * QB)
            fresh = scores_of(q[own], k[own])
            stored = scores_of(q[own], cache_ref[request, 0, :, cut])
            slots = lax.broadcasted_iota(jnp.int32, stored.shape, 1)
            stored = jnp.where(slots < len_ref[request], stored, -1e30)
            top = jnp.maximum(
                jnp.max(fresh, axis=-1, keepdims=True), jnp.max(stored, axis=-1, keepdims=True)
            )
            fresh, stored = jnp.exp(fresh - top), jnp.exp(stored - top)
            total = jnp.sum(fresh, axis=-1, keepdims=True) + jnp.sum(stored, axis=-1, keepdims=True)
            mixed = mix(fresh, v[own]) + mix(stored, cache_ref[request, 1, :, cut])
            outs.append((mixed / total).astype(jnp.bfloat16))
        heads.append(jnp.concatenate(outs, axis=0))
    out_ref[...] += jnp.dot(
        jnp.concatenate(heads, axis=1), w_out_ref[...], preferred_element_type=jnp.float32
    )


def attention(rows, gain, w_qkv, cache, cache_len, w_out):
    count, width = rows.shape
    units = w_qkv.shape[2]
    block = min(2 * HD, units)
    return pl.pallas_call(
        functools.partial(attention_kernel, 1.0 / math.sqrt(HD)),
        grid=(units // block,),
        in_specs=[
            pl.BlockSpec(memory_space=pltpu.SMEM),
            pl.BlockSpec((count, width), lambda i: (0, 0)),
            pl.BlockSpec((1, width), lambda i: (0, 0)),
            pl.BlockSpec((3, width, block), lambda i: (0, 0, i)),
            pl.BlockSpec((REQ_DEV, 2, CMAX, block), lambda i: (0, 0, 0, i)),
            pl.BlockSpec((block, width), lambda i: (i, 0)),
        ],
        out_specs=pl.BlockSpec((count, width), lambda i: (0, 0)),
        out_shape=jax.ShapeDtypeStruct((count, width), jnp.float32),
        scratch_shapes=[pltpu.VMEM((count, width), jnp.bfloat16)],
        compiler_params=pltpu.CompilerParams(vmem_limit_bytes=48 * 1024 * 1024),
        cost_estimate=pl.CostEstimate(
            flops=8 * count * width * units + 4 * PLEN * PLEN * units,
            bytes_accessed=8 * width * units + 6 * count * width,
            transcendentals=PLEN * PLEN * units // HD,
        ),
        name="attention",
    )(cache_len, rows, gain[None], jnp.transpose(w_qkv, (1, 0, 2)), cache, w_out)


def share_columns(share):
    high = share.astype(jnp.bfloat16)
    low = (share - high.astype(jnp.float32)).astype(jnp.bfloat16)
    spare = -2 * share.shape[1] % 128
    return jnp.concatenate([high, low, jnp.zeros((share.shape[0], spare), jnp.bfloat16)], axis=1)


def hidden_kernel(experts, width, me_ref, *refs):
    x_refs, weight_refs, out_refs = refs[:2], refs[2:-2], refs[-2:]
    units = weight_refs[0].shape[2]
    me = me_ref[0]
    for x_ref, out_ref in zip(x_refs, out_refs):
        extra = x_ref[:, width:].astype(jnp.float32)
        lanes = lax.broadcasted_iota(jnp.int32, extra.shape, 1)
        mine = (lanes == me) | (lanes == me + experts)
        share = jnp.sum(jnp.where(mine, extra, 0.0), axis=-1, keepdims=True)
        for part in range(len(weight_refs) // 2):
            gate_w, up_w = (r[...].reshape(width, units) for r in weight_refs[2 * part : 2 * part + 2])
            x = x_ref[:, :width]
            gate = jnp.dot(x, gate_w, preferred_element_type=jnp.float32)
            up = jnp.dot(x, up_w, preferred_element_type=jnp.float32)
            out_ref[:, part * units : (part + 1) * units] = (
                gate * jax.nn.sigmoid(gate) * up * share
            ).astype(jnp.bfloat16)


def expert_hidden(experts, me, blocks, weights):
    count = blocks[0].shape[0]
    sources, slice_width, units = weights[0].shape
    width, hidden = sources * slice_width, units * len(weights) // 2
    vmem = pl.BlockSpec(memory_space=pltpu.VMEM)
    out = jax.ShapeDtypeStruct((count, hidden), jnp.bfloat16)
    return pl.pallas_call(
        functools.partial(hidden_kernel, experts, width),
        in_specs=[pl.BlockSpec(memory_space=pltpu.SMEM)] + [vmem] * (2 + len(weights)),
        out_specs=[vmem] * 2,
        out_shape=[out, out],
        compiler_params=pltpu.CompilerParams(vmem_limit_bytes=16 * 1024 * 1024),
        cost_estimate=pl.CostEstimate(
            flops=8 * count * width * hidden,
            bytes_accessed=4 * count * (width + hidden) + 4 * width * hidden,
            transcendentals=2 * count * hidden,
        ),
        name="expert_hidden",
    )(me, *blocks, *weights)


def down_kernel(*refs):
    hidden_refs, weight_refs, out_refs = refs[:2], refs[2:-2], refs[-2:]
    sources, slice_width, units = weight_refs[0].shape
    group = max(1, min(sources, 1024 // slice_width))
    for hidden_ref, out_ref in zip(hidden_refs, out_refs):
        for first in range(0, sources, group):
            total = None
            for part, weight_ref in enumerate(weight_refs):
                term = lax.dot_general(
                    hidden_ref[:, part * units : (part + 1) * units],
                    weight_ref[first : first + group].reshape(group * slice_width, units),
                    (((1,), (1,)), ((), ())),
                    preferred_element_type=jnp.float32,
                )
                total = term if total is None else total + term
            cut = slice(first * slice_width, (first + group) * slice_width)
            out_ref[:, cut] = total.astype(jnp.bfloat16)


def expert_down(hiddens, weights):
    count, hidden = hiddens[0].shape
    width = weights[0].shape[0] * weights[0].shape[1]
    vmem = pl.BlockSpec(memory_space=pltpu.VMEM)
    out = jax.ShapeDtypeStruct((count, width), jnp.bfloat16)
    return pl.pallas_call(
        down_kernel,
        in_specs=[vmem] * (2 + len(weights)),
        out_specs=[vmem] * 2,
        out_shape=[out, out],
        compiler_params=pltpu.CompilerParams(vmem_limit_bytes=16 * 1024 * 1024),
        cost_estimate=pl.CostEstimate(
            flops=4 * count * width * hidden,
            bytes_accessed=4 * count * (width + hidden) + 2 * width * hidden,
            transcendentals=0,
        ),
        name="expert_down",
    )(*hiddens, *weights)


def sum_kernel(cut, refs):
    total = refs[0][:, cut].astype(jnp.float32) + refs[1][:, cut].astype(jnp.float32)
    for ref in refs[2:-1]:
        total = total + ref[...].astype(jnp.float32)
    refs[-1][...] = total.astype(jnp.bfloat16)


def add_terms(cut, keep, got, running):
    terms = [keep, got] + ([] if running is None else [running])
    columns = cut.stop - cut.start
    vmem = pl.BlockSpec(memory_space=pltpu.VMEM)
    return pl.pallas_call(
        lambda *refs: sum_kernel(cut, refs),
        in_specs=[vmem] * len(terms),
        out_specs=vmem,
        out_shape=jax.ShapeDtypeStruct((keep.shape[0], columns), jnp.bfloat16),
        compiler_params=pltpu.CompilerParams(vmem_limit_bytes=16 * 1024 * 1024),
        cost_estimate=pl.CostEstimate(
            flops=2 * keep.shape[0] * columns,
            bytes_accessed=8 * keep.shape[0] * columns,
            transcendentals=0,
        ),
        name="add_terms",
    )(*terms)


def chip_ring(chips):
    rows = 4
    columns = chips // rows
    if chips % rows or columns < 2:
        return list(range(chips))
    order = [z * columns for z in range(rows)]
    for turn, z in enumerate(reversed(range(rows))):
        line = [z * columns + x for x in range(1, columns)]
        order += line if turn % 2 == 0 else line[::-1]
    return order


def on_device(
    x_tokens,
    attn_gain,
    w_qkv,
    w_out,
    cache,
    cache_len,
    moe_gain,
    w_trainer,
    expert_ids,
    route_probs,
):
    kv, ex = lax.axis_size("kv"), lax.axis_size("ex")
    me, me_kv = lax.axis_index("ex"), lax.axis_index("kv")
    experts = w_trainer.shape[0]

    def over_experts(part):
        return lax.all_to_all(part, "ex", split_axis=0, concat_axis=0, tiled=True)

    def over_kv(part):
        return [
            lax.ppermute(part, "kv", [(i, (i + turn) % kv) for i in range(kv)])
            for turn in range(1, kv)
        ]

    probs = route_probs[0]
    share = probs / jnp.sum(probs, axis=-1, keepdims=True)
    named = expert_ids[0][:, :, None] == jnp.arange(experts, dtype=jnp.int32)[None, None, :]
    factor = jnp.sum(jnp.where(named, share[:, :, None], 0.0), axis=1)
    factor = share_columns(factor)

    rows = x_tokens[0]
    row_count = rows.shape[0]
    rows_dev = row_count // kv
    gate, up, down = (w_trainer[:, kind].astype(jnp.bfloat16) for kind in range(3))
    gate = over_experts(gate)
    mixed = attention(rows, attn_gain, w_qkv, cache, cache_len, w_out)
    mixed, gate, up, down = lax.optimization_barrier((mixed, gate, up, down))
    gates = over_kv(gate)
    up = over_experts(up)
    mixed = mixed.reshape(kv, rows_dev, mixed.shape[1])

    def rows_of(part):
        return lax.dynamic_index_in_dim(mixed, part, 0, keepdims=False)

    own_rows = lax.dynamic_slice_in_dim(rows, me_kv * rows_dev, rows_dev, 0)
    resid = own_rows.astype(jnp.float32) + rows_of(me_kv)
    for turn in range(1, kv):
        sent = rows_of(lax.rem(me_kv + turn, kv)).astype(jnp.bfloat16)
        sent = lax.ppermute(sent, "kv", [(i, (i + turn) % kv) for i in range(kv)])
        resid = resid + sent.astype(jnp.float32)
    moe_in = rms_scale(resid, moe_gain).astype(jnp.bfloat16)
    moe_in = jnp.concatenate([moe_in, factor], axis=1)
    moe_in, gates, up, down = lax.optimization_barrier((moe_in, gates, up, down))
    ups = over_kv(up)
    down = over_experts(down)

    cores = 2
    order = chip_ring(ex // cores)
    chips = len(order)
    half = rows_dev // 2
    core = lax.rem(me, cores)
    ring, swap = [], [(i, i ^ 1) for i in range(ex)]
    for spot, chip in enumerate(order):
        for c in range(cores):
            here = chip * cores + c
            ring.append((here, order[(spot + 1 - 2 * c) % chips] * cores + c))

    def half_of(array, which):
        return lax.dynamic_slice_in_dim(array, which * half, half, 0)

    got = lax.ppermute(half_of(moe_in, 1 - core), "ex", swap)
    held = jnp.concatenate([half_of(moe_in, core), got], axis=0)
    blocks = [held]
    for step in range(1, chips):
        held = lax.ppermute(held, "ex", ring)
        if step == min(2, chips - 1):
            held, ups, down = lax.optimization_barrier((held, ups, down))
            downs = over_kv(down)
        blocks.append(held)

    first_weights = [gate, up]
    for turn in range(kv - 1):
        first_weights += [gates[turn], ups[turn]]
    hiddens = []
    for block in blocks:
        other = lax.ppermute(block, "ex", swap)
        hiddens.append(expert_hidden(experts, me[None], [block, other], first_weights))
    ahead = chips
    hiddens[:ahead], downs = lax.optimization_barrier((hiddens[:ahead], downs))
    keeps, gots = [], []
    for pair in hiddens:
        keep, give = expert_down(pair, [down] + downs)
        keeps.append(keep)
        gots.append(lax.ppermute(give, "ex", swap))

    width = w_out.shape[1]
    sums = []
    for cut in (slice(0, width // 2), slice(width // 2, width)):
        running = None
        for step in list(range(1, chips)) + [0]:
            running = add_terms(cut, keeps[step], gots[step], running)
            if step:
                running = lax.ppermute(running, "ex", ring)
        sums.append(running)
    running = jnp.concatenate(sums, axis=1)
    got = lax.ppermute(running[half:], "ex", swap)
    moe_out = jnp.where(
        core == 0,
        jnp.concatenate([running[:half], got], axis=0),
        jnp.concatenate([got, running[:half]], axis=0),
    )
    return (resid + moe_out.astype(jnp.float32)).astype(jnp.bfloat16)[None]


def solution(mesh):
    return jax.shard_map(
        on_device,
        mesh=mesh,
        in_specs=(
            P("ex", None, None),
            P(),
            P(None, None, "kv"),
            P("kv", None),
            P("ex", None, None, "kv"),
            P("ex"),
            P(),
            P(None, None, "ex", "kv"),
            P("ex", "kv", None),
            P("ex", "kv", None),
        ),
        out_specs=P("ex", "kv", None),
        check_vma=False,
    )
```

profile of v0, /device:TPU:0, one launch (start us, length us, event | category | flops | bytes accessed | tf_op | source)
XLA Modules:
  0.0 460.7 jit_solution(17282966142337214663)
XLA Ops:
  0.0 7.6 %slice_bitcast_fusion = (bf16[16,128,512]{2,1,0:T(8,128)(2,1)}, bf16[16,128,512]{2,1,0:T(8,128)(2,1)}, bf16[16,128,512]{2,1,0:T(8,128)(2,1)}) fusion(f32[16,3,128,512]{3,2,1,0:T(8,128)} %param.17), kind=kLoop, calls=%fused_computation.6 | loop fusion | bytes 12582912 | tf_op jit(solution)/shard_map/convert_element_type | solution.py:258
  7.6 7.5 %all-to-all-start = ((bf16[16,128,512]{2,1,0:T(8,128)(2,1)}), bf16[16,128,512]{2,1,0:T(8,128)(2,1)S(1)}, u32[]{:S(2)}, u32[]{:S(2)}) async-start(bf16[16,128,512]{2,1,0:T(8,128)(2,1)} %get-tuple-element.129), calls=%async_computation | async-start | bytes 4194304 | tf_op jit(solution)/shard_map/all_to_all | solution.py:241
  16.8 26.3 %attention.1 = f32[576,2048]{1,0:T(8,128)} custom-call(s32[2]{0:T(128)S(1)} %copy-done.9, bf16[576,2048]{1,0:T(8,128)(2,1)S(1)} %bitcast.21, f32[1,2048]{1,0:T(1,128)S(1)} %bitcast.22, bf16[3,2048,1024]{2,1,0:T(8,128)(2,1)} %bitcast.26, bf16[2,2,512,1024]{3,2,1,0:T(8,128)(2,1)} %cache_ref.1, bf16[1024,2048]{1,0:T(8,128)(2,1)} %w_out_ref.1), custom_call_target="tpu_custom_call" | custom-call | flops 10737418240 | bytes 23855104 | tf_op jit(solution)/shard_map/attention/pallas_call | solution.py:76
  43.1 13.1 %all-to-all-done.refs_2_ = bf16[16,128,512]{2,1,0:T(8,128)(2,1)S(1)} async-done(((bf16[16,128,512]{2,1,0:T(8,128)(2,1)}), bf16[16,128,512]{2,1,0:T(8,128)(2,1)S(1)}, u32[]{:S(2)}, u32[]{:S(2)}) %all-to-all-start) | async-done | bytes 2097184 | tf_op jit(solution)/shard_map/all_to_all | solution.py:241
  56.2 11.3 %all-to-all-start.1 = ((bf16[16,128,512]{2,1,0:T(8,128)(2,1)}), bf16[16,128,512]{2,1,0:T(8,128)(2,1)}, u32[]{:S(2)}, u32[]{:S(2)}) async-start(bf16[16,128,512]{2,1,0:T(8,128)(2,1)} %get-tuple-element.67), calls=%async_computation.1 | async-start | bytes 4194304 | tf_op jit(solution)/shard_map/all_to_all | solution.py:241
  74.1 24.2 %collective-permute-done = bf16[288,2048]{1,0:T(8,128)(2,1)} collective-permute-done((bf16[288,2048]{1,0:T(8,128)(2,1)S(1)}, bf16[288,2048]{1,0:T(8,128)(2,1)}, u32[]{:S(2)}, u32[]{:S(2)}) %collective-permute-start) | collective-permute-done | bytes 1179680 | tf_op jit(solution)/shard_map/ppermute | solution.py:273
  98.3 2.9 multiply_reduce_fusion
  105.2 37.5 %collective-permute-done.1.refs_4_ = bf16[16,128,512]{2,1,0:T(8,128)(2,1)} collective-permute-done((bf16[16,128,512]{2,1,0:T(8,128)(2,1)S(1)}, bf16[16,128,512]{2,1,0:T(8,128)(2,1)}, u32[]{:S(2)}, u32[]{:S(2)}) %collective-permute-start.1) | collective-permute-done | bytes 2097184 | tf_op jit(solution)/shard_map/ppermute | solution.py:245
  142.7 5.8 %all-to-all-start.2 = ((bf16[16,128,512]{2,1,0:T(8,128)(2,1)}), bf16[16,128,512]{2,1,0:T(8,128)(2,1)S(1)}, u32[]{:S(2)}, u32[]{:S(2)}) async-start(bf16[16,128,512]{2,1,0:T(8,128)(2,1)} %get-tuple-element.72), calls=%async_computation.2 | async-start | bytes 4194304 | tf_op jit(solution)/shard_map/all_to_all | solution.py:241
  154.3 42.5 %collective-permute-done.4.refs_0_ = bf16[288,2176]{1,0:T(8,128)(2,1)S(1)} collective-permute-done((bf16[288,2176]{1,0:T(8,128)(2,1)S(1)}, bf16[288,2176]{1,0:T(8,128)(2,1)S(1)}, u32[]{:S(2)}, u32[]{:S(2)}) %collective-permute-start.4) | collective-permute-done | bytes 1253408 | tf_op jit(solution)/shard_map/ppermute | solution.py:299
  196.8 12.9 %collective-permute-start.5 = (bf16[288,2176]{1,0:T(8,128)(2,1)S(1)}, bf16[288,2176]{1,0:T(8,128)(2,1)}, u32[]{:S(2)}, u32[]{:S(2)}) collective-permute-start(bf16[288,2176]{1,0:T(8,128)(2,1)S(1)} %collective-permute-done.4.refs_0_), channel_id=1, source_target_pairs={{0,4},{1,3},{4,8},{5,1},{8,12},{9,5},{12,14},{13,9},{14,10},{15,13... | collective-permute-start | bytes 3760136 | tf_op jit(solution)/shard_map/ppermute | solution.py:299
  211.1 13.1 %collective-permute-done.5.refs_0_ = bf16[288,2176]{1,0:T(8,128)(2,1)} collective-permute-done((bf16[288,2176]{1,0:T(8,128)(2,1)S(1)}, bf16[288,2176]{1,0:T(8,128)(2,1)}, u32[]{:S(2)}, u32[]{:S(2)}) %collective-permute-start.5) | collective-permute-done | bytes 1253408 | tf_op jit(solution)/shard_map/ppermute | solution.py:299
  224.2 2.6 collective-permute-start.9
  226.8 16.6 %collective-permute-done.9.refs_0_ = bf16[288,2176]{1,0:T(8,128)(2,1)S(1)} collective-permute-done((bf16[288,2176]{1,0:T(8,128)(2,1)}, bf16[288,2176]{1,0:T(8,128)(2,1)S(1)}, u32[]{:S(2)}, u32[]{:S(2)}) %collective-permute-start.9) | collective-permute-done | bytes 1253408 | tf_op jit(solution)/shard_map/ppermute | solution.py:299
  244.1 16.2 %collective-permute-done.11.refs_0_ = bf16[288,2176]{1,0:T(8,128)(2,1)S(1)} collective-permute-done((bf16[288,2176]{1,0:T(8,128)(2,1)S(1)}, bf16[288,2176]{1,0:T(8,128)(2,1)S(1)}, u32[]{:S(2)}, u32[]{:S(2)}) %collective-permute-start.11) | collective-permute-done | bytes 1253408 | tf_op jit(solution)/shard_map/ppermute | solution.py:299
  261.6 15.7 %collective-permute-done.13.refs_0_ = bf16[288,2176]{1,0:T(8,128)(2,1)S(1)} collective-permute-done((bf16[288,2176]{1,0:T(8,128)(2,1)S(1)}, bf16[288,2176]{1,0:T(8,128)(2,1)S(1)}, u32[]{:S(2)}, u32[]{:S(2)}) %collective-permute-start.13) | collective-permute-done | bytes 1253408 | tf_op jit(solution)/shard_map/ppermute | solution.py:299
  283.3 7.4 %expert_hidden.8 = (bf16[288,1024]{1,0:T(8,128)(2,1)S(1)}, bf16[288,1024]{1,0:T(8,128)(2,1)S(1)}) custom-call(s32[1]{0:T(128)} %bitcast.9.me_ref, bf16[288,2176]{1,0:T(8,128)(2,1)S(1)} %pad_maximum_fusion.refs_0_, bf16[288,2176]{1,0:T(8,128)(2,1)S(1)} %collective-permute-done.3.refs_1_, bf16[16,128,512]{2,1,0:T(8,128)(2,1)S(1)} %copy-done.1, ...), custom_call_target="tpu_custom_call" | custom-call | flops 4831838208 | bytes 11927552 | tf_op jit(solution)/shard_map/expert_hidden/pallas_call | solution.py:132
  291.1 3.5 collective-permute-done.15.refs_0_
  295.3 7.3 %expert_hidden.9 = (bf16[288,1024]{1,0:T(8,128)(2,1)S(1)}, bf16[288,1024]{1,0:T(8,128)(2,1)S(1)}) custom-call(s32[1]{0:T(128)} %bitcast.9.me_ref, bf16[288,2176]{1,0:T(8,128)(2,1)S(1)} %copy-done.7, bf16[288,2176]{1,0:T(8,128)(2,1)S(1)} %collective-permute-done.7.refs_1_, bf16[16,128,512]{2,1,0:T(8,128)(2,1)S(1)} %copy-done.2, ...), custom_call_target="tpu_custom_call" | custom-call | flops 4831838208 | bytes 11927552 | tf_op jit(solution)/shard_map/expert_hidden/pallas_call | solution.py:132
  302.7 7.7 %expert_hidden.10 = (bf16[288,1024]{1,0:T(8,128)(2,1)S(1)}, bf16[288,1024]{1,0:T(8,128)(2,1)S(1)}) custom-call(s32[1]{0:T(128)} %bitcast.9.me_ref, bf16[288,2176]{1,0:T(8,128)(2,1)} %collective-permute-done.5.refs_0_, bf16[288,2176]{1,0:T(8,128)(2,1)S(1)} %collective-permute-done.8.refs_1_, bf16[16,128,512]{2,1,0:T(8,128)(2,1)S(1)} %copy-done.2, ...), custom_call_target="tpu_custom_call" | custom-call | flops 4831838208 | bytes 11927552 | tf_op jit(solution)/shard_map/expert_hidden/pallas_call | solution.py:132
  311.0 7.3 %expert_hidden.11 = (bf16[288,1024]{1,0:T(8,128)(2,1)S(1)}, bf16[288,1024]{1,0:T(8,128)(2,1)S(1)}) custom-call(s32[1]{0:T(128)} %bitcast.9.me_ref, bf16[288,2176]{1,0:T(8,128)(2,1)S(1)} %collective-permute-done.9.refs_0_, bf16[288,2176]{1,0:T(8,128)(2,1)S(1)} %collective-permute-done.10.refs_1_, bf16[16,128,512]{2,1,0:T(8,128)(2,1)S(1)} %copy-done.2, ...), custom_call_target="tpu_custom_call" | custom-call | flops 4831838208 | bytes 11927552 | tf_op jit(solution)/shard_map/expert_hidden/pallas_call | solution.py:132
  318.3 16.0 %expert_hidden.12 = (bf16[288,1024]{1,0:T(8,128)(2,1)S(1)}, bf16[288,1024]{1,0:T(8,128)(2,1)S(1)}) custom-call(s32[1]{0:T(128)} %bitcast.9.me_ref, bf16[288,2176]{1,0:T(8,128)(2,1)S(1)} %collective-permute-done.11.refs_0_, bf16[288,2176]{1,0:T(8,128)(2,1)S(1)} %collective-permute-done.12.refs_1_, bf16[16,128,512]{2,1,0:T(8,128)(2,1)S(1)} %copy-done.2, ...), custom_call_target="tpu_custom_call" | custom-call | flops 4831838208 | bytes 11927552 | tf_op jit(solution)/shard_map/expert_hidden/pallas_call | solution.py:132
  334.4 7.3 %expert_hidden.13 = (bf16[288,1024]{1,0:T(8,128)(2,1)S(1)}, bf16[288,1024]{1,0:T(8,128)(2,1)S(1)}) custom-call(s32[1]{0:T(128)} %bitcast.9.me_ref, bf16[288,2176]{1,0:T(8,128)(2,1)S(1)} %collective-permute-done.13.refs_0_, bf16[288,2176]{1,0:T(8,128)(2,1)S(1)} %collective-permute-done.14.refs_1_, bf16[16,128,512]{2,1,0:T(8,128)(2,1)S(1)} %copy-done.2, ...), custom_call_target="tpu_custom_call" | custom-call | flops 4831838208 | bytes 11927552 | tf_op jit(solution)/shard_map/expert_hidden/pallas_call | solution.py:132
  341.7 7.3 %expert_hidden.14 = (bf16[288,1024]{1,0:T(8,128)(2,1)S(1)}, bf16[288,1024]{1,0:T(8,128)(2,1)S(1)}) custom-call(s32[1]{0:T(128)} %bitcast.9.me_ref, bf16[288,2176]{1,0:T(8,128)(2,1)S(1)} %collective-permute-done.15.refs_0_, bf16[288,2176]{1,0:T(8,128)(2,1)S(1)} %collective-permute-done.16.refs_1_, bf16[16,128,512]{2,1,0:T(8,128)(2,1)S(1)} %copy-done.2, ...), custom_call_target="tpu_custom_call" | custom-call | flops 4831838208 | bytes 11927552 | tf_op jit(solution)/shard_map/expert_hidden/pallas_call | solution.py:132
  349.0 7.3 %expert_hidden.15 = (bf16[288,1024]{1,0:T(8,128)(2,1)S(1)}, bf16[288,1024]{1,0:T(8,128)(2,1)S(1)}) custom-call(s32[1]{0:T(128)} %bitcast.9.me_ref, bf16[288,2176]{1,0:T(8,128)(2,1)S(1)} %collective-permute-done.17.refs_0_, bf16[288,2176]{1,0:T(8,128)(2,1)S(1)} %collective-permute-done.18.refs_1_, bf16[16,128,512]{2,1,0:T(8,128)(2,1)S(1)} %copy-done.2, ...), custom_call_target="tpu_custom_call" | custom-call | flops 4831838208 | bytes 11927552 | tf_op jit(solution)/shard_map/expert_hidden/pallas_call | solution.py:132
  356.3 2.6 expert_down.15
  359.5 2.8 expert_down.14
  362.6 2.4 collective-permute-start.28
  365.0 2.6 expert_down.13
  368.4 4.1 collective-permute-done.28.refs_2_
  372.8 2.4 collective-permute-start.29
  375.2 2.6 expert_down.12
  379.1 2.4 collective-permute-start.36
  381.5 3.7 collective-permute-done.29.refs_2_
  385.4 2.4 collective-permute-start.30
  387.8 2.6 expert_down.11
  394.1 3.7 collective-permute-done.30.refs_2_
  400.4 2.6 expert_down.10
  404.4 2.7 collective-permute-start.38
  407.0 3.4 collective-permute-done.31.refs_2_
  413.1 2.6 expert_down.9
  419.4 2.6 expert_down.8
  425.7 3.7 collective-permute-done.39.refs_2_
  432.0 3.7 collective-permute-done.33.refs_2_
  438.4 3.7 collective-permute-done.40.refs_2_
  444.7 3.7 collective-permute-done.34.refs_2_
  448.6 6.1 %collective-permute-done.41.refs_2_ = bf16[288,1024]{1,0:T(8,128)(2,1)S(1)} collective-permute-done((bf16[288,1024]{1,0:T(8,128)(2,1)S(1)}, bf16[288,1024]{1,0:T(8,128)(2,1)S(1)}, u32[]{:S(2)}, u32[]{:S(2)}) %collective-permute-start.41) | collective-permute-done | bytes 589856 | tf_op jit(solution)/shard_map/ppermute | solution.py:327
  457.1 3.2 fusion.1
  (124 shorter events, 60.4 us)
Async XLA Ops:
  7.6 48.6 %all-to-all-start = ((bf16[16,128,512]{2,1,0:T(8,128)(2,1)}), bf16[16,128,512]{2,1,0:T(8,128)(2,1)S(1)}, u32[]{:S(2)}, u32[]{:S(2)}) async-start(bf16[16,128,512]{2,1,0:T(8,128)(2,1)} %get-tuple-element.129), calls=%async_computation | async-start | bytes 4194304 | tf_op jit(solution)/shard_map/all_to_all | solution.py:241
  56.2 14.7 %copy-start = (bf16[16,128,512]{2,1,0:T(8,128)(2,1)}, bf16[16,128,512]{2,1,0:T(8,128)(2,1)S(1)}, u32[]{:S(2)}) copy-start(bf16[16,128,512]{2,1,0:T(8,128)(2,1)S(1)} %all-to-all-done.refs_2_) | copy-start | bytes 6291460
  56.2 86.5 %all-to-all-start.1 = ((bf16[16,128,512]{2,1,0:T(8,128)(2,1)}), bf16[16,128,512]{2,1,0:T(8,128)(2,1)}, u32[]{:S(2)}, u32[]{:S(2)}) async-start(bf16[16,128,512]{2,1,0:T(8,128)(2,1)} %get-tuple-element.67), calls=%async_computation.1 | async-start | bytes 4194304 | tf_op jit(solution)/shard_map/all_to_all | solution.py:241
  69.3 29.0 %collective-permute-start = (bf16[288,2048]{1,0:T(8,128)(2,1)S(1)}, bf16[288,2048]{1,0:T(8,128)(2,1)}, u32[]{:S(2)}, u32[]{:S(2)}) collective-permute-start(bf16[288,2048]{1,0:T(8,128)(2,1)S(1)} %fusion), channel_id=1, source_target_pairs={{0,16},{16,0},{1,17},{17,1},{2,18},{18,2},{3,19},{19,3},{4,20},{20... | collective-permute-start | bytes 3538952 | tf_op jit(solution)/shard_map/ppermute | solution.py:273
  70.9 71.8 %collective-permute-start.1 = (bf16[16,128,512]{2,1,0:T(8,128)(2,1)S(1)}, bf16[16,128,512]{2,1,0:T(8,128)(2,1)}, u32[]{:S(2)}, u32[]{:S(2)}) collective-permute-start(bf16[16,128,512]{2,1,0:T(8,128)(2,1)S(1)} %all-to-all-done.refs_2_), channel_id=1, source_target_pairs={{0,16},{16,0},{1,17},{17,1},{2,18},{18,2},{3,19},{19,3},{4,20},{20... | collective-permute-start | bytes 6291464 | tf_op jit(solution)/shard_map/ppermute | solution.py:245
  74.1 27.1 %copy-start.13 = (f32[2048]{0:T(1024)S(1)}, f32[2048]{0:T(1024)}, u32[]{:S(2)}) copy-start(f32[2048]{0:T(1024)} %param.16) | copy-start | bytes 24580
  142.7 81.5 %all-to-all-start.2 = ((bf16[16,128,512]{2,1,0:T(8,128)(2,1)}), bf16[16,128,512]{2,1,0:T(8,128)(2,1)S(1)}, u32[]{:S(2)}, u32[]{:S(2)}) async-start(bf16[16,128,512]{2,1,0:T(8,128)(2,1)} %get-tuple-element.72), calls=%async_computation.2 | async-start | bytes 4194304 | tf_op jit(solution)/shard_map/all_to_all | solution.py:241
  148.6 2.1 collective-permute-start.2
  150.8 46.0 %collective-permute-start.4 = (bf16[288,2176]{1,0:T(8,128)(2,1)S(1)}, bf16[288,2176]{1,0:T(8,128)(2,1)S(1)}, u32[]{:S(2)}, u32[]{:S(2)}) collective-permute-start(bf16[288,2176]{1,0:T(8,128)(2,1)S(1)} %pad_maximum_fusion.refs_0_), channel_id=1, source_target_pairs={{0,4},{1,3},{4,8},{5,1},{8,12},{9,5},{12,14},{13,9},{14,10},{15,13... | collective-permute-start | bytes 3760136 | tf_op jit(solution)/shard_map/ppermute | solution.py:299
  152.8 56.9 %collective-permute-start.6 = (bf16[16,128,512]{2,1,0:T(8,128)(2,1)}, bf16[16,128,512]{2,1,0:T(8,128)(2,1)S(1)}, u32[]{:S(2)}, u32[]{:S(2)}) collective-permute-start(bf16[16,128,512]{2,1,0:T(8,128)(2,1)} %all-to-all-done.1.refs_3_), channel_id=1, source_target_pairs={{0,16},{16,0},{1,17},{17,1},{2,18},{18,2},{3,19},{19,3},{4,20},{20... | collective-permute-start | bytes 6291464 | tf_op jit(solution)/shard_map/ppermute | solution.py:245
  196.8 27.4 %collective-permute-start.5 = (bf16[288,2176]{1,0:T(8,128)(2,1)S(1)}, bf16[288,2176]{1,0:T(8,128)(2,1)}, u32[]{:S(2)}, u32[]{:S(2)}) collective-permute-start(bf16[288,2176]{1,0:T(8,128)(2,1)S(1)} %collective-permute-done.4.refs_0_), channel_id=1, source_target_pairs={{0,4},{1,3},{4,8},{5,1},{8,12},{9,5},{12,14},{13,9},{14,10},{15,13... | collective-permute-start | bytes 3760136 | tf_op jit(solution)/shard_map/ppermute | solution.py:299
  224.2 19.1 %collective-permute-start.9 = (bf16[288,2176]{1,0:T(8,128)(2,1)}, bf16[288,2176]{1,0:T(8,128)(2,1)S(1)}, u32[]{:S(2)}, u32[]{:S(2)}) collective-permute-start(bf16[288,2176]{1,0:T(8,128)(2,1)} %collective-permute-done.5.refs_0_), channel_id=1, source_target_pairs={{0,4},{1,3},{4,8},{5,1},{8,12},{9,5},{12,14},{13,9},{14,10},{15,13... | collective-permute-start | bytes 3760136 | tf_op jit(solution)/shard_map/ppermute | solution.py:299
  243.4 17.0 %collective-permute-start.11 = (bf16[288,2176]{1,0:T(8,128)(2,1)S(1)}, bf16[288,2176]{1,0:T(8,128)(2,1)S(1)}, u32[]{:S(2)}, u32[]{:S(2)}) collective-permute-start(bf16[288,2176]{1,0:T(8,128)(2,1)S(1)} %collective-permute-done.9.refs_0_), channel_id=1, source_target_pairs={{0,4},{1,3},{4,8},{5,1},{8,12},{9,5},{12,14},{13,9},{14,10},{15,13... | collective-permute-start | bytes 3760136 | tf_op jit(solution)/shard_map/ppermute | solution.py:299
  260.4 17.0 %collective-permute-start.13 = (bf16[288,2176]{1,0:T(8,128)(2,1)S(1)}, bf16[288,2176]{1,0:T(8,128)(2,1)S(1)}, u32[]{:S(2)}, u32[]{:S(2)}) collective-permute-start(bf16[288,2176]{1,0:T(8,128)(2,1)S(1)} %collective-permute-done.11.refs_0_), channel_id=1, source_target_pairs={{0,4},{1,3},{4,8},{5,1},{8,12},{9,5},{12,14},{13,9},{14,10},{15,13... | collective-permute-start | bytes 3760136 | tf_op jit(solution)/shard_map/ppermute | solution.py:299
  261.1 18.8 %collective-permute-start.3 = (bf16[288,2176]{1,0:T(8,128)(2,1)S(1)}, bf16[288,2176]{1,0:T(8,128)(2,1)S(1)}, u32[]{:S(2)}, u32[]{:S(2)}) collective-permute-start(bf16[288,2176]{1,0:T(8,128)(2,1)S(1)} %pad_maximum_fusion.refs_0_), channel_id=1, source_target_pairs={{0,1},{1,0},{2,3},{3,2},{4,5},{5,4},{6,7},{7,6},{8,9},{9,8},{10,11... | collective-permute-start | bytes 3760136 | tf_op jit(solution)/shard_map/ppermute | solution.py:310
  261.1 29.6 %collective-permute-start.7 = (bf16[288,2176]{1,0:T(8,128)(2,1)}, bf16[288,2176]{1,0:T(8,128)(2,1)S(1)}, u32[]{:S(2)}, u32[]{:S(2)}) collective-permute-start(bf16[288,2176]{1,0:T(8,128)(2,1)} %copy-done.6), channel_id=1, source_target_pairs={{0,1},{1,0},{2,3},{3,2},{4,5},{5,4},{6,7},{7,6},{8,9},{9,8},{10,11... | collective-permute-start | bytes 3760136 | tf_op jit(solution)/shard_map/ppermute | solution.py:310
  277.3 17.2 %collective-permute-start.15 = (bf16[288,2176]{1,0:T(8,128)(2,1)S(1)}, bf16[288,2176]{1,0:T(8,128)(2,1)S(1)}, u32[]{:S(2)}, u32[]{:S(2)}) collective-permute-start(bf16[288,2176]{1,0:T(8,128)(2,1)S(1)} %collective-permute-done.13.refs_0_), channel_id=1, source_target_pairs={{0,4},{1,3},{4,8},{5,1},{8,12},{9,5},{12,14},{13,9},{14,10},{15,13... | collective-permute-start | bytes 3760136 | tf_op jit(solution)/shard_map/ppermute | solution.py:299
  278.3 24.3 %collective-permute-start.8 = (bf16[288,2176]{1,0:T(8,128)(2,1)}, bf16[288,2176]{1,0:T(8,128)(2,1)S(1)}, u32[]{:S(2)}, u32[]{:S(2)}) collective-permute-start(bf16[288,2176]{1,0:T(8,128)(2,1)} %collective-permute-done.5.refs_0_), channel_id=1, source_target_pairs={{0,1},{1,0},{2,3},{3,2},{4,5},{5,4},{6,7},{7,6},{8,9},{9,8},{10,11... | collective-permute-start | bytes 3760136 | tf_op jit(solution)/shard_map/ppermute | solution.py:310
  278.3 78.0 %collective-permute-start.19 = (bf16[16,128,512]{2,1,0:T(8,128)(2,1)S(1)}, bf16[16,128,512]{2,1,0:T(8,128)(2,1)S(1)}, u32[]{:S(2)}, u32[]{:S(2)}) collective-permute-start(bf16[16,128,512]{2,1,0:T(8,128)(2,1)S(1)} %all-to-all-done.2.refs_2_), channel_id=1, source_target_pairs={{0,16},{16,0},{1,17},{17,1},{2,18},{18,2},{3,19},{19,3},{4,20},{20... | collective-permute-start | bytes 6291464 | tf_op jit(solution)/shard_map/ppermute | solution.py:245
  279.9 30.5 %collective-permute-start.10 = (bf16[288,2176]{1,0:T(8,128)(2,1)S(1)}, bf16[288,2176]{1,0:T(8,128)(2,1)S(1)}, u32[]{:S(2)}, u32[]{:S(2)}) collective-permute-start(bf16[288,2176]{1,0:T(8,128)(2,1)S(1)} %collective-permute-done.9.refs_0_), channel_id=1, source_target_pairs={{0,1},{1,0},{2,3},{3,2},{4,5},{5,4},{6,7},{7,6},{8,9},{9,8},{10,11... | collective-permute-start | bytes 3760136 | tf_op jit(solution)/shard_map/ppermute | solution.py:310
  290.7 27.6 %collective-permute-start.12 = (bf16[288,2176]{1,0:T(8,128)(2,1)S(1)}, bf16[288,2176]{1,0:T(8,128)(2,1)S(1)}, u32[]{:S(2)}, u32[]{:S(2)}) collective-permute-start(bf16[288,2176]{1,0:T(8,128)(2,1)S(1)} %collective-permute-done.11.refs_0_), channel_id=1, source_target_pairs={{0,1},{1,0},{2,3},{3,2},{4,5},{5,4},{6,7},{7,6},{8,9},{9,8},{10,11... | collective-permute-start | bytes 3760136 | tf_op jit(solution)/shard_map/ppermute | solution.py:310
  294.6 23.7 %collective-permute-start.17 = (bf16[288,2176]{1,0:T(8,128)(2,1)S(1)}, bf16[288,2176]{1,0:T(8,128)(2,1)S(1)}, u32[]{:S(2)}, u32[]{:S(2)}) collective-permute-start(bf16[288,2176]{1,0:T(8,128)(2,1)S(1)} %collective-permute-done.15.refs_0_), channel_id=1, source_target_pairs={{0,4},{1,3},{4,8},{5,1},{8,12},{9,5},{12,14},{13,9},{14,10},{15,13... | collective-permute-start | bytes 3760136 | tf_op jit(solution)/shard_map/ppermute | solution.py:299
  302.6 31.8 %collective-permute-start.14 = (bf16[288,2176]{1,0:T(8,128)(2,1)S(1)}, bf16[288,2176]{1,0:T(8,128)(2,1)S(1)}, u32[]{:S(2)}, u32[]{:S(2)}) collective-permute-start(bf16[288,2176]{1,0:T(8,128)(2,1)S(1)} %collective-permute-done.13.refs_0_), channel_id=1, source_target_pairs={{0,1},{1,0},{2,3},{3,2},{4,5},{5,4},{6,7},{7,6},{8,9},{9,8},{10,11... | collective-permute-start | bytes 3760136 | tf_op jit(solution)/shard_map/ppermute | solution.py:310
  310.4 31.3 %collective-permute-start.16 = (bf16[288,2176]{1,0:T(8,128)(2,1)S(1)}, bf16[288,2176]{1,0:T(8,128)(2,1)S(1)}, u32[]{:S(2)}, u32[]{:S(2)}) collective-permute-start(bf16[288,2176]{1,0:T(8,128)(2,1)S(1)} %collective-permute-done.15.refs_0_), channel_id=1, source_target_pairs={{0,1},{1,0},{2,3},{3,2},{4,5},{5,4},{6,7},{7,6},{8,9},{9,8},{10,11... | collective-permute-start | bytes 3760136 | tf_op jit(solution)/shard_map/ppermute | solution.py:310
  318.3 30.7 %collective-permute-start.18 = (bf16[288,2176]{1,0:T(8,128)(2,1)S(1)}, bf16[288,2176]{1,0:T(8,128)(2,1)S(1)}, u32[]{:S(2)}, u32[]{:S(2)}) collective-permute-start(bf16[288,2176]{1,0:T(8,128)(2,1)S(1)} %collective-permute-done.17.refs_0_), channel_id=1, source_target_pairs={{0,1},{1,0},{2,3},{3,2},{4,5},{5,4},{6,7},{7,6},{8,9},{9,8},{10,11... | collective-permute-start | bytes 3760136 | tf_op jit(solution)/shard_map/ppermute | solution.py:310
  358.9 3.5 collective-permute-start.27
  362.4 6.0 %collective-permute-start.26 = (bf16[288,2048]{1,0:T(8,128)(2,1)S(1)}, bf16[288,2048]{1,0:T(8,128)(2,1)S(1)}, u32[]{:S(2)}, u32[]{:S(2)}) collective-permute-start(bf16[288,2048]{1,0:T(8,128)(2,1)S(1)} %get-tuple-element.120), channel_id=1, source_target_pairs={{0,1},{1,0},{2,3},{3,2},{4,5},{5,4},{6,7},{7,6},{8,9},{9,8},{10,11... | collective-permute-start | bytes 3538952 | tf_op jit(solution)/shard_map/ppermute | solution.py:318
  362.6 9.9 %collective-permute-start.28 = (bf16[288,1024]{1,0:T(8,128)(2,1)S(1)}, bf16[288,1024]{1,0:T(8,128)(2,1)S(1)}, u32[]{:S(2)}, u32[]{:S(2)}) collective-permute-start(bf16[288,1024]{1,0:T(8,128)(2,1)S(1)} %add_terms.16), channel_id=1, source_target_pairs={{0,4},{1,3},{4,8},{5,1},{8,12},{9,5},{12,14},{13,9},{14,10},{15,13... | collective-permute-start | bytes 1769480 | tf_op jit(solution)/shard_map/ppermute | solution.py:327
  367.7 13.8 %collective-permute-start.25 = (bf16[288,2048]{1,0:T(8,128)(2,1)S(1)}, bf16[288,2048]{1,0:T(8,128)(2,1)S(1)}, u32[]{:S(2)}, u32[]{:S(2)}) collective-permute-start(bf16[288,2048]{1,0:T(8,128)(2,1)S(1)} %get-tuple-element.116), channel_id=1, source_target_pairs={{0,1},{1,0},{2,3},{3,2},{4,5},{5,4},{6,7},{7,6},{8,9},{9,8},{10,11... | collective-permute-start | bytes 3538952 | tf_op jit(solution)/shard_map/ppermute | solution.py:318
  367.9 11.0 %collective-permute-start.35 = (bf16[288,1024]{1,0:T(8,128)(2,1)S(1)}, bf16[288,1024]{1,0:T(8,128)(2,1)S(1)}, u32[]{:S(2)}, u32[]{:S(2)}) collective-permute-start(bf16[288,1024]{1,0:T(8,128)(2,1)S(1)} %add_terms.24), channel_id=1, source_target_pairs={{0,4},{1,3},{4,8},{5,1},{8,12},{9,5},{12,14},{13,9},{14,10},{15,13... | collective-permute-start | bytes 1769480 | tf_op jit(solution)/shard_map/ppermute | solution.py:327
  372.8 12.4 %collective-permute-start.29 = (bf16[288,1024]{1,0:T(8,128)(2,1)S(1)}, bf16[288,1024]{1,0:T(8,128)(2,1)S(1)}, u32[]{:S(2)}, u32[]{:S(2)}) collective-permute-start(bf16[288,1024]{1,0:T(8,128)(2,1)S(1)} %add_terms.17), channel_id=1, source_target_pairs={{0,4},{1,3},{4,8},{5,1},{8,12},{9,5},{12,14},{13,9},{14,10},{15,13... | collective-permute-start | bytes 1769480 | tf_op jit(solution)/shard_map/ppermute | solution.py:327
  377.8 16.3 %collective-permute-start.24 = (bf16[288,2048]{1,0:T(8,128)(2,1)S(1)}, bf16[288,2048]{1,0:T(8,128)(2,1)S(1)}, u32[]{:S(2)}, u32[]{:S(2)}) collective-permute-start(bf16[288,2048]{1,0:T(8,128)(2,1)S(1)} %get-tuple-element.112), channel_id=1, source_target_pairs={{0,1},{1,0},{2,3},{3,2},{4,5},{5,4},{6,7},{7,6},{8,9},{9,8},{10,11... | collective-permute-start | bytes 3538952 | tf_op jit(solution)/shard_map/ppermute | solution.py:318
  379.1 12.4 %collective-permute-start.36 = (bf16[288,1024]{1,0:T(8,128)(2,1)S(1)}, bf16[288,1024]{1,0:T(8,128)(2,1)S(1)}, u32[]{:S(2)}, u32[]{:S(2)}) collective-permute-start(bf16[288,1024]{1,0:T(8,128)(2,1)S(1)} %add_terms.25), channel_id=1, source_target_pairs={{0,4},{1,3},{4,8},{5,1},{8,12},{9,5},{12,14},{13,9},{14,10},{15,13... | collective-permute-start | bytes 1769480 | tf_op jit(solution)/shard_map/ppermute | solution.py:327
  385.4 12.4 %collective-permute-start.30 = (bf16[288,1024]{1,0:T(8,128)(2,1)S(1)}, bf16[288,1024]{1,0:T(8,128)(2,1)S(1)}, u32[]{:S(2)}, u32[]{:S(2)}) collective-permute-start(bf16[288,1024]{1,0:T(8,128)(2,1)S(1)} %add_terms.18), channel_id=1, source_target_pairs={{0,4},{1,3},{4,8},{5,1},{8,12},{9,5},{12,14},{13,9},{14,10},{15,13... | collective-permute-start | bytes 1769480 | tf_op jit(solution)/shard_map/ppermute | solution.py:327
  390.4 16.6 %collective-permute-start.23 = (bf16[288,2048]{1,0:T(8,128)(2,1)S(1)}, bf16[288,2048]{1,0:T(8,128)(2,1)S(1)}, u32[]{:S(2)}, u32[]{:S(2)}) collective-permute-start(bf16[288,2048]{1,0:T(8,128)(2,1)S(1)} %get-tuple-element.108), channel_id=1, source_target_pairs={{0,1},{1,0},{2,3},{3,2},{4,5},{5,4},{6,7},{7,6},{8,9},{9,8},{10,11... | collective-permute-start | bytes 3538952 | tf_op jit(solution)/shard_map/ppermute | solution.py:318
  391.7 12.4 %collective-permute-start.37 = (bf16[288,1024]{1,0:T(8,128)(2,1)S(1)}, bf16[288,1024]{1,0:T(8,128)(2,1)S(1)}, u32[]{:S(2)}, u32[]{:S(2)}) collective-permute-start(bf16[288,1024]{1,0:T(8,128)(2,1)S(1)} %add_terms.26), channel_id=1, source_target_pairs={{0,4},{1,3},{4,8},{5,1},{8,12},{9,5},{12,14},{13,9},{14,10},{15,13... | collective-permute-start | bytes 1769480 | tf_op jit(solution)/shard_map/ppermute | solution.py:327
  398.0 12.4 %collective-permute-start.31 = (bf16[288,1024]{1,0:T(8,128)(2,1)S(1)}, bf16[288,1024]{1,0:T(8,128)(2,1)S(1)}, u32[]{:S(2)}, u32[]{:S(2)}) collective-permute-start(bf16[288,1024]{1,0:T(8,128)(2,1)S(1)} %add_terms.19), channel_id=1, source_target_pairs={{0,4},{1,3},{4,8},{5,1},{8,12},{9,5},{12,14},{13,9},{14,10},{15,13... | collective-permute-start | bytes 1769480 | tf_op jit(solution)/shard_map/ppermute | solution.py:327
  403.1 19.0 %collective-permute-start.22 = (bf16[288,2048]{1,0:T(8,128)(2,1)S(1)}, bf16[288,2048]{1,0:T(8,128)(2,1)S(1)}, u32[]{:S(2)}, u32[]{:S(2)}) collective-permute-start(bf16[288,2048]{1,0:T(8,128)(2,1)S(1)} %get-tuple-element.104), channel_id=1, source_target_pairs={{0,1},{1,0},{2,3},{3,2},{4,5},{5,4},{6,7},{7,6},{8,9},{9,8},{10,11... | collective-permute-start | bytes 3538952 | tf_op jit(solution)/shard_map/ppermute | solution.py:318
  404.4 12.4 %collective-permute-start.38 = (bf16[288,1024]{1,0:T(8,128)(2,1)S(1)}, bf16[288,1024]{1,0:T(8,128)(2,1)S(1)}, u32[]{:S(2)}, u32[]{:S(2)}) collective-permute-start(bf16[288,1024]{1,0:T(8,128)(2,1)S(1)} %add_terms.27), channel_id=1, source_target_pairs={{0,4},{1,3},{4,8},{5,1},{8,12},{9,5},{12,14},{13,9},{14,10},{15,13... | collective-permute-start | bytes 1769480 | tf_op jit(solution)/shard_map/ppermute | solution.py:327
  410.7 12.4 %collective-permute-start.32 = (bf16[288,1024]{1,0:T(8,128)(2,1)S(1)}, bf16[288,1024]{1,0:T(8,128)(2,1)S(1)}, u32[]{:S(2)}, u32[]{:S(2)}) collective-permute-start(bf16[288,1024]{1,0:T(8,128)(2,1)S(1)} %add_terms.20), channel_id=1, source_target_pairs={{0,4},{1,3},{4,8},{5,1},{8,12},{9,5},{12,14},{13,9},{14,10},{15,13... | collective-permute-start | bytes 1769480 | tf_op jit(solution)/shard_map/ppermute | solution.py:327
  415.7 16.3 %collective-permute-start.21 = (bf16[288,2048]{1,0:T(8,128)(2,1)S(1)}, bf16[288,2048]{1,0:T(8,128)(2,1)S(1)}, u32[]{:S(2)}, u32[]{:S(2)}) collective-permute-start(bf16[288,2048]{1,0:T(8,128)(2,1)S(1)} %get-tuple-element.100), channel_id=1, source_target_pairs={{0,1},{1,0},{2,3},{3,2},{4,5},{5,4},{6,7},{7,6},{8,9},{9,8},{10,11... | collective-permute-start | bytes 3538952 | tf_op jit(solution)/shard_map/ppermute | solution.py:318
  417.0 12.4 %collective-permute-start.39 = (bf16[288,1024]{1,0:T(8,128)(2,1)S(1)}, bf16[288,1024]{1,0:T(8,128)(2,1)S(1)}, u32[]{:S(2)}, u32[]{:S(2)}) collective-permute-start(bf16[288,1024]{1,0:T(8,128)(2,1)S(1)} %add_terms.28), channel_id=1, source_target_pairs={{0,4},{1,3},{4,8},{5,1},{8,12},{9,5},{12,14},{13,9},{14,10},{15,13... | collective-permute-start | bytes 1769480 | tf_op jit(solution)/shard_map/ppermute | solution.py:327
  423.3 12.4 %collective-permute-start.33 = (bf16[288,1024]{1,0:T(8,128)(2,1)S(1)}, bf16[288,1024]{1,0:T(8,128)(2,1)S(1)}, u32[]{:S(2)}, u32[]{:S(2)}) collective-permute-start(bf16[288,1024]{1,0:T(8,128)(2,1)S(1)} %add_terms.21), channel_id=1, source_target_pairs={{0,4},{1,3},{4,8},{5,1},{8,12},{9,5},{12,14},{13,9},{14,10},{15,13... | collective-permute-start | bytes 1769480 | tf_op jit(solution)/shard_map/ppermute | solution.py:327
  425.7 19.0 %collective-permute-start.20 = (bf16[288,2048]{1,0:T(8,128)(2,1)S(1)}, bf16[288,2048]{1,0:T(8,128)(2,1)S(1)}, u32[]{:S(2)}, u32[]{:S(2)}) collective-permute-start(bf16[288,2048]{1,0:T(8,128)(2,1)S(1)} %get-tuple-element.96), channel_id=1, source_target_pairs={{0,1},{1,0},{2,3},{3,2},{4,5},{5,4},{6,7},{7,6},{8,9},{9,8},{10,11... | collective-permute-start | bytes 3538952 | tf_op jit(solution)/shard_map/ppermute | solution.py:318
  429.6 12.4 %collective-permute-start.40 = (bf16[288,1024]{1,0:T(8,128)(2,1)S(1)}, bf16[288,1024]{1,0:T(8,128)(2,1)S(1)}, u32[]{:S(2)}, u32[]{:S(2)}) collective-permute-start(bf16[288,1024]{1,0:T(8,128)(2,1)S(1)} %add_terms.29), channel_id=1, source_target_pairs={{0,4},{1,3},{4,8},{5,1},{8,12},{9,5},{12,14},{13,9},{14,10},{15,13... | collective-permute-start | bytes 1769480 | tf_op jit(solution)/shard_map/ppermute | solution.py:327
  436.0 12.4 %collective-permute-start.34 = (bf16[288,1024]{1,0:T(8,128)(2,1)S(1)}, bf16[288,1024]{1,0:T(8,128)(2,1)S(1)}, u32[]{:S(2)}, u32[]{:S(2)}) collective-permute-start(bf16[288,1024]{1,0:T(8,128)(2,1)S(1)} %add_terms.22), channel_id=1, source_target_pairs={{0,4},{1,3},{4,8},{5,1},{8,12},{9,5},{12,14},{13,9},{14,10},{15,13... | collective-permute-start | bytes 1769480 | tf_op jit(solution)/shard_map/ppermute | solution.py:327
  442.3 12.4 %collective-permute-start.41 = (bf16[288,1024]{1,0:T(8,128)(2,1)S(1)}, bf16[288,1024]{1,0:T(8,128)(2,1)S(1)}, u32[]{:S(2)}, u32[]{:S(2)}) collective-permute-start(bf16[288,1024]{1,0:T(8,128)(2,1)S(1)} %add_terms.30), channel_id=1, source_target_pairs={{0,4},{1,3},{4,8},{5,1},{8,12},{9,5},{12,14},{13,9},{14,10},{15,13... | collective-permute-start | bytes 1769480 | tf_op jit(solution)/shard_map/ppermute | solution.py:327
  455.0 2.1 collective-permute-start.42
  (12 other events, 68.0 us)
where the time goes:
time: 468 us; the launch traced here: 461 us
  waiting for transfers between devices  227 us (49%)
  Pallas kernels  118 us (25%)
  starting transfers between devices  85.9 us (18%)
  local copies, waits for them, and re-layouts  19.3 us (4%)
  other arithmetic  9.39 us (2%)
    ppermute x7, waiting for transfers between devices, on_device(): held = lax.ppermute(held, 'ex', ring)  108 us
    pallas_call x8, Pallas kernels, expert_hidden(): pl.pallas_call(functools.partial(hidden_kernel, experts, width), in_specs...  67.5 us
    ppermute x14, waiting for transfers between devices, on_device(): running = lax.ppermute(running, 'ex', ring)  40.7 us
    ppermute x3, waiting for transfers between devices, over_kv(): lax.ppermute(part, 'kv', [(i, (i + turn) % kv) for i in range(kv)])  37.5 us
    ppermute x14, starting transfers between devices, on_device(): running = lax.ppermute(running, 'ex', ring)  32.1 us
    pallas_call x1, Pallas kernels, attention(): pl.pallas_call(functools.partial(attention_kernel, 1.0 / math.sqrt(HD)),...  26.3 us
    all_to_all x3, starting transfers between devices, over_experts(): return lax.all_to_all(part, 'ex', split_axis=0, concat_axis=0, tiled=True)  24.5 us
    ppermute x1, waiting for transfers between devices, on_device(): sent = lax.ppermute(sent, 'kv', [(i, (i + turn) % kv) for i in range(kv)])  24.2 us
  transfers between devices with their start and end apart: 46, of which 25 were waited for; matrix products, arithmetic and copies ran while one was open for 2% of the time, Pallas kernels for 25%

commit v1 on v0

--- a/solution.py
+++ b/solution.py
@@ -118,8 +118,9 @@
             x = x_ref[:, :width]
             gate = jnp.dot(x, gate_w, preferred_element_type=jnp.float32)
             up = jnp.dot(x, up_w, preferred_element_type=jnp.float32)
+            gate = 0.5 * gate
             out_ref[:, part * units : (part + 1) * units] = (
-                gate * jax.nn.sigmoid(gate) * up * share
+                (gate + gate * jnp.tanh(gate)) * (up * share)
             ).astype(jnp.bfloat16)
 
 
@@ -241,10 +242,17 @@
         return lax.all_to_all(part, "ex", split_axis=0, concat_axis=0, tiled=True)
 
     def over_kv(part):
+        middle = part.shape[0] // 2
         return [
-            lax.ppermute(part, "kv", [(i, (i + turn) % kv) for i in range(kv)])
-            for turn in range(1, kv)
+            [
+                lax.ppermute(half, "kv", [(i, (i + turn) % kv) for i in range(kv)])
+                for turn in range(1, kv)
+            ]
+            for half in (part[:middle], part[middle:])
         ]
+
+    def joined(halves):
+        return [jnp.concatenate(pair, axis=0) for pair in zip(*halves)]
 
     probs = route_probs[0]
     share = probs / jnp.sum(probs, axis=-1, keepdims=True)
@@ -255,7 +263,9 @@
     rows = x_tokens[0]
     row_count = rows.shape[0]
     rows_dev = row_count // kv
-    gate, up, down = (w_trainer[:, kind].astype(jnp.bfloat16) for kind in range(3))
+    gate = w_trainer[:, 0].astype(jnp.bfloat16)
+    gate, rest = lax.optimization_barrier((gate, w_trainer))
+    up, down = (rest[:, kind].astype(jnp.bfloat16) for kind in (1, 2))
     gate = over_experts(gate)
     mixed = attention(rows, attn_gain, w_qkv, cache, cache_len, w_out)
     mixed, gate, up, down = lax.optimization_barrier((mixed, gate, up, down))
@@ -274,7 +284,7 @@
         resid = resid + sent.astype(jnp.float32)
     moe_in = rms_scale(resid, moe_gain).astype(jnp.bfloat16)
     moe_in = jnp.concatenate([moe_in, factor], axis=1)
-    moe_in, gates, up, down = lax.optimization_barrier((moe_in, gates, up, down))
+    moe_in, gates[0], up, down = lax.optimization_barrier((moe_in, gates[0], up, down))
     ups = over_kv(up)
     down = over_experts(down)
 
@@ -294,23 +304,33 @@
 
     got = lax.ppermute(half_of(moe_in, 1 - core), "ex", swap)
     held = jnp.concatenate([half_of(moe_in, core), got], axis=0)
-    blocks = [held]
+    first_weights = [gate, up]
+    due = {4: [0], 5: [1, 2], 6: [3], 7: [4]}
+    blocks, hiddens = [held], {}
+
+    def hidden_of(step):
+        other = lax.ppermute(blocks[step], "ex", swap)
+        return expert_hidden(experts, me[None], [blocks[step], other], first_weights)
+
     for step in range(1, chips):
         held = lax.ppermute(held, "ex", ring)
-        if step == min(2, chips - 1):
+        if step == 1:
+            held, gates[1] = lax.optimization_barrier((held, gates[1]))
+        if step == 2:
             held, ups, down = lax.optimization_barrier((held, ups, down))
             downs = over_kv(down)
+            for pair in zip(joined(gates), joined(ups)):
+                first_weights += pair
         blocks.append(held)
-
-    first_weights = [gate, up]
-    for turn in range(kv - 1):
-        first_weights += [gates[turn], ups[turn]]
-    hiddens = []
-    for block in blocks:
-        other = lax.ppermute(block, "ex", swap)
-        hiddens.append(expert_hidden(experts, me[None], [block, other], first_weights))
-    ahead = chips
-    hiddens[:ahead], downs = lax.optimization_barrier((hiddens[:ahead], downs))
+        for early in due.get(step, []):
+            hiddens[early] = hidden_of(early)
+            held, hiddens[early] = lax.optimization_barrier((held, hiddens[early]))
+        blocks[step] = held
+    for step in range(chips):
+        if step not in hiddens:
+            hiddens[step] = hidden_of(step)
+    hiddens = [hiddens[step] for step in range(chips)]
+    downs = joined(downs)
     keeps, gots = [], []
     for pair in hiddens:
         keep, give = expert_down(pair, [down] + downs)

time: 468 us -> 462 us (0.987)
  waiting for transfers between devices: 227 us -> 216 us
  local copies, waits for them, and re-layouts: 19.3 us -> 25.9 us
    ppermute x7, waiting for transfers between devices: 108 us -> 33.4 us  [on_device(): held = lax.ppermute(held, 'ex', ring)]
    ppermute x11 -> x14, waiting for transfers between devices: 37.5 us -> 100 us  [the longest x6 100 us: over_kv(): lax.ppermute(half, 'kv', [(i, (i + turn) % kv) for i in range(kv)])]
    ppermute x14, starting transfers between devices: 32.1 us -> 14.9 us  [on_device(): running = lax.ppermute(running, 'ex', ring)]
    ppermute x7, starting transfers between devices: 20.7 us -> 34.9 us  [on_device(): held = lax.ppermute(held, 'ex', ring)]
    pallas_call x8, Pallas kernels: 67.5 us -> 54.8 us  [expert_hidden(): pl.pallas_call(functools.partial(hidden_kernel, experts, width), in_specs...]
    pallas_call x8, Pallas kernels: 21.3 us -> 33.8 us  [expert_down(): pl.pallas_call(down_kernel, in_specs=[vmem] * (2 + len(weights)), out_spe...]
    ppermute x14, waiting for transfers between devices: 40.7 us -> 47.1 us  [on_device(): running = lax.ppermute(running, 'ex', ring)]
    slice x0 -> x3, local copies, waits for them, and re-layouts: none -> 4.98 us  [over_kv(): part[middle:]]
  transfers between devices with their start and end apart: 46 -> 49, of which waited for: 25 -> 19; matrix products, arithmetic and copies ran while one was open for 2% -> 6% of each run, Pallas kernels for 25% -> 26%
where the time goes in v1:
time: 462 us; the launch traced here: 454 us
  waiting for transfers between devices  216 us (47%)
  Pallas kernels  118 us (26%)
  starting transfers between devices  84.8 us (18%)
  local copies, waits for them, and re-layouts  25.9 us (6%)
  other arithmetic  8.06 us (2%)
    ppermute x6, waiting for transfers between devices, over_kv(): lax.ppermute(half, 'kv', [(i, (i + turn) % kv) for i in range(kv)])  100 us
    pallas_call x8, Pallas kernels, expert_hidden(): pl.pallas_call(functools.partial(hidden_kernel, experts, width), in_specs...  54.8 us
    ppermute x14, waiting for transfers between devices, on_device(): running = lax.ppermute(running, 'ex', ring)  47.1 us
    ppermute x7, starting transfers between devices, on_device(): held = lax.ppermute(held, 'ex', ring)  34.9 us
    pallas_call x8, Pallas kernels, expert_down(): pl.pallas_call(down_kernel, in_specs=[vmem] * (2 + len(weights)), out_spe...  33.8 us
    ppermute x7, waiting for transfers between devices, on_device(): held = lax.ppermute(held, 'ex', ring)  33.4 us
    pallas_call x1, Pallas kernels, attention(): pl.pallas_call(functools.partial(attention_kernel, 1.0 / math.sqrt(HD)),...  26.3 us
    all_to_all x3, starting transfers between devices, over_experts(): return lax.all_to_all(part, 'ex', split_axis=0, concat_axis=0, tiled=True)  24.4 us
  transfers between devices with their start and end apart: 49, of which 19 were waited for; matrix products, arithmetic and copies ran while one was open for 6% of the time, Pallas kernels for 26%

profile of v1, /device:TPU:0, one launch (start us, length us, event | category | flops | bytes accessed | tf_op | source)
XLA Modules:
  0.0 454.0 jit_solution(14605167090211945155)
XLA Ops:
  0.0 3.8 fusion
  3.8 7.4 %all-to-all-start = ((bf16[16,128,512]{2,1,0:T(8,128)(2,1)}), bf16[16,128,512]{2,1,0:T(8,128)(2,1)S(1)}, u32[]{:S(2)}, u32[]{:S(2)}) async-start(bf16[16,128,512]{2,1,0:T(8,128)(2,1)} %fusion), calls=%async_computation | async-start | bytes 4194304 | tf_op jit(solution)/shard_map/all_to_all | solution.py:242
  11.2 6.2 %slice_bitcast_fusion = (bf16[16,128,512]{2,1,0:T(8,128)(2,1)}, bf16[16,128,512]{2,1,0:T(8,128)(2,1)}) fusion(f32[16,3,128,512]{3,2,1,0:T(8,128)} %param.17), kind=kLoop, calls=%fused_computation.8 | loop fusion | bytes 8388608 | tf_op jit(solution)/shard_map/convert_element_type | solution.py:268
  17.4 26.3 %attention.1 = f32[576,2048]{1,0:T(8,128)} custom-call(s32[2]{0:T(128)S(1)} %copy-done.5, bf16[576,2048]{1,0:T(8,128)(2,1)S(1)} %bitcast.21, f32[1,2048]{1,0:T(1,128)S(1)} %bitcast.22, bf16[3,2048,1024]{2,1,0:T(8,128)(2,1)} %bitcast.26, bf16[2,2,512,1024]{3,2,1,0:T(8,128)(2,1)} %cache_ref.1, bf16[1024,2048]{1,0:T(8,128)(2,1)} %w_out_ref.1), custom_call_target="tpu_custom_call" | custom-call | flops 10737418240 | bytes 23855104 | tf_op jit(solution)/shard_map/attention/pallas_call | solution.py:76
  43.7 8.5 %all-to-all-done.refs_2_ = bf16[16,128,512]{2,1,0:T(8,128)(2,1)S(1)} async-done(((bf16[16,128,512]{2,1,0:T(8,128)(2,1)}), bf16[16,128,512]{2,1,0:T(8,128)(2,1)S(1)}, u32[]{:S(2)}, u32[]{:S(2)}) %all-to-all-start) | async-done | bytes 2097184 | tf_op jit(solution)/shard_map/all_to_all | solution.py:242
  52.3 11.3 %all-to-all-start.1 = ((bf16[16,128,512]{2,1,0:T(8,128)(2,1)}), bf16[16,128,512]{2,1,0:T(8,128)(2,1)}, u32[]{:S(2)}, u32[]{:S(2)}) async-start(bf16[16,128,512]{2,1,0:T(8,128)(2,1)} %get-tuple-element.72), calls=%async_computation.1 | async-start | bytes 4194304 | tf_op jit(solution)/shard_map/all_to_all | solution.py:242
  63.6 1.8 fusion.1
  71.7 22.7 %collective-permute-done = bf16[288,2048]{1,0:T(8,128)(2,1)} collective-permute-done((bf16[288,2048]{1,0:T(8,128)(2,1)S(1)}, bf16[288,2048]{1,0:T(8,128)(2,1)}, u32[]{:S(2)}, u32[]{:S(2)}) %collective-permute-start) | collective-permute-done | bytes 1179680 | tf_op jit(solution)/shard_map/ppermute | solution.py:283
  94.4 2.6 multiply_reduce_fusion
  99.7 2.2 concatenate.24
  101.9 14.4 %collective-permute-done.1 = bf16[8,128,512]{2,1,0:T(8,128)(2,1)} collective-permute-done((bf16[8,128,512]{2,1,0:T(8,128)(2,1)}, bf16[8,128,512]{2,1,0:T(8,128)(2,1)}, u32[]{:S(2)}, u32[]{:S(2)}) %collective-permute-start.1) | collective-permute-done | bytes 1048608 | tf_op jit(solution)/shard_map/ppermute | solution.py:248
  116.3 5.8 %all-to-all-start.2 = ((bf16[16,128,512]{2,1,0:T(8,128)(2,1)}), bf16[16,128,512]{2,1,0:T(8,128)(2,1)}, u32[]{:S(2)}, u32[]{:S(2)}) async-start(bf16[16,128,512]{2,1,0:T(8,128)(2,1)} %get-tuple-element.77), calls=%async_computation.2 | async-start | bytes 4194304 | tf_op jit(solution)/shard_map/all_to_all | solution.py:242
  124.5 1.9 collective-permute-start.3
  127.9 23.4 %collective-permute-done.4 = bf16[8,128,512]{2,1,0:T(8,128)(2,1)S(1)} collective-permute-done((bf16[8,128,512]{2,1,0:T(8,128)(2,1)S(1)}, bf16[8,128,512]{2,1,0:T(8,128)(2,1)S(1)}, u32[]{:S(2)}, u32[]{:S(2)}) %collective-permute-start.4) | collective-permute-done | bytes 1048608 | tf_op jit(solution)/shard_map/ppermute | solution.py:248
  151.3 19.1 %collective-permute-done.3.refs_0_ = bf16[288,2176]{1,0:T(8,128)(2,1)S(1)} collective-permute-done((bf16[288,2176]{1,0:T(8,128)(2,1)S(1)}, bf16[288,2176]{1,0:T(8,128)(2,1)S(1)}, u32[]{:S(2)}, u32[]{:S(2)}) %collective-permute-start.3) | collective-permute-done | bytes 1253408 | tf_op jit(solution)/shard_map/ppermute | solution.py:316
  170.4 12.9 %collective-permute-start.5 = (bf16[288,2176]{1,0:T(8,128)(2,1)S(1)}, bf16[288,2176]{1,0:T(8,128)(2,1)}, u32[]{:S(2)}, u32[]{:S(2)}) collective-permute-start(bf16[288,2176]{1,0:T(8,128)(2,1)S(1)} %collective-permute-done.3.refs_0_), channel_id=1, source_target_pairs={{0,4},{1,3},{4,8},{5,1},{8,12},{9,5},{12,14},{13,9},{14,10},{15,13... | collective-permute-start | bytes 3760136 | tf_op jit(solution)/shard_map/ppermute | solution.py:316
  187.1 23.7 %collective-permute-done.7 = bf16[8,128,512]{2,1,0:T(8,128)(2,1)} collective-permute-done((bf16[8,128,512]{2,1,0:T(8,128)(2,1)S(1)}, bf16[8,128,512]{2,1,0:T(8,128)(2,1)}, u32[]{:S(2)}, u32[]{:S(2)}) %collective-permute-start.7) | collective-permute-done | bytes 1048608 | tf_op jit(solution)/shard_map/ppermute | solution.py:248
  210.8 11.2 %collective-permute-done.6 = bf16[8,128,512]{2,1,0:T(8,128)(2,1)} collective-permute-done((bf16[8,128,512]{2,1,0:T(8,128)(2,1)S(1)}, bf16[8,128,512]{2,1,0:T(8,128)(2,1)}, u32[]{:S(2)}, u32[]{:S(2)}) %collective-permute-start.6) | collective-permute-done | bytes 1048608 | tf_op jit(solution)/shard_map/ppermute | solution.py:248
  222.1 12.8 %collective-permute-start.8 = (bf16[288,2176]{1,0:T(8,128)(2,1)}, bf16[288,2176]{1,0:T(8,128)(2,1)S(1)}, u32[]{:S(2)}, u32[]{:S(2)}) collective-permute-start(bf16[288,2176]{1,0:T(8,128)(2,1)} %collective-permute-done.5.refs_0_), channel_id=1, source_target_pairs={{0,4},{1,3},{4,8},{5,1},{8,12},{9,5},{12,14},{13,9},{14,10},{15,13... | collective-permute-start | bytes 3760136 | tf_op jit(solution)/shard_map/ppermute | solution.py:316
  235.4 14.3 %collective-permute-done.8.refs_0_ = bf16[288,2176]{1,0:T(8,128)(2,1)S(1)} collective-permute-done((bf16[288,2176]{1,0:T(8,128)(2,1)}, bf16[288,2176]{1,0:T(8,128)(2,1)S(1)}, u32[]{:S(2)}, u32[]{:S(2)}) %collective-permute-start.8) | collective-permute-done | bytes 1253408 | tf_op jit(solution)/shard_map/ppermute | solution.py:316
  249.8 2.6 collective-permute-start.9
  260.5 6.9 %expert_hidden.8 = (bf16[288,1024]{1,0:T(8,128)(2,1)S(1)}, bf16[288,1024]{1,0:T(8,128)(2,1)S(1)}) custom-call(s32[1]{0:T(128)} %bitcast.11.me_ref, bf16[288,2176]{1,0:T(8,128)(2,1)S(1)} %pad_maximum_fusion.refs_0_, bf16[288,2176]{1,0:T(8,128)(2,1)S(1)} %collective-permute-done.10.refs_1_, bf16[16,128,512]{2,1,0:T(8,128)(2,1)S(1)} %all-to-all-done.refs_2_, ...), custom_call_target="tpu_custom_call" | custom-call | flops 4831838208 | bytes 11927552 | tf_op jit(solution)/shard_map/expert_hidden/pallas_call | solution.py:133
  267.4 2.0 collective-permute-start.14
  269.3 6.8 %expert_hidden.9 = (bf16[288,1024]{1,0:T(8,128)(2,1)S(1)}, bf16[288,1024]{1,0:T(8,128)(2,1)S(1)}) custom-call(s32[1]{0:T(128)} %bitcast.11.me_ref, bf16[288,2176]{1,0:T(8,128)(2,1)S(1)} %copy-done.3, bf16[288,2176]{1,0:T(8,128)(2,1)S(1)} %collective-permute-done.15.refs_1_, bf16[16,128,512]{2,1,0:T(8,128)(2,1)S(1)} %all-to-all-done.refs_2_, ...), custom_call_target="tpu_custom_call" | custom-call | flops 4831838208 | bytes 11927552 | tf_op jit(solution)/shard_map/expert_hidden/pallas_call | solution.py:133
  276.1 5.5 %collective-permute-done.11 = bf16[8,128,512]{2,1,0:T(8,128)(2,1)S(1)} collective-permute-done((bf16[8,128,512]{2,1,0:T(8,128)(2,1)S(1)}, bf16[8,128,512]{2,1,0:T(8,128)(2,1)S(1)}, u32[]{:S(2)}, u32[]{:S(2)}) %collective-permute-start.11) | collective-permute-done | bytes 1048608 | tf_op jit(solution)/shard_map/ppermute | solution.py:248
  281.7 22.0 %collective-permute-done.12 = bf16[8,128,512]{2,1,0:T(8,128)(2,1)S(1)} collective-permute-done((bf16[8,128,512]{2,1,0:T(8,128)(2,1)S(1)}, bf16[8,128,512]{2,1,0:T(8,128)(2,1)S(1)}, u32[]{:S(2)}, u32[]{:S(2)}) %collective-permute-start.12) | collective-permute-done | bytes 1048608 | tf_op jit(solution)/shard_map/ppermute | solution.py:248
  303.9 7.2 %expert_hidden.10 = (bf16[288,1024]{1,0:T(8,128)(2,1)S(1)}, bf16[288,1024]{1,0:T(8,128)(2,1)S(1)}) custom-call(s32[1]{0:T(128)} %bitcast.11.me_ref, bf16[288,2176]{1,0:T(8,128)(2,1)} %collective-permute-done.5.refs_0_, bf16[288,2176]{1,0:T(8,128)(2,1)S(1)} %collective-permute-done.16.refs_1_, bf16[16,128,512]{2,1,0:T(8,128)(2,1)S(1)} %all-to-all-done.refs_2_, ...), custom_call_target="tpu_custom_call" | custom-call | flops 4831838208 | bytes 11927552 | tf_op jit(solution)/shard_map/expert_hidden/pallas_call | solution.py:133
  312.8 4.2 expert_down.15
  317.1 4.2 expert_down.14
  322.0 6.8 %expert_hidden.11 = (bf16[288,1024]{1,0:T(8,128)(2,1)S(1)}, bf16[288,1024]{1,0:T(8,128)(2,1)S(1)}) custom-call(s32[1]{0:T(128)} %bitcast.11.me_ref, bf16[288,2176]{1,0:T(8,128)(2,1)S(1)} %collective-permute-done.8.refs_0_, bf16[288,2176]{1,0:T(8,128)(2,1)S(1)} %collective-permute-done.18.refs_1_, bf16[16,128,512]{2,1,0:T(8,128)(2,1)S(1)} %all-to-all-done.refs_2_, ...), custom_call_target="tpu_custom_call" | custom-call | flops 4831838208 | bytes 11927552 | tf_op jit(solution)/shard_map/expert_hidden/pallas_call | solution.py:133
  332.0 4.2 expert_down.13
  336.2 16.0 %collective-permute-done.31.refs_2_ = bf16[288,1024]{1,0:T(8,128)(2,1)S(1)} collective-permute-done((bf16[288,1024]{1,0:T(8,128)(2,1)S(1)}, bf16[288,1024]{1,0:T(8,128)(2,1)S(1)}, u32[]{:S(2)}, u32[]{:S(2)}) %collective-permute-start.31) | collective-permute-done | bytes 589856 | tf_op jit(solution)/shard_map/ppermute | solution.py:347
  353.0 5.5 %collective-permute-done.38.refs_2_ = bf16[288,1024]{1,0:T(8,128)(2,1)S(1)} collective-permute-done((bf16[288,1024]{1,0:T(8,128)(2,1)S(1)}, bf16[288,1024]{1,0:T(8,128)(2,1)S(1)}, u32[]{:S(2)}, u32[]{:S(2)}) %collective-permute-start.38) | collective-permute-done | bytes 589856 | tf_op jit(solution)/shard_map/ppermute | solution.py:347
  359.6 6.8 %expert_hidden.12 = (bf16[288,1024]{1,0:T(8,128)(2,1)S(1)}, bf16[288,1024]{1,0:T(8,128)(2,1)S(1)}) custom-call(s32[1]{0:T(128)} %bitcast.11.me_ref, bf16[288,2176]{1,0:T(8,128)(2,1)S(1)} %collective-permute-done.9.refs_0_, bf16[288,2176]{1,0:T(8,128)(2,1)S(1)} %collective-permute-done.20.refs_1_, bf16[16,128,512]{2,1,0:T(8,128)(2,1)S(1)} %all-to-all-done.refs_2_, ...), custom_call_target="tpu_custom_call" | custom-call | flops 4831838208 | bytes 11927552 | tf_op jit(solution)/shard_map/expert_hidden/pallas_call | solution.py:133
  366.6 4.2 expert_down.12
  372.2 6.8 %expert_hidden.15 = (bf16[288,1024]{1,0:T(8,128)(2,1)S(1)}, bf16[288,1024]{1,0:T(8,128)(2,1)S(1)}) custom-call(s32[1]{0:T(128)} %bitcast.11.me_ref, bf16[288,2176]{1,0:T(8,128)(2,1)S(1)} %collective-permute-done.14.refs_0_, bf16[288,2176]{1,0:T(8,128)(2,1)S(1)} %collective-permute-done.25.refs_1_, bf16[16,128,512]{2,1,0:T(8,128)(2,1)S(1)} %all-to-all-done.refs_2_, ...), custom_call_target="tpu_custom_call" | custom-call | flops 4831838208 | bytes 11927552 | tf_op jit(solution)/shard_map/expert_hidden/pallas_call | solution.py:133
  380.5 4.2 expert_down.11
  386.4 6.8 %expert_hidden.14 = (bf16[288,1024]{1,0:T(8,128)(2,1)S(1)}, bf16[288,1024]{1,0:T(8,128)(2,1)S(1)}) custom-call(s32[1]{0:T(128)} %bitcast.11.me_ref, bf16[288,2176]{1,0:T(8,128)(2,1)S(1)} %collective-permute-done.17.refs_0_, bf16[288,2176]{1,0:T(8,128)(2,1)S(1)} %collective-permute-done.23.refs_1_, bf16[16,128,512]{2,1,0:T(8,128)(2,1)S(1)} %all-to-all-done.refs_2_, ...), custom_call_target="tpu_custom_call" | custom-call | flops 4831838208 | bytes 11927552 | tf_op jit(solution)/shard_map/expert_hidden/pallas_call | solution.py:133
  394.0 4.2 expert_down.10
  400.1 6.8 %expert_hidden.13 = (bf16[288,1024]{1,0:T(8,128)(2,1)S(1)}, bf16[288,1024]{1,0:T(8,128)(2,1)S(1)}) custom-call(s32[1]{0:T(128)} %bitcast.11.me_ref, bf16[288,2176]{1,0:T(8,128)(2,1)S(1)} %collective-permute-done.19.refs_0_, bf16[288,2176]{1,0:T(8,128)(2,1)S(1)} %collective-permute-done.21.refs_1_, bf16[16,128,512]{2,1,0:T(8,128)(2,1)S(1)} %all-to-all-done.refs_2_, ...), custom_call_target="tpu_custom_call" | custom-call | flops 4831838208 | bytes 11927552 | tf_op jit(solution)/shard_map/expert_hidden/pallas_call | solution.py:133
  408.2 4.2 expert_down.9
  414.0 4.2 expert_down.8
  419.2 4.3 collective-permute-done.42.refs_2_
  424.7 5.1 %collective-permute-done.36.refs_2_ = bf16[288,1024]{1,0:T(8,128)(2,1)S(1)} collective-permute-done((bf16[288,1024]{1,0:T(8,128)(2,1)S(1)}, bf16[288,1024]{1,0:T(8,128)(2,1)S(1)}, u32[]{:S(2)}, u32[]{:S(2)}) %collective-permute-start.36) | collective-permute-done | bytes 589856 | tf_op jit(solution)/shard_map/ppermute | solution.py:347
  431.0 5.1 %collective-permute-done.43.refs_2_ = bf16[288,1024]{1,0:T(8,128)(2,1)S(1)} collective-permute-done((bf16[288,1024]{1,0:T(8,128)(2,1)S(1)}, bf16[288,1024]{1,0:T(8,128)(2,1)S(1)}, u32[]{:S(2)}, u32[]{:S(2)}) %collective-permute-start.43) | collective-permute-done | bytes 589856 | tf_op jit(solution)/shard_map/ppermute | solution.py:347
  437.3 5.1 %collective-permute-done.37.refs_2_ = bf16[288,1024]{1,0:T(8,128)(2,1)S(1)} collective-permute-done((bf16[288,1024]{1,0:T(8,128)(2,1)S(1)}, bf16[288,1024]{1,0:T(8,128)(2,1)S(1)}, u32[]{:S(2)}, u32[]{:S(2)}) %collective-permute-start.37) | collective-permute-done | bytes 589856 | tf_op jit(solution)/shard_map/ppermute | solution.py:347
  442.6 6.1 %collective-permute-done.44.refs_2_ = bf16[288,1024]{1,0:T(8,128)(2,1)S(1)} collective-permute-done((bf16[288,1024]{1,0:T(8,128)(2,1)S(1)}, bf16[288,1024]{1,0:T(8,128)(2,1)S(1)}, u32[]{:S(2)}, u32[]{:S(2)}) %collective-permute-start.44) | collective-permute-done | bytes 589856 | tf_op jit(solution)/shard_map/ppermute | solution.py:347
  449.8 2.2 collective-permute-done.45
  (140 shorter events, 50.6 us)
Async XLA Ops:
  3.8 48.5 %all-to-all-start = ((bf16[16,128,512]{2,1,0:T(8,128)(2,1)}), bf16[16,128,512]{2,1,0:T(8,128)(2,1)S(1)}, u32[]{:S(2)}, u32[]{:S(2)}) async-start(bf16[16,128,512]{2,1,0:T(8,128)(2,1)} %fusion), calls=%async_computation | async-start | bytes 4194304 | tf_op jit(solution)/shard_map/all_to_all | solution.py:242
  52.3 64.0 %all-to-all-start.1 = ((bf16[16,128,512]{2,1,0:T(8,128)(2,1)}), bf16[16,128,512]{2,1,0:T(8,128)(2,1)}, u32[]{:S(2)}, u32[]{:S(2)}) async-start(bf16[16,128,512]{2,1,0:T(8,128)(2,1)} %get-tuple-element.72), calls=%async_computation.1 | async-start | bytes 4194304 | tf_op jit(solution)/shard_map/all_to_all | solution.py:242
  65.4 29.0 %collective-permute-start = (bf16[288,2048]{1,0:T(8,128)(2,1)S(1)}, bf16[288,2048]{1,0:T(8,128)(2,1)}, u32[]{:S(2)}, u32[]{:S(2)}) collective-permute-start(bf16[288,2048]{1,0:T(8,128)(2,1)S(1)} %fusion.1), channel_id=1, source_target_pairs={{0,16},{16,0},{1,17},{17,1},{2,18},{18,2},{3,19},{19,3},{4,20},{20... | collective-permute-start | bytes 3538952 | tf_op jit(solution)/shard_map/ppermute | solution.py:283
  71.2 45.1 %collective-permute-start.1 = (bf16[8,128,512]{2,1,0:T(8,128)(2,1)}, bf16[8,128,512]{2,1,0:T(8,128)(2,1)}, u32[]{:S(2)}, u32[]{:S(2)}) collective-permute-start(bf16[8,128,512]{2,1,0:T(8,128)(2,1)} %get-tuple-element.140), channel_id=1, source_target_pairs={{0,16},{16,0},{1,17},{17,1},{2,18},{18,2},{3,19},{19,3},{4,20},{20... | collective-permute-start | bytes 3145736 | tf_op jit(solution)/shard_map/ppermute | solution.py:248
  116.3 105.8 %all-to-all-start.2 = ((bf16[16,128,512]{2,1,0:T(8,128)(2,1)}), bf16[16,128,512]{2,1,0:T(8,128)(2,1)}, u32[]{:S(2)}, u32[]{:S(2)}) async-start(bf16[16,128,512]{2,1,0:T(8,128)(2,1)} %get-tuple-element.77), calls=%async_computation.2 | async-start | bytes 4194304 | tf_op jit(solution)/shard_map/all_to_all | solution.py:242
  124.5 45.9 %collective-permute-start.3 = (bf16[288,2176]{1,0:T(8,128)(2,1)S(1)}, bf16[288,2176]{1,0:T(8,128)(2,1)S(1)}, u32[]{:S(2)}, u32[]{:S(2)}) collective-permute-start(bf16[288,2176]{1,0:T(8,128)(2,1)S(1)} %pad_maximum_fusion.refs_0_), channel_id=1, source_target_pairs={{0,4},{1,3},{4,8},{5,1},{8,12},{9,5},{12,14},{13,9},{14,10},{15,13... | collective-permute-start | bytes 3760136 | tf_op jit(solution)/shard_map/ppermute | solution.py:316
  126.4 24.9 %collective-permute-start.4 = (bf16[8,128,512]{2,1,0:T(8,128)(2,1)S(1)}, bf16[8,128,512]{2,1,0:T(8,128)(2,1)S(1)}, u32[]{:S(2)}, u32[]{:S(2)}) collective-permute-start(bf16[8,128,512]{2,1,0:T(8,128)(2,1)S(1)} %copy-done.10), channel_id=1, source_target_pairs={{0,16},{16,0},{1,17},{17,1},{2,18},{18,2},{3,19},{19,3},{4,20},{20... | collective-permute-start | bytes 3145736 | tf_op jit(solution)/shard_map/ppermute | solution.py:248
  170.4 51.7 %collective-permute-start.5 = (bf16[288,2176]{1,0:T(8,128)(2,1)S(1)}, bf16[288,2176]{1,0:T(8,128)(2,1)}, u32[]{:S(2)}, u32[]{:S(2)}) collective-permute-start(bf16[288,2176]{1,0:T(8,128)(2,1)S(1)} %collective-permute-done.3.refs_0_), channel_id=1, source_target_pairs={{0,4},{1,3},{4,8},{5,1},{8,12},{9,5},{12,14},{13,9},{14,10},{15,13... | collective-permute-start | bytes 3760136 | tf_op jit(solution)/shard_map/ppermute | solution.py:316
  185.0 25.8 %collective-permute-start.7 = (bf16[8,128,512]{2,1,0:T(8,128)(2,1)S(1)}, bf16[8,128,512]{2,1,0:T(8,128)(2,1)}, u32[]{:S(2)}, u32[]{:S(2)}) collective-permute-start(bf16[8,128,512]{2,1,0:T(8,128)(2,1)S(1)} %get-tuple-element.137), channel_id=1, source_target_pairs={{0,16},{16,0},{1,17},{17,1},{2,18},{18,2},{3,19},{19,3},{4,20},{20... | collective-permute-start | bytes 3145736 | tf_op jit(solution)/shard_map/ppermute | solution.py:248
  186.6 35.5 %collective-permute-start.6 = (bf16[8,128,512]{2,1,0:T(8,128)(2,1)S(1)}, bf16[8,128,512]{2,1,0:T(8,128)(2,1)}, u32[]{:S(2)}, u32[]{:S(2)}) collective-permute-start(bf16[8,128,512]{2,1,0:T(8,128)(2,1)S(1)} %get-tuple-element.138), channel_id=1, source_target_pairs={{0,16},{16,0},{1,17},{17,1},{2,18},{18,2},{3,19},{19,3},{4,20},{20... | collective-permute-start | bytes 3145736 | tf_op jit(solution)/shard_map/ppermute | solution.py:248
  222.1 27.7 %collective-permute-start.8 = (bf16[288,2176]{1,0:T(8,128)(2,1)}, bf16[288,2176]{1,0:T(8,128)(2,1)S(1)}, u32[]{:S(2)}, u32[]{:S(2)}) collective-permute-start(bf16[288,2176]{1,0:T(8,128)(2,1)} %collective-permute-done.5.refs_0_), channel_id=1, source_target_pairs={{0,4},{1,3},{4,8},{5,1},{8,12},{9,5},{12,14},{13,9},{14,10},{15,13... | collective-permute-start | bytes 3760136 | tf_op jit(solution)/shard_map/ppermute | solution.py:316
  234.9 24.9 %collective-permute-start.10 = (bf16[288,2176]{1,0:T(8,128)(2,1)S(1)}, bf16[288,2176]{1,0:T(8,128)(2,1)S(1)}, u32[]{:S(2)}, u32[]{:S(2)}) collective-permute-start(bf16[288,2176]{1,0:T(8,128)(2,1)S(1)} %pad_maximum_fusion.refs_0_), channel_id=1, source_target_pairs={{0,1},{1,0},{2,3},{3,2},{4,5},{5,4},{6,7},{7,6},{8,9},{9,8},{10,11... | collective-permute-start | bytes 3760136 | tf_op jit(solution)/shard_map/ppermute | solution.py:312
  234.9 34.4 %collective-permute-start.15 = (bf16[288,2176]{1,0:T(8,128)(2,1)}, bf16[288,2176]{1,0:T(8,128)(2,1)S(1)}, u32[]{:S(2)}, u32[]{:S(2)}) collective-permute-start(bf16[288,2176]{1,0:T(8,128)(2,1)} %copy-done.2), channel_id=1, source_target_pairs={{0,1},{1,0},{2,3},{3,2},{4,5},{5,4},{6,7},{7,6},{8,9},{9,8},{10,11... | collective-permute-start | bytes 3760136 | tf_op jit(solution)/shard_map/ppermute | solution.py:312
  249.8 17.6 %collective-permute-start.9 = (bf16[288,2176]{1,0:T(8,128)(2,1)S(1)}, bf16[288,2176]{1,0:T(8,128)(2,1)S(1)}, u32[]{:S(2)}, u32[]{:S(2)}) collective-permute-start(bf16[288,2176]{1,0:T(8,128)(2,1)S(1)} %collective-permute-done.8.refs_0_), channel_id=1, source_target_pairs={{0,4},{1,3},{4,8},{5,1},{8,12},{9,5},{12,14},{13,9},{14,10},{15,13... | collective-permute-start | bytes 3760136 | tf_op jit(solution)/shard_map/ppermute | solution.py:316
  253.8 50.1 %collective-permute-start.16 = (bf16[288,2176]{1,0:T(8,128)(2,1)}, bf16[288,2176]{1,0:T(8,128)(2,1)S(1)}, u32[]{:S(2)}, u32[]{:S(2)}) collective-permute-start(bf16[288,2176]{1,0:T(8,128)(2,1)} %collective-permute-done.5.refs_0_), channel_id=1, source_target_pairs={{0,1},{1,0},{2,3},{3,2},{4,5},{5,4},{6,7},{7,6},{8,9},{9,8},{10,11... | collective-permute-start | bytes 3760136 | tf_op jit(solution)/shard_map/ppermute | solution.py:312
  255.6 26.0 %collective-permute-start.11 = (bf16[8,128,512]{2,1,0:T(8,128)(2,1)S(1)}, bf16[8,128,512]{2,1,0:T(8,128)(2,1)S(1)}, u32[]{:S(2)}, u32[]{:S(2)}) collective-permute-start(bf16[8,128,512]{2,1,0:T(8,128)(2,1)S(1)} %get-tuple-element.136), channel_id=1, source_target_pairs={{0,16},{16,0},{1,17},{17,1},{2,18},{18,2},{3,19},{19,3},{4,20},{20... | collective-permute-start | bytes 3145736 | tf_op jit(solution)/shard_map/ppermute | solution.py:248
  259.9 43.8 %collective-permute-start.12 = (bf16[8,128,512]{2,1,0:T(8,128)(2,1)S(1)}, bf16[8,128,512]{2,1,0:T(8,128)(2,1)S(1)}, u32[]{:S(2)}, u32[]{:S(2)}) collective-permute-start(bf16[8,128,512]{2,1,0:T(8,128)(2,1)S(1)} %get-tuple-element.135), channel_id=1, source_target_pairs={{0,16},{16,0},{1,17},{17,1},{2,18},{18,2},{3,19},{19,3},{4,20},{20... | collective-permute-start | bytes 3145736 | tf_op jit(solution)/shard_map/ppermute | solution.py:248
  267.4 43.7 %collective-permute-start.14 = (bf16[288,2176]{1,0:T(8,128)(2,1)S(1)}, bf16[288,2176]{1,0:T(8,128)(2,1)S(1)}, u32[]{:S(2)}, u32[]{:S(2)}) collective-permute-start(bf16[288,2176]{1,0:T(8,128)(2,1)S(1)} %collective-permute-done.9.refs_0_), channel_id=1, source_target_pairs={{0,4},{1,3},{4,8},{5,1},{8,12},{9,5},{12,14},{13,9},{14,10},{15,13... | collective-permute-start | bytes 3760136 | tf_op jit(solution)/shard_map/ppermute | solution.py:316
  303.8 18.2 %collective-permute-start.18 = (bf16[288,2176]{1,0:T(8,128)(2,1)S(1)}, bf16[288,2176]{1,0:T(8,128)(2,1)S(1)}, u32[]{:S(2)}, u32[]{:S(2)}) collective-permute-start(bf16[288,2176]{1,0:T(8,128)(2,1)S(1)} %collective-permute-done.8.refs_0_), channel_id=1, source_target_pairs={{0,1},{1,0},{2,3},{3,2},{4,5},{5,4},{6,7},{7,6},{8,9},{9,8},{10,11... | collective-permute-start | bytes 3760136 | tf_op jit(solution)/shard_map/ppermute | solution.py:312
  311.1 17.7 %collective-permute-start.17 = (bf16[288,2176]{1,0:T(8,128)(2,1)S(1)}, bf16[288,2176]{1,0:T(8,128)(2,1)S(1)}, u32[]{:S(2)}, u32[]{:S(2)}) collective-permute-start(bf16[288,2176]{1,0:T(8,128)(2,1)S(1)} %collective-permute-done.14.refs_0_), channel_id=1, source_target_pairs={{0,4},{1,3},{4,8},{5,1},{8,12},{9,5},{12,14},{13,9},{14,10},{15,13... | collective-permute-start | bytes 3760136 | tf_op jit(solution)/shard_map/ppermute | solution.py:316
  317.1 12.8 %collective-permute-start.30 = (bf16[288,2048]{1,0:T(8,128)(2,1)S(1)}, bf16[288,2048]{1,0:T(8,128)(2,1)S(1)}, u32[]{:S(2)}, u32[]{:S(2)}) collective-permute-start(bf16[288,2048]{1,0:T(8,128)(2,1)S(1)} %get-tuple-element.130), channel_id=1, source_target_pairs={{0,1},{1,0},{2,3},{3,2},{4,5},{5,4},{6,7},{7,6},{8,9},{9,8},{10,11... | collective-permute-start | bytes 3538952 | tf_op jit(solution)/shard_map/ppermute | solution.py:338
  321.4 10.6 %collective-permute-start.29 = (bf16[288,2048]{1,0:T(8,128)(2,1)S(1)}, bf16[288,2048]{1,0:T(8,128)(2,1)S(1)}, u32[]{:S(2)}, u32[]{:S(2)}) collective-permute-start(bf16[288,2048]{1,0:T(8,128)(2,1)S(1)} %get-tuple-element.126), channel_id=1, source_target_pairs={{0,1},{1,0},{2,3},{3,2},{4,5},{5,4},{6,7},{7,6},{8,9},{9,8},{10,11... | collective-permute-start | bytes 3538952 | tf_op jit(solution)/shard_map/ppermute | solution.py:338
  321.9 30.5 %collective-permute-start.20 = (bf16[288,2176]{1,0:T(8,128)(2,1)S(1)}, bf16[288,2176]{1,0:T(8,128)(2,1)S(1)}, u32[]{:S(2)}, u32[]{:S(2)}) collective-permute-start(bf16[288,2176]{1,0:T(8,128)(2,1)S(1)} %collective-permute-done.9.refs_0_), channel_id=1, source_target_pairs={{0,1},{1,0},{2,3},{3,2},{4,5},{5,4},{6,7},{7,6},{8,9},{9,8},{10,11... | collective-permute-start | bytes 3760136 | tf_op jit(solution)/shard_map/ppermute | solution.py:312
  328.8 37.8 %collective-permute-start.19 = (bf16[288,2176]{1,0:T(8,128)(2,1)S(1)}, bf16[288,2176]{1,0:T(8,128)(2,1)S(1)}, u32[]{:S(2)}, u32[]{:S(2)}) collective-permute-start(bf16[288,2176]{1,0:T(8,128)(2,1)S(1)} %collective-permute-done.17.refs_0_), channel_id=1, source_target_pairs={{0,4},{1,3},{4,8},{5,1},{8,12},{9,5},{12,14},{13,9},{14,10},{15,13... | collective-permute-start | bytes 3760136 | tf_op jit(solution)/shard_map/ppermute | solution.py:316
  330.0 22.2 %collective-permute-start.31 = (bf16[288,1024]{1,0:T(8,128)(2,1)S(1)}, bf16[288,1024]{1,0:T(8,128)(2,1)S(1)}, u32[]{:S(2)}, u32[]{:S(2)}) collective-permute-start(bf16[288,1024]{1,0:T(8,128)(2,1)S(1)} %add_terms.16), channel_id=1, source_target_pairs={{0,4},{1,3},{4,8},{5,1},{8,12},{9,5},{12,14},{13,9},{14,10},{15,13... | collective-permute-start | bytes 1769480 | tf_op jit(solution)/shard_map/ppermute | solution.py:347
  331.3 27.1 %collective-permute-start.38 = (bf16[288,1024]{1,0:T(8,128)(2,1)S(1)}, bf16[288,1024]{1,0:T(8,128)(2,1)S(1)}, u32[]{:S(2)}, u32[]{:S(2)}) collective-permute-start(bf16[288,1024]{1,0:T(8,128)(2,1)S(1)} %add_terms.24), channel_id=1, source_target_pairs={{0,4},{1,3},{4,8},{5,1},{8,12},{9,5},{12,14},{13,9},{14,10},{15,13... | collective-permute-start | bytes 1769480 | tf_op jit(solution)/shard_map/ppermute | solution.py:347
  332.0 39.0 %collective-permute-start.25 = (bf16[288,2176]{1,0:T(8,128)(2,1)S(1)}, bf16[288,2176]{1,0:T(8,128)(2,1)S(1)}, u32[]{:S(2)}, u32[]{:S(2)}) collective-permute-start(bf16[288,2176]{1,0:T(8,128)(2,1)S(1)} %collective-permute-done.14.refs_0_), channel_id=1, source_target_pairs={{0,1},{1,0},{2,3},{3,2},{4,5},{5,4},{6,7},{7,6},{8,9},{9,8},{10,11... | collective-permute-start | bytes 3760136 | tf_op jit(solution)/shard_map/ppermute | solution.py:312
  352.2 26.9 %collective-permute-start.28 = (bf16[288,2048]{1,0:T(8,128)(2,1)S(1)}, bf16[288,2048]{1,0:T(8,128)(2,1)S(1)}, u32[]{:S(2)}, u32[]{:S(2)}) collective-permute-start(bf16[288,2048]{1,0:T(8,128)(2,1)S(1)} %get-tuple-element.122), channel_id=1, source_target_pairs={{0,1},{1,0},{2,3},{3,2},{4,5},{5,4},{6,7},{7,6},{8,9},{9,8},{10,11... | collective-permute-start | bytes 3538952 | tf_op jit(solution)/shard_map/ppermute | solution.py:338
  352.4 32.7 %collective-permute-start.23 = (bf16[288,2176]{1,0:T(8,128)(2,1)S(1)}, bf16[288,2176]{1,0:T(8,128)(2,1)S(1)}, u32[]{:S(2)}, u32[]{:S(2)}) collective-permute-start(bf16[288,2176]{1,0:T(8,128)(2,1)S(1)} %collective-permute-done.17.refs_0_), channel_id=1, source_target_pairs={{0,1},{1,0},{2,3},{3,2},{4,5},{5,4},{6,7},{7,6},{8,9},{9,8},{10,11... | collective-permute-start | bytes 3760136 | tf_op jit(solution)/shard_map/ppermute | solution.py:312
  358.5 13.7 %collective-permute-start.32 = (bf16[288,1024]{1,0:T(8,128)(2,1)S(1)}, bf16[288,1024]{1,0:T(8,128)(2,1)S(1)}, u32[]{:S(2)}, u32[]{:S(2)}) collective-permute-start(bf16[288,1024]{1,0:T(8,128)(2,1)S(1)} %add_terms.17), channel_id=1, source_target_pairs={{0,4},{1,3},{4,8},{5,1},{8,12},{9,5},{12,14},{13,9},{14,10},{15,13... | collective-permute-start | bytes 1769480 | tf_op jit(solution)/shard_map/ppermute | solution.py:347
  370.9 22.3 %collective-permute-start.27 = (bf16[288,2048]{1,0:T(8,128)(2,1)S(1)}, bf16[288,2048]{1,0:T(8,128)(2,1)S(1)}, u32[]{:S(2)}, u32[]{:S(2)}) collective-permute-start(bf16[288,2048]{1,0:T(8,128)(2,1)S(1)} %get-tuple-element.118), channel_id=1, source_target_pairs={{0,1},{1,0},{2,3},{3,2},{4,5},{5,4},{6,7},{7,6},{8,9},{9,8},{10,11... | collective-permute-start | bytes 3538952 | tf_op jit(solution)/shard_map/ppermute | solution.py:338
  371.0 13.8 %collective-permute-start.39 = (bf16[288,1024]{1,0:T(8,128)(2,1)S(1)}, bf16[288,1024]{1,0:T(8,128)(2,1)S(1)}, u32[]{:S(2)}, u32[]{:S(2)}) collective-permute-start(bf16[288,1024]{1,0:T(8,128)(2,1)S(1)} %add_terms.25), channel_id=1, source_target_pairs={{0,4},{1,3},{4,8},{5,1},{8,12},{9,5},{12,14},{13,9},{14,10},{15,13... | collective-permute-start | bytes 1769480 | tf_op jit(solution)/shard_map/ppermute | solution.py:347
  372.2 27.9 %collective-permute-start.21 = (bf16[288,2176]{1,0:T(8,128)(2,1)S(1)}, bf16[288,2176]{1,0:T(8,128)(2,1)S(1)}, u32[]{:S(2)}, u32[]{:S(2)}) collective-permute-start(bf16[288,2176]{1,0:T(8,128)(2,1)S(1)} %collective-permute-done.19.refs_0_), channel_id=1, source_target_pairs={{0,1},{1,0},{2,3},{3,2},{4,5},{5,4},{6,7},{7,6},{8,9},{9,8},{10,11... | collective-permute-start | bytes 3760136 | tf_op jit(solution)/shard_map/ppermute | solution.py:312
  379.3 13.9 %collective-permute-start.33 = (bf16[288,1024]{1,0:T(8,128)(2,1)S(1)}, bf16[288,1024]{1,0:T(8,128)(2,1)S(1)}, u32[]{:S(2)}, u32[]{:S(2)}) collective-permute-start(bf16[288,1024]{1,0:T(8,128)(2,1)S(1)} %add_terms.18), channel_id=1, source_target_pairs={{0,4},{1,3},{4,8},{5,1},{8,12},{9,5},{12,14},{13,9},{14,10},{15,13... | collective-permute-start | bytes 1769480 | tf_op jit(solution)/shard_map/ppermute | solution.py:347
  384.7 22.2 %collective-permute-start.26 = (bf16[288,2048]{1,0:T(8,128)(2,1)S(1)}, bf16[288,2048]{1,0:T(8,128)(2,1)S(1)}, u32[]{:S(2)}, u32[]{:S(2)}) collective-permute-start(bf16[288,2048]{1,0:T(8,128)(2,1)S(1)} %get-tuple-element.114), channel_id=1, source_target_pairs={{0,1},{1,0},{2,3},{3,2},{4,5},{5,4},{6,7},{7,6},{8,9},{9,8},{10,11... | collective-permute-start | bytes 3538952 | tf_op jit(solution)/shard_map/ppermute | solution.py:338
  385.1 13.2 %collective-permute-start.40 = (bf16[288,1024]{1,0:T(8,128)(2,1)S(1)}, bf16[288,1024]{1,0:T(8,128)(2,1)S(1)}, u32[]{:S(2)}, u32[]{:S(2)}) collective-permute-start(bf16[288,1024]{1,0:T(8,128)(2,1)S(1)} %add_terms.26), channel_id=1, source_target_pairs={{0,4},{1,3},{4,8},{5,1},{8,12},{9,5},{12,14},{13,9},{14,10},{15,13... | collective-permute-start | bytes 1769480 | tf_op jit(solution)/shard_map/ppermute | solution.py:347
  393.4 13.6 %collective-permute-start.34 = (bf16[288,1024]{1,0:T(8,128)(2,1)S(1)}, bf16[288,1024]{1,0:T(8,128)(2,1)S(1)}, u32[]{:S(2)}, u32[]{:S(2)}) collective-permute-start(bf16[288,1024]{1,0:T(8,128)(2,1)S(1)} %add_terms.19), channel_id=1, source_target_pairs={{0,4},{1,3},{4,8},{5,1},{8,12},{9,5},{12,14},{13,9},{14,10},{15,13... | collective-permute-start | bytes 1769480 | tf_op jit(solution)/shard_map/ppermute | solution.py:347
  398.2 19.9 %collective-permute-start.24 = (bf16[288,2048]{1,0:T(8,128)(2,1)S(1)}, bf16[288,2048]{1,0:T(8,128)(2,1)S(1)}, u32[]{:S(2)}, u32[]{:S(2)}) collective-permute-start(bf16[288,2048]{1,0:T(8,128)(2,1)S(1)} %get-tuple-element.110), channel_id=1, source_target_pairs={{0,1},{1,0},{2,3},{3,2},{4,5},{5,4},{6,7},{7,6},{8,9},{9,8},{10,11... | collective-permute-start | bytes 3538952 | tf_op jit(solution)/shard_map/ppermute | solution.py:338
  398.6 13.9 %collective-permute-start.41 = (bf16[288,1024]{1,0:T(8,128)(2,1)S(1)}, bf16[288,1024]{1,0:T(8,128)(2,1)S(1)}, u32[]{:S(2)}, u32[]{:S(2)}) collective-permute-start(bf16[288,1024]{1,0:T(8,128)(2,1)S(1)} %add_terms.27), channel_id=1, source_target_pairs={{0,4},{1,3},{4,8},{5,1},{8,12},{9,5},{12,14},{13,9},{14,10},{15,13... | collective-permute-start | bytes 1769480 | tf_op jit(solution)/shard_map/ppermute | solution.py:347
  407.2 11.0 %collective-permute-start.35 = (bf16[288,1024]{1,0:T(8,128)(2,1)S(1)}, bf16[288,1024]{1,0:T(8,128)(2,1)S(1)}, u32[]{:S(2)}, u32[]{:S(2)}) collective-permute-start(bf16[288,1024]{1,0:T(8,128)(2,1)S(1)} %add_terms.20), channel_id=1, source_target_pairs={{0,4},{1,3},{4,8},{5,1},{8,12},{9,5},{12,14},{13,9},{14,10},{15,13... | collective-permute-start | bytes 1769480 | tf_op jit(solution)/shard_map/ppermute | solution.py:347
  412.4 12.2 %collective-permute-start.22 = (bf16[288,2048]{1,0:T(8,128)(2,1)S(1)}, bf16[288,2048]{1,0:T(8,128)(2,1)S(1)}, u32[]{:S(2)}, u32[]{:S(2)}) collective-permute-start(bf16[288,2048]{1,0:T(8,128)(2,1)S(1)} %get-tuple-element.106), channel_id=1, source_target_pairs={{0,1},{1,0},{2,3},{3,2},{4,5},{5,4},{6,7},{7,6},{8,9},{9,8},{10,11... | collective-permute-start | bytes 3538952 | tf_op jit(solution)/shard_map/ppermute | solution.py:338
  412.7 10.7 %collective-permute-start.42 = (bf16[288,1024]{1,0:T(8,128)(2,1)S(1)}, bf16[288,1024]{1,0:T(8,128)(2,1)S(1)}, u32[]{:S(2)}, u32[]{:S(2)}) collective-permute-start(bf16[288,1024]{1,0:T(8,128)(2,1)S(1)} %add_terms.28), channel_id=1, source_target_pairs={{0,4},{1,3},{4,8},{5,1},{8,12},{9,5},{12,14},{13,9},{14,10},{15,13... | collective-permute-start | bytes 1769480 | tf_op jit(solution)/shard_map/ppermute | solution.py:347
  418.4 11.3 %collective-permute-start.36 = (bf16[288,1024]{1,0:T(8,128)(2,1)S(1)}, bf16[288,1024]{1,0:T(8,128)(2,1)S(1)}, u32[]{:S(2)}, u32[]{:S(2)}) collective-permute-start(bf16[288,1024]{1,0:T(8,128)(2,1)S(1)} %add_terms.21), channel_id=1, source_target_pairs={{0,4},{1,3},{4,8},{5,1},{8,12},{9,5},{12,14},{13,9},{14,10},{15,13... | collective-permute-start | bytes 1769480 | tf_op jit(solution)/shard_map/ppermute | solution.py:347
  419.2 18.1 %collective-permute-start.13 = (bf16[288,2048]{1,0:T(8,128)(2,1)S(1)}, bf16[288,2048]{1,0:T(8,128)(2,1)S(1)}, u32[]{:S(2)}, u32[]{:S(2)}) collective-permute-start(bf16[288,2048]{1,0:T(8,128)(2,1)S(1)} %get-tuple-element.89), channel_id=1, source_target_pairs={{0,1},{1,0},{2,3},{3,2},{4,5},{5,4},{6,7},{7,6},{8,9},{9,8},{10,11... | collective-permute-start | bytes 3538952 | tf_op jit(solution)/shard_map/ppermute | solution.py:338
  423.6 12.4 %collective-permute-start.43 = (bf16[288,1024]{1,0:T(8,128)(2,1)S(1)}, bf16[288,1024]{1,0:T(8,128)(2,1)S(1)}, u32[]{:S(2)}, u32[]{:S(2)}) collective-permute-start(bf16[288,1024]{1,0:T(8,128)(2,1)S(1)} %add_terms.29), channel_id=1, source_target_pairs={{0,4},{1,3},{4,8},{5,1},{8,12},{9,5},{12,14},{13,9},{14,10},{15,13... | collective-permute-start | bytes 1769480 | tf_op jit(solution)/shard_map/ppermute | solution.py:347
  430.0 12.4 %collective-permute-start.37 = (bf16[288,1024]{1,0:T(8,128)(2,1)S(1)}, bf16[288,1024]{1,0:T(8,128)(2,1)S(1)}, u32[]{:S(2)}, u32[]{:S(2)}) collective-permute-start(bf16[288,1024]{1,0:T(8,128)(2,1)S(1)} %add_terms.22), channel_id=1, source_target_pairs={{0,4},{1,3},{4,8},{5,1},{8,12},{9,5},{12,14},{13,9},{14,10},{15,13... | collective-permute-start | bytes 1769480 | tf_op jit(solution)/shard_map/ppermute | solution.py:347
  436.3 12.4 %collective-permute-start.44 = (bf16[288,1024]{1,0:T(8,128)(2,1)S(1)}, bf16[288,1024]{1,0:T(8,128)(2,1)S(1)}, u32[]{:S(2)}, u32[]{:S(2)}) collective-permute-start(bf16[288,1024]{1,0:T(8,128)(2,1)S(1)} %add_terms.30), channel_id=1, source_target_pairs={{0,4},{1,3},{4,8},{5,1},{8,12},{9,5},{12,14},{13,9},{14,10},{15,13... | collective-permute-start | bytes 1769480 | tf_op jit(solution)/shard_map/ppermute | solution.py:347
  449.8 2.2 collective-permute-start.45
  (15 other events, 169.0 us)

commit v2 on v1

--- a/solution.py
+++ b/solution.py
@@ -242,17 +242,10 @@
         return lax.all_to_all(part, "ex", split_axis=0, concat_axis=0, tiled=True)
 
     def over_kv(part):
-        middle = part.shape[0] // 2
         return [
-            [
-                lax.ppermute(half, "kv", [(i, (i + turn) % kv) for i in range(kv)])
-                for turn in range(1, kv)
-            ]
-            for half in (part[:middle], part[middle:])
+            lax.ppermute(part, "kv", [(i, (i + turn) % kv) for i in range(kv)])
+            for turn in range(1, kv)
         ]
-
-    def joined(halves):
-        return [jnp.concatenate(pair, axis=0) for pair in zip(*halves)]
 
     probs = route_probs[0]
     share = probs / jnp.sum(probs, axis=-1, keepdims=True)
@@ -284,7 +277,7 @@
         resid = resid + sent.astype(jnp.float32)
     moe_in = rms_scale(resid, moe_gain).astype(jnp.bfloat16)
     moe_in = jnp.concatenate([moe_in, factor], axis=1)
-    moe_in, gates[0], up, down = lax.optimization_barrier((moe_in, gates[0], up, down))
+    moe_in, up, down = lax.optimization_barrier((moe_in, up, down))
     ups = over_kv(up)
     down = over_experts(down)
 
@@ -305,7 +298,7 @@
     got = lax.ppermute(half_of(moe_in, 1 - core), "ex", swap)
     held = jnp.concatenate([half_of(moe_in, core), got], axis=0)
     first_weights = [gate, up]
-    due = {4: [0], 5: [1, 2], 6: [3], 7: [4]}
+    due = {3: [0], 4: [1], 5: [2], 6: [3], 7: [4]}
     blocks, hiddens = [held], {}
 
     def hidden_of(step):
@@ -315,12 +308,14 @@
     for step in range(1, chips):
         held = lax.ppermute(held, "ex", ring)
         if step == 1:
-            held, gates[1] = lax.optimization_barrier((held, gates[1]))
+            held, gates = lax.optimization_barrier((held, gates))
         if step == 2:
             held, ups, down = lax.optimization_barrier((held, ups, down))
             downs = over_kv(down)
-            for pair in zip(joined(gates), joined(ups)):
+            for pair in zip(gates, ups):
                 first_weights += pair
+        if step == min(4, chips - 1):
+            held, downs = lax.optimization_barrier((held, downs))
         blocks.append(held)
         for early in due.get(step, []):
             hiddens[early] = hidden_of(early)
@@ -330,7 +325,6 @@
         if step not in hiddens:
             hiddens[step] = hidden_of(step)
     hiddens = [hiddens[step] for step in range(chips)]
-    downs = joined(downs)
     keeps, gots = [], []
     for pair in hiddens:
         keep, give = expert_down(pair, [down] + downs)

time: 462 us -> 424 us (0.918)
  waiting for transfers between devices: 216 us -> 193 us
  starting transfers between devices: 84.8 us -> 73.5 us
    ppermute x7, waiting for transfers between devices: 33.4 us -> 11 us  [on_device(): held = lax.ppermute(held, 'ex', ring)]
    ppermute x7, starting transfers between devices: 34.9 us -> 18.3 us  [on_device(): held = lax.ppermute(held, 'ex', ring)]
    all_to_all x3, starting transfers between devices: 24.4 us -> 29.9 us  [over_experts(): return lax.all_to_all(part, 'ex', split_axis=0, concat_axis=0, tiled=True)]
    slice x3 -> x0, local copies, waits for them, and re-layouts: 4.98 us -> none  [over_kv(): part[middle:]]
    ppermute x6 -> x3, waiting for transfers between devices: 100 us -> 98.3 us  [over_kv(): lax.ppermute(part, 'kv', [(i, (i + turn) % kv) for i in range(kv)])]
  transfers between devices with their start and end apart: 49 -> 46, of which waited for: 19 -> 18; matrix products, arithmetic and copies ran while one was open for 6% -> 4% of each run, Pallas kernels for 26% -> 28%
where the time goes in v2:
time: 424 us; the launch traced here: 417 us
  waiting for transfers between devices  193 us (46%)
  Pallas kernels  119 us (28%)
  starting transfers between devices  73.5 us (17%)
  local copies, waits for them, and re-layouts  21.4 us (5%)
  other arithmetic  9.4 us (2%)
    ppermute x3, waiting for transfers between devices, over_kv(): lax.ppermute(part, 'kv', [(i, (i + turn) % kv) for i in range(kv)])  98.3 us
    pallas_call x8, Pallas kernels, expert_hidden(): pl.pallas_call(functools.partial(hidden_kernel, experts, width), in_specs...  55.1 us
    ppermute x14, waiting for transfers between devices, on_device(): running = lax.ppermute(running, 'ex', ring)  44.5 us
    pallas_call x8, Pallas kernels, expert_down(): pl.pallas_call(down_kernel, in_specs=[vmem] * (2 + len(weights)), out_spe...  34.2 us
    all_to_all x3, starting transfers between devices, over_experts(): return lax.all_to_all(part, 'ex', split_axis=0, concat_axis=0, tiled=True)  29.9 us
    pallas_call x1, Pallas kernels, attention(): pl.pallas_call(functools.partial(attention_kernel, 1.0 / math.sqrt(HD)),...  26.4 us
    ppermute x1, waiting for transfers between devices, on_device(): sent = lax.ppermute(sent, 'kv', [(i, (i + turn) % kv) for i in range(kv)])  24.2 us
    ppermute x7, starting transfers between devices, on_device(): held = lax.ppermute(held, 'ex', ring)  18.3 us
  transfers between devices with their start and end apart: 46, of which 18 were waited for; matrix products, arithmetic and copies ran while one was open for 4% of the time, Pallas kernels for 28%

profile of v2, /device:TPU:0, one launch (start us, length us, event | category | flops | bytes accessed | tf_op | source)
XLA Modules:
  0.0 416.9 jit_solution(13733718889759006571)
XLA Ops:
  0.0 3.8 fusion
  3.8 7.4 %all-to-all-start = ((bf16[16,128,512]{2,1,0:T(8,128)(2,1)}), bf16[16,128,512]{2,1,0:T(8,128)(2,1)S(1)}, u32[]{:S(2)}, u32[]{:S(2)}) async-start(bf16[16,128,512]{2,1,0:T(8,128)(2,1)} %fusion), calls=%async_computation | async-start | bytes 4194304 | tf_op jit(solution)/shard_map/all_to_all | solution.py:242
  11.2 6.3 %slice_bitcast_fusion = (bf16[16,128,512]{2,1,0:T(8,128)(2,1)}, bf16[16,128,512]{2,1,0:T(8,128)(2,1)}) fusion(f32[16,3,128,512]{3,2,1,0:T(8,128)} %param.17), kind=kLoop, calls=%fused_computation.8 | loop fusion | bytes 8388608 | tf_op jit(solution)/shard_map/convert_element_type | solution.py:261
  17.5 26.4 %attention.1 = f32[576,2048]{1,0:T(8,128)} custom-call(s32[2]{0:T(128)S(1)} %copy-done.10, bf16[576,2048]{1,0:T(8,128)(2,1)S(1)} %bitcast.21, f32[1,2048]{1,0:T(1,128)S(1)} %bitcast.22, bf16[3,2048,1024]{2,1,0:T(8,128)(2,1)} %bitcast.26, bf16[2,2,512,1024]{3,2,1,0:T(8,128)(2,1)} %cache_ref.1, bf16[1024,2048]{1,0:T(8,128)(2,1)} %w_out_ref.1), custom_call_target="tpu_custom_call" | custom-call | flops 10737418240 | bytes 23855104 | tf_op jit(solution)/shard_map/attention/pallas_call | solution.py:76
  43.8 8.4 %all-to-all-done.refs_2_ = bf16[16,128,512]{2,1,0:T(8,128)(2,1)S(1)} async-done(((bf16[16,128,512]{2,1,0:T(8,128)(2,1)}), bf16[16,128,512]{2,1,0:T(8,128)(2,1)S(1)}, u32[]{:S(2)}, u32[]{:S(2)}) %all-to-all-start) | async-done | bytes 2097184 | tf_op jit(solution)/shard_map/all_to_all | solution.py:242
  52.3 11.3 %all-to-all-start.1 = ((bf16[16,128,512]{2,1,0:T(8,128)(2,1)}), bf16[16,128,512]{2,1,0:T(8,128)(2,1)}, u32[]{:S(2)}, u32[]{:S(2)}) async-start(bf16[16,128,512]{2,1,0:T(8,128)(2,1)} %get-tuple-element.71), calls=%async_computation.1 | async-start | bytes 4194304 | tf_op jit(solution)/shard_map/all_to_all | solution.py:242
  63.6 1.8 fusion.1
  69.6 24.2 %collective-permute-done = bf16[288,2048]{1,0:T(8,128)(2,1)} collective-permute-done((bf16[288,2048]{1,0:T(8,128)(2,1)S(1)}, bf16[288,2048]{1,0:T(8,128)(2,1)}, u32[]{:S(2)}, u32[]{:S(2)}) %collective-permute-start) | collective-permute-done | bytes 1179680 | tf_op jit(solution)/shard_map/ppermute | solution.py:276
  93.8 2.9 multiply_reduce_fusion
  98.5 2.2 concatenate.15
  100.8 3.9 all-to-all-done.1.refs_3_
  104.7 11.3 %all-to-all-start.2 = ((bf16[16,128,512]{2,1,0:T(8,128)(2,1)}), bf16[16,128,512]{2,1,0:T(8,128)(2,1)}, u32[]{:S(2)}, u32[]{:S(2)}) async-start(bf16[16,128,512]{2,1,0:T(8,128)(2,1)} %get-tuple-element.77), calls=%async_computation.2 | async-start | bytes 4194304 | tf_op jit(solution)/shard_map/all_to_all | solution.py:242
  118.3 1.9 collective-permute-start.2
  121.8 43.2 %collective-permute-done.3.refs_4_ = bf16[16,128,512]{2,1,0:T(8,128)(2,1)S(1)} collective-permute-done((bf16[16,128,512]{2,1,0:T(8,128)(2,1)S(1)}, bf16[16,128,512]{2,1,0:T(8,128)(2,1)S(1)}, u32[]{:S(2)}, u32[]{:S(2)}) %collective-permute-start.3) | collective-permute-done | bytes 2097184 | tf_op jit(solution)/shard_map/ppermute | solution.py:246
  166.3 10.9 %collective-permute-start.4 = (bf16[288,2176]{1,0:T(8,128)(2,1)S(1)}, bf16[288,2176]{1,0:T(8,128)(2,1)}, u32[]{:S(2)}, u32[]{:S(2)}) collective-permute-start(bf16[288,2176]{1,0:T(8,128)(2,1)S(1)} %collective-permute-done.2.refs_0_), channel_id=1, source_target_pairs={{0,4},{1,3},{4,8},{5,1},{8,12},{9,5},{12,14},{13,9},{14,10},{15,13... | collective-permute-start | bytes 3760136 | tf_op jit(solution)/shard_map/ppermute | solution.py:309
  177.2 32.0 %collective-permute-done.5.refs_5_ = bf16[16,128,512]{2,1,0:T(8,128)(2,1)S(1)} collective-permute-done((bf16[16,128,512]{2,1,0:T(8,128)(2,1)}, bf16[16,128,512]{2,1,0:T(8,128)(2,1)S(1)}, u32[]{:S(2)}, u32[]{:S(2)}) %collective-permute-start.5) | collective-permute-done | bytes 2097184 | tf_op jit(solution)/shard_map/ppermute | solution.py:246
  210.5 2.1 collective-permute-start.6
  217.3 7.3 %expert_hidden.8 = (bf16[288,1024]{1,0:T(8,128)(2,1)S(1)}, bf16[288,1024]{1,0:T(8,128)(2,1)S(1)}) custom-call(s32[1]{0:T(128)} %bitcast.11.me_ref, bf16[288,2176]{1,0:T(8,128)(2,1)S(1)} %pad_maximum_fusion.refs_0_, bf16[288,2176]{1,0:T(8,128)(2,1)} %collective-permute-done.7.refs_1_, bf16[16,128,512]{2,1,0:T(8,128)(2,1)S(1)} %all-to-all-done.refs_2_, ...), custom_call_target="tpu_custom_call" | custom-call | flops 4831838208 | bytes 11927552 | tf_op jit(solution)/shard_map/expert_hidden/pallas_call | solution.py:133
  224.5 3.3 collective-permute-done.6.refs_0_
  227.9 1.9 collective-permute-start.8
  229.8 6.8 %expert_hidden.9 = (bf16[288,1024]{1,0:T(8,128)(2,1)S(1)}, bf16[288,1024]{1,0:T(8,128)(2,1)S(1)}) custom-call(s32[1]{0:T(128)} %bitcast.11.me_ref, bf16[288,2176]{1,0:T(8,128)(2,1)S(1)} %copy-done.8, bf16[288,2176]{1,0:T(8,128)(2,1)S(1)} %collective-permute-done.11.refs_1_, bf16[16,128,512]{2,1,0:T(8,128)(2,1)S(1)} %all-to-all-done.refs_2_, ...), custom_call_target="tpu_custom_call" | custom-call | flops 4831838208 | bytes 11927552 | tf_op jit(solution)/shard_map/expert_hidden/pallas_call | solution.py:133
  236.6 23.1 %collective-permute-done.9.refs_3_ = bf16[16,128,512]{2,1,0:T(8,128)(2,1)S(1)} collective-permute-done((bf16[16,128,512]{2,1,0:T(8,128)(2,1)}, bf16[16,128,512]{2,1,0:T(8,128)(2,1)S(1)}, u32[]{:S(2)}, u32[]{:S(2)}) %collective-permute-start.9) | collective-permute-done | bytes 2097184 | tf_op jit(solution)/shard_map/ppermute | solution.py:246
  260.5 4.6 %expert_down.15 = (bf16[288,2048]{1,0:T(8,128)(2,1)S(1)}, bf16[288,2048]{1,0:T(8,128)(2,1)S(1)}) custom-call(bf16[288,1024]{1,0:T(8,128)(2,1)S(1)} %get-tuple-element.127.refs_0_, bf16[288,1024]{1,0:T(8,128)(2,1)S(1)} %get-tuple-element.128.refs_1_, bf16[16,128,512]{2,1,0:T(8,128)(2,1)} %all-to-all-done.2.refs_2_, ...), custom_call_target="tpu_custom_call" | custom-call | flops 2415919104 | bytes 7733248 | tf_op jit(solution)/shard_map/expert_down/pallas_call | solution.py:172
  265.7 7.2 %expert_hidden.10 = (bf16[288,1024]{1,0:T(8,128)(2,1)S(1)}, bf16[288,1024]{1,0:T(8,128)(2,1)S(1)}) custom-call(s32[1]{0:T(128)} %bitcast.11.me_ref, bf16[288,2176]{1,0:T(8,128)(2,1)} %collective-permute-done.4.refs_0_, bf16[288,2176]{1,0:T(8,128)(2,1)S(1)} %collective-permute-done.13.refs_1_, bf16[16,128,512]{2,1,0:T(8,128)(2,1)S(1)} %all-to-all-done.refs_2_, ...), custom_call_target="tpu_custom_call" | custom-call | flops 4831838208 | bytes 11927552 | tf_op jit(solution)/shard_map/expert_hidden/pallas_call | solution.py:133
  272.9 4.2 %collective-permute-done.12.refs_0_ = bf16[288,2176]{1,0:T(8,128)(2,1)S(1)} collective-permute-done((bf16[288,2176]{1,0:T(8,128)(2,1)S(1)}, bf16[288,2176]{1,0:T(8,128)(2,1)S(1)}, u32[]{:S(2)}, u32[]{:S(2)}) %collective-permute-start.12) | collective-permute-done | bytes 1253408 | tf_op jit(solution)/shard_map/ppermute | solution.py:309
  279.4 4.2 %expert_down.14 = (bf16[288,2048]{1,0:T(8,128)(2,1)S(1)}, bf16[288,2048]{1,0:T(8,128)(2,1)S(1)}) custom-call(bf16[288,1024]{1,0:T(8,128)(2,1)S(1)} %get-tuple-element.123.refs_0_, bf16[288,1024]{1,0:T(8,128)(2,1)S(1)} %get-tuple-element.124.refs_1_, bf16[16,128,512]{2,1,0:T(8,128)(2,1)} %all-to-all-done.2.refs_2_, ...), custom_call_target="tpu_custom_call" | custom-call | flops 2415919104 | bytes 7733248 | tf_op jit(solution)/shard_map/expert_down/pallas_call | solution.py:172
  283.9 6.8 %expert_hidden.11 = (bf16[288,1024]{1,0:T(8,128)(2,1)S(1)}, bf16[288,1024]{1,0:T(8,128)(2,1)S(1)}) custom-call(s32[1]{0:T(128)} %bitcast.11.me_ref, bf16[288,2176]{1,0:T(8,128)(2,1)S(1)} %collective-permute-done.6.refs_0_, bf16[288,2176]{1,0:T(8,128)(2,1)S(1)} %collective-permute-done.15.refs_1_, bf16[16,128,512]{2,1,0:T(8,128)(2,1)S(1)} %all-to-all-done.refs_2_, ...), custom_call_target="tpu_custom_call" | custom-call | flops 4831838208 | bytes 11927552 | tf_op jit(solution)/shard_map/expert_hidden/pallas_call | solution.py:133
  290.7 3.4 collective-permute-done.14.refs_0_
  294.6 1.9 collective-permute-start.35
  296.5 3.9 collective-permute-done.28.refs_2_
  300.4 4.2 %expert_down.13 = (bf16[288,2048]{1,0:T(8,128)(2,1)S(1)}, bf16[288,2048]{1,0:T(8,128)(2,1)S(1)}) custom-call(bf16[288,1024]{1,0:T(8,128)(2,1)S(1)} %get-tuple-element.119.refs_0_, bf16[288,1024]{1,0:T(8,128)(2,1)S(1)} %get-tuple-element.120.refs_1_, bf16[16,128,512]{2,1,0:T(8,128)(2,1)} %all-to-all-done.2.refs_2_, ...), custom_call_target="tpu_custom_call" | custom-call | flops 2415919104 | bytes 7733248 | tf_op jit(solution)/shard_map/expert_down/pallas_call | solution.py:172
  305.9 14.3 %collective-permute-done.35.refs_2_ = bf16[288,1024]{1,0:T(8,128)(2,1)S(1)} collective-permute-done((bf16[288,1024]{1,0:T(8,128)(2,1)S(1)}, bf16[288,1024]{1,0:T(8,128)(2,1)S(1)}, u32[]{:S(2)}, u32[]{:S(2)}) %collective-permute-start.35) | collective-permute-done | bytes 589856 | tf_op jit(solution)/shard_map/ppermute | solution.py:341
  320.2 6.8 %expert_hidden.12 = (bf16[288,1024]{1,0:T(8,128)(2,1)S(1)}, bf16[288,1024]{1,0:T(8,128)(2,1)S(1)}) custom-call(s32[1]{0:T(128)} %bitcast.11.me_ref, bf16[288,2176]{1,0:T(8,128)(2,1)S(1)} %collective-permute-done.8.refs_0_, bf16[288,2176]{1,0:T(8,128)(2,1)S(1)} %collective-permute-done.17.refs_1_, bf16[16,128,512]{2,1,0:T(8,128)(2,1)S(1)} %all-to-all-done.refs_2_, ...), custom_call_target="tpu_custom_call" | custom-call | flops 4831838208 | bytes 11927552 | tf_op jit(solution)/shard_map/expert_hidden/pallas_call | solution.py:133
  327.2 4.2 %expert_down.12 = (bf16[288,2048]{1,0:T(8,128)(2,1)S(1)}, bf16[288,2048]{1,0:T(8,128)(2,1)S(1)}) custom-call(bf16[288,1024]{1,0:T(8,128)(2,1)S(1)} %get-tuple-element.115.refs_0_, bf16[288,1024]{1,0:T(8,128)(2,1)S(1)} %get-tuple-element.116.refs_1_, bf16[16,128,512]{2,1,0:T(8,128)(2,1)} %all-to-all-done.2.refs_2_, ...), custom_call_target="tpu_custom_call" | custom-call | flops 2415919104 | bytes 7733248 | tf_op jit(solution)/shard_map/expert_down/pallas_call | solution.py:172
  333.5 6.8 %expert_hidden.15 = (bf16[288,1024]{1,0:T(8,128)(2,1)S(1)}, bf16[288,1024]{1,0:T(8,128)(2,1)S(1)}) custom-call(s32[1]{0:T(128)} %bitcast.11.me_ref, bf16[288,2176]{1,0:T(8,128)(2,1)S(1)} %collective-permute-done.12.refs_0_, bf16[288,2176]{1,0:T(8,128)(2,1)S(1)} %collective-permute-done.22.refs_1_, bf16[16,128,512]{2,1,0:T(8,128)(2,1)S(1)} %all-to-all-done.refs_2_, ...), custom_call_target="tpu_custom_call" | custom-call | flops 4831838208 | bytes 11927552 | tf_op jit(solution)/shard_map/expert_hidden/pallas_call | solution.py:133
  341.3 4.2 %expert_down.11 = (bf16[288,2048]{1,0:T(8,128)(2,1)S(1)}, bf16[288,2048]{1,0:T(8,128)(2,1)S(1)}) custom-call(bf16[288,1024]{1,0:T(8,128)(2,1)S(1)} %get-tuple-element.111.refs_0_, bf16[288,1024]{1,0:T(8,128)(2,1)S(1)} %get-tuple-element.112.refs_1_, bf16[16,128,512]{2,1,0:T(8,128)(2,1)} %all-to-all-done.2.refs_2_, ...), custom_call_target="tpu_custom_call" | custom-call | flops 2415919104 | bytes 7733248 | tf_op jit(solution)/shard_map/expert_down/pallas_call | solution.py:172
  347.4 6.8 %expert_hidden.14 = (bf16[288,1024]{1,0:T(8,128)(2,1)S(1)}, bf16[288,1024]{1,0:T(8,128)(2,1)S(1)}) custom-call(s32[1]{0:T(128)} %bitcast.11.me_ref, bf16[288,2176]{1,0:T(8,128)(2,1)S(1)} %collective-permute-done.14.refs_0_, bf16[288,2176]{1,0:T(8,128)(2,1)S(1)} %collective-permute-done.20.refs_1_, bf16[16,128,512]{2,1,0:T(8,128)(2,1)S(1)} %all-to-all-done.refs_2_, ...), custom_call_target="tpu_custom_call" | custom-call | flops 4831838208 | bytes 11927552 | tf_op jit(solution)/shard_map/expert_hidden/pallas_call | solution.py:133
  356.2 4.2 %expert_down.10 = (bf16[288,2048]{1,0:T(8,128)(2,1)S(1)}, bf16[288,2048]{1,0:T(8,128)(2,1)S(1)}) custom-call(bf16[288,1024]{1,0:T(8,128)(2,1)S(1)} %get-tuple-element.107.refs_0_, bf16[288,1024]{1,0:T(8,128)(2,1)S(1)} %get-tuple-element.108.refs_1_, bf16[16,128,512]{2,1,0:T(8,128)(2,1)} %all-to-all-done.2.refs_2_, ...), custom_call_target="tpu_custom_call" | custom-call | flops 2415919104 | bytes 7733248 | tf_op jit(solution)/shard_map/expert_down/pallas_call | solution.py:172
  362.3 6.8 %expert_hidden.13 = (bf16[288,1024]{1,0:T(8,128)(2,1)S(1)}, bf16[288,1024]{1,0:T(8,128)(2,1)S(1)}) custom-call(s32[1]{0:T(128)} %bitcast.11.me_ref, bf16[288,2176]{1,0:T(8,128)(2,1)S(1)} %collective-permute-done.16.refs_0_, bf16[288,2176]{1,0:T(8,128)(2,1)S(1)} %collective-permute-done.18.refs_1_, bf16[16,128,512]{2,1,0:T(8,128)(2,1)S(1)} %all-to-all-done.refs_2_, ...), custom_call_target="tpu_custom_call" | custom-call | flops 4831838208 | bytes 11927552 | tf_op jit(solution)/shard_map/expert_hidden/pallas_call | solution.py:133
  370.1 4.2 %expert_down.9 = (bf16[288,2048]{1,0:T(8,128)(2,1)S(1)}, bf16[288,2048]{1,0:T(8,128)(2,1)S(1)}) custom-call(bf16[288,1024]{1,0:T(8,128)(2,1)S(1)} %get-tuple-element.103.refs_0_, bf16[288,1024]{1,0:T(8,128)(2,1)S(1)} %get-tuple-element.104.refs_1_, bf16[16,128,512]{2,1,0:T(8,128)(2,1)} %all-to-all-done.2.refs_2_, ...), custom_call_target="tpu_custom_call" | custom-call | flops 2415919104 | bytes 7733248 | tf_op jit(solution)/shard_map/expert_down/pallas_call | solution.py:172
  376.2 4.2 %expert_down.8 = (bf16[288,2048]{1,0:T(8,128)(2,1)S(1)}, bf16[288,2048]{1,0:T(8,128)(2,1)S(1)}) custom-call(bf16[288,1024]{1,0:T(8,128)(2,1)S(1)} %get-tuple-element.83.refs_0_, bf16[288,1024]{1,0:T(8,128)(2,1)S(1)} %get-tuple-element.84.refs_1_, bf16[16,128,512]{2,1,0:T(8,128)(2,1)} %all-to-all-done.2.refs_2_, ...), custom_call_target="tpu_custom_call" | custom-call | flops 2415919104 | bytes 7733248 | tf_op jit(solution)/shard_map/expert_down/pallas_call | solution.py:172
  381.3 4.3 %collective-permute-done.39.refs_2_ = bf16[288,1024]{1,0:T(8,128)(2,1)S(1)} collective-permute-done((bf16[288,1024]{1,0:T(8,128)(2,1)S(1)}, bf16[288,1024]{1,0:T(8,128)(2,1)S(1)}, u32[]{:S(2)}, u32[]{:S(2)}) %collective-permute-start.39) | collective-permute-done | bytes 589856 | tf_op jit(solution)/shard_map/ppermute | solution.py:341
  386.6 5.3 %collective-permute-done.33.refs_2_ = bf16[288,1024]{1,0:T(8,128)(2,1)S(1)} collective-permute-done((bf16[288,1024]{1,0:T(8,128)(2,1)S(1)}, bf16[288,1024]{1,0:T(8,128)(2,1)S(1)}, u32[]{:S(2)}, u32[]{:S(2)}) %collective-permute-start.33) | collective-permute-done | bytes 589856 | tf_op jit(solution)/shard_map/ppermute | solution.py:341
  392.9 5.3 %collective-permute-done.40.refs_2_ = bf16[288,1024]{1,0:T(8,128)(2,1)S(1)} collective-permute-done((bf16[288,1024]{1,0:T(8,128)(2,1)S(1)}, bf16[288,1024]{1,0:T(8,128)(2,1)S(1)}, u32[]{:S(2)}, u32[]{:S(2)}) %collective-permute-start.40) | collective-permute-done | bytes 589856 | tf_op jit(solution)/shard_map/ppermute | solution.py:341
  399.2 5.3 %collective-permute-done.34.refs_2_ = bf16[288,1024]{1,0:T(8,128)(2,1)S(1)} collective-permute-done((bf16[288,1024]{1,0:T(8,128)(2,1)S(1)}, bf16[288,1024]{1,0:T(8,128)(2,1)S(1)}, u32[]{:S(2)}, u32[]{:S(2)}) %collective-permute-start.34) | collective-permute-done | bytes 589856 | tf_op jit(solution)/shard_map/ppermute | solution.py:341
  404.7 6.1 %collective-permute-done.41.refs_2_ = bf16[288,1024]{1,0:T(8,128)(2,1)S(1)} collective-permute-done((bf16[288,1024]{1,0:T(8,128)(2,1)S(1)}, bf16[288,1024]{1,0:T(8,128)(2,1)S(1)}, u32[]{:S(2)}, u32[]{:S(2)}) %collective-permute-start.41) | collective-permute-done | bytes 589856 | tf_op jit(solution)/shard_map/ppermute | solution.py:341
  411.2 2.0 collective-permute-done.42
  413.2 3.2 fusion.2
  (127 shorter events, 39.1 us)
Async XLA Ops:
  3.8 48.5 %all-to-all-start = ((bf16[16,128,512]{2,1,0:T(8,128)(2,1)}), bf16[16,128,512]{2,1,0:T(8,128)(2,1)S(1)}, u32[]{:S(2)}, u32[]{:S(2)}) async-start(bf16[16,128,512]{2,1,0:T(8,128)(2,1)} %fusion), calls=%async_computation | async-start | bytes 4194304 | tf_op jit(solution)/shard_map/all_to_all | solution.py:242
  52.3 52.4 %all-to-all-start.1 = ((bf16[16,128,512]{2,1,0:T(8,128)(2,1)}), bf16[16,128,512]{2,1,0:T(8,128)(2,1)}, u32[]{:S(2)}, u32[]{:S(2)}) async-start(bf16[16,128,512]{2,1,0:T(8,128)(2,1)} %get-tuple-element.71), calls=%async_computation.1 | async-start | bytes 4194304 | tf_op jit(solution)/shard_map/all_to_all | solution.py:242
  65.4 28.4 %collective-permute-start = (bf16[288,2048]{1,0:T(8,128)(2,1)S(1)}, bf16[288,2048]{1,0:T(8,128)(2,1)}, u32[]{:S(2)}, u32[]{:S(2)}) collective-permute-start(bf16[288,2048]{1,0:T(8,128)(2,1)S(1)} %fusion.1), channel_id=1, source_target_pairs={{0,16},{16,0},{1,17},{17,1},{2,18},{18,2},{3,19},{19,3},{4,20},{20... | collective-permute-start | bytes 3538952 | tf_op jit(solution)/shard_map/ppermute | solution.py:276
  69.6 27.1 %copy-start.14 = (f32[2048]{0:T(1024)S(1)}, f32[2048]{0:T(1024)}, u32[]{:S(2)}) copy-start(f32[2048]{0:T(1024)} %param.16) | copy-start | bytes 24580
  104.7 105.8 %all-to-all-start.2 = ((bf16[16,128,512]{2,1,0:T(8,128)(2,1)}), bf16[16,128,512]{2,1,0:T(8,128)(2,1)}, u32[]{:S(2)}, u32[]{:S(2)}) async-start(bf16[16,128,512]{2,1,0:T(8,128)(2,1)} %get-tuple-element.77), calls=%async_computation.2 | async-start | bytes 4194304 | tf_op jit(solution)/shard_map/all_to_all | solution.py:242
  116.1 2.1 collective-permute-start.1
  116.5 48.5 %collective-permute-start.3 = (bf16[16,128,512]{2,1,0:T(8,128)(2,1)S(1)}, bf16[16,128,512]{2,1,0:T(8,128)(2,1)S(1)}, u32[]{:S(2)}, u32[]{:S(2)}) collective-permute-start(bf16[16,128,512]{2,1,0:T(8,128)(2,1)S(1)} %all-to-all-done.refs_2_), channel_id=1, source_target_pairs={{0,16},{16,0},{1,17},{17,1},{2,18},{18,2},{3,19},{19,3},{4,20},{20... | collective-permute-start | bytes 6291464 | tf_op jit(solution)/shard_map/ppermute | solution.py:246
  118.3 47.9 %collective-permute-start.2 = (bf16[288,2176]{1,0:T(8,128)(2,1)S(1)}, bf16[288,2176]{1,0:T(8,128)(2,1)S(1)}, u32[]{:S(2)}, u32[]{:S(2)}) collective-permute-start(bf16[288,2176]{1,0:T(8,128)(2,1)S(1)} %pad_maximum_fusion.refs_0_), channel_id=1, source_target_pairs={{0,4},{1,3},{4,8},{5,1},{8,12},{9,5},{12,14},{13,9},{14,10},{15,13... | collective-permute-start | bytes 3760136 | tf_op jit(solution)/shard_map/ppermute | solution.py:309
  120.2 88.9 %collective-permute-start.5 = (bf16[16,128,512]{2,1,0:T(8,128)(2,1)}, bf16[16,128,512]{2,1,0:T(8,128)(2,1)S(1)}, u32[]{:S(2)}, u32[]{:S(2)}) collective-permute-start(bf16[16,128,512]{2,1,0:T(8,128)(2,1)} %all-to-all-done.1.refs_3_), channel_id=1, source_target_pairs={{0,16},{16,0},{1,17},{17,1},{2,18},{18,2},{3,19},{19,3},{4,20},{20... | collective-permute-start | bytes 6291464 | tf_op jit(solution)/shard_map/ppermute | solution.py:246
  166.3 42.9 %copy-start.7 = (bf16[288,2176]{1,0:T(8,128)(2,1)}, bf16[288,2176]{1,0:T(8,128)(2,1)S(1)}, u32[]{:S(2)}) copy-start(bf16[288,2176]{1,0:T(8,128)(2,1)S(1)} %collective-permute-done.2.refs_0_) | copy-start | bytes 3760132
  166.3 44.2 %collective-permute-start.4 = (bf16[288,2176]{1,0:T(8,128)(2,1)S(1)}, bf16[288,2176]{1,0:T(8,128)(2,1)}, u32[]{:S(2)}, u32[]{:S(2)}) collective-permute-start(bf16[288,2176]{1,0:T(8,128)(2,1)S(1)} %collective-permute-done.2.refs_0_), channel_id=1, source_target_pairs={{0,4},{1,3},{4,8},{5,1},{8,12},{9,5},{12,14},{13,9},{14,10},{15,13... | collective-permute-start | bytes 3760136 | tf_op jit(solution)/shard_map/ppermute | solution.py:309
  177.2 36.9 %collective-permute-start.7 = (bf16[288,2176]{1,0:T(8,128)(2,1)S(1)}, bf16[288,2176]{1,0:T(8,128)(2,1)}, u32[]{:S(2)}, u32[]{:S(2)}) collective-permute-start(bf16[288,2176]{1,0:T(8,128)(2,1)S(1)} %pad_maximum_fusion.refs_0_), channel_id=1, source_target_pairs={{0,1},{1,0},{2,3},{3,2},{4,5},{5,4},{6,7},{7,6},{8,9},{9,8},{10,11... | collective-permute-start | bytes 3760136 | tf_op jit(solution)/shard_map/ppermute | solution.py:305
  210.5 17.4 %collective-permute-start.6 = (bf16[288,2176]{1,0:T(8,128)(2,1)}, bf16[288,2176]{1,0:T(8,128)(2,1)S(1)}, u32[]{:S(2)}, u32[]{:S(2)}) collective-permute-start(bf16[288,2176]{1,0:T(8,128)(2,1)} %collective-permute-done.4.refs_0_), channel_id=1, source_target_pairs={{0,4},{1,3},{4,8},{5,1},{8,12},{9,5},{12,14},{13,9},{14,10},{15,13... | collective-permute-start | bytes 3760136 | tf_op jit(solution)/shard_map/ppermute | solution.py:309
  212.6 47.1 %collective-permute-start.9 = (bf16[16,128,512]{2,1,0:T(8,128)(2,1)}, bf16[16,128,512]{2,1,0:T(8,128)(2,1)S(1)}, u32[]{:S(2)}, u32[]{:S(2)}) collective-permute-start(bf16[16,128,512]{2,1,0:T(8,128)(2,1)} %all-to-all-done.2.refs_2_), channel_id=1, source_target_pairs={{0,16},{16,0},{1,17},{17,1},{2,18},{18,2},{3,19},{19,3},{4,20},{20... | collective-permute-start | bytes 6291464 | tf_op jit(solution)/shard_map/ppermute | solution.py:246
  214.1 15.7 %collective-permute-start.11 = (bf16[288,2176]{1,0:T(8,128)(2,1)}, bf16[288,2176]{1,0:T(8,128)(2,1)S(1)}, u32[]{:S(2)}, u32[]{:S(2)}) collective-permute-start(bf16[288,2176]{1,0:T(8,128)(2,1)} %copy-done.7), channel_id=1, source_target_pairs={{0,1},{1,0},{2,3},{3,2},{4,5},{5,4},{6,7},{7,6},{8,9},{9,8},{10,11... | collective-permute-start | bytes 3760136 | tf_op jit(solution)/shard_map/ppermute | solution.py:305
  227.9 31.8 %collective-permute-start.8 = (bf16[288,2176]{1,0:T(8,128)(2,1)S(1)}, bf16[288,2176]{1,0:T(8,128)(2,1)S(1)}, u32[]{:S(2)}, u32[]{:S(2)}) collective-permute-start(bf16[288,2176]{1,0:T(8,128)(2,1)S(1)} %collective-permute-done.6.refs_0_), channel_id=1, source_target_pairs={{0,4},{1,3},{4,8},{5,1},{8,12},{9,5},{12,14},{13,9},{14,10},{15,13... | collective-permute-start | bytes 3760136 | tf_op jit(solution)/shard_map/ppermute | solution.py:309
  229.8 35.9 %collective-permute-start.13 = (bf16[288,2176]{1,0:T(8,128)(2,1)}, bf16[288,2176]{1,0:T(8,128)(2,1)S(1)}, u32[]{:S(2)}, u32[]{:S(2)}) collective-permute-start(bf16[288,2176]{1,0:T(8,128)(2,1)} %collective-permute-done.4.refs_0_), channel_id=1, source_target_pairs={{0,1},{1,0},{2,3},{3,2},{4,5},{5,4},{6,7},{7,6},{8,9},{9,8},{10,11... | collective-permute-start | bytes 3760136 | tf_op jit(solution)/shard_map/ppermute | solution.py:305
  259.7 17.4 %collective-permute-start.12 = (bf16[288,2176]{1,0:T(8,128)(2,1)S(1)}, bf16[288,2176]{1,0:T(8,128)(2,1)S(1)}, u32[]{:S(2)}, u32[]{:S(2)}) collective-permute-start(bf16[288,2176]{1,0:T(8,128)(2,1)S(1)} %collective-permute-done.8.refs_0_), channel_id=1, source_target_pairs={{0,4},{1,3},{4,8},{5,1},{8,12},{9,5},{12,14},{13,9},{14,10},{15,13... | collective-permute-start | bytes 3760136 | tf_op jit(solution)/shard_map/ppermute | solution.py:309
  265.1 12.4 %collective-permute-start.27 = (bf16[288,2048]{1,0:T(8,128)(2,1)S(1)}, bf16[288,2048]{1,0:T(8,128)(2,1)S(1)}, u32[]{:S(2)}, u32[]{:S(2)}) collective-permute-start(bf16[288,2048]{1,0:T(8,128)(2,1)S(1)} %get-tuple-element.130), channel_id=1, source_target_pairs={{0,1},{1,0},{2,3},{3,2},{4,5},{5,4},{6,7},{7,6},{8,9},{9,8},{10,11... | collective-permute-start | bytes 3538952 | tf_op jit(solution)/shard_map/ppermute | solution.py:332
  265.4 18.4 %collective-permute-start.15 = (bf16[288,2176]{1,0:T(8,128)(2,1)S(1)}, bf16[288,2176]{1,0:T(8,128)(2,1)S(1)}, u32[]{:S(2)}, u32[]{:S(2)}) collective-permute-start(bf16[288,2176]{1,0:T(8,128)(2,1)S(1)} %collective-permute-done.6.refs_0_), channel_id=1, source_target_pairs={{0,1},{1,0},{2,3},{3,2},{4,5},{5,4},{6,7},{7,6},{8,9},{9,8},{10,11... | collective-permute-start | bytes 3760136 | tf_op jit(solution)/shard_map/ppermute | solution.py:305
  277.1 17.0 %collective-permute-start.14 = (bf16[288,2176]{1,0:T(8,128)(2,1)S(1)}, bf16[288,2176]{1,0:T(8,128)(2,1)S(1)}, u32[]{:S(2)}, u32[]{:S(2)}) collective-permute-start(bf16[288,2176]{1,0:T(8,128)(2,1)S(1)} %collective-permute-done.12.refs_0_), channel_id=1, source_target_pairs={{0,4},{1,3},{4,8},{5,1},{8,12},{9,5},{12,14},{13,9},{14,10},{15,13... | collective-permute-start | bytes 3760136 | tf_op jit(solution)/shard_map/ppermute | solution.py:309
  277.5 28.0 %collective-permute-start.17 = (bf16[288,2176]{1,0:T(8,128)(2,1)S(1)}, bf16[288,2176]{1,0:T(8,128)(2,1)S(1)}, u32[]{:S(2)}, u32[]{:S(2)}) collective-permute-start(bf16[288,2176]{1,0:T(8,128)(2,1)S(1)} %collective-permute-done.8.refs_0_), channel_id=1, source_target_pairs={{0,1},{1,0},{2,3},{3,2},{4,5},{5,4},{6,7},{7,6},{8,9},{9,8},{10,11... | collective-permute-start | bytes 3760136 | tf_op jit(solution)/shard_map/ppermute | solution.py:305
  277.6 22.8 %collective-permute-start.28 = (bf16[288,1024]{1,0:T(8,128)(2,1)S(1)}, bf16[288,1024]{1,0:T(8,128)(2,1)S(1)}, u32[]{:S(2)}, u32[]{:S(2)}) collective-permute-start(bf16[288,1024]{1,0:T(8,128)(2,1)S(1)} %add_terms.16), channel_id=1, source_target_pairs={{0,4},{1,3},{4,8},{5,1},{8,12},{9,5},{12,14},{13,9},{14,10},{15,13... | collective-permute-start | bytes 1769480 | tf_op jit(solution)/shard_map/ppermute | solution.py:341
  283.6 21.1 %collective-permute-start.26 = (bf16[288,2048]{1,0:T(8,128)(2,1)S(1)}, bf16[288,2048]{1,0:T(8,128)(2,1)S(1)}, u32[]{:S(2)}, u32[]{:S(2)}) collective-permute-start(bf16[288,2048]{1,0:T(8,128)(2,1)S(1)} %get-tuple-element.126), channel_id=1, source_target_pairs={{0,1},{1,0},{2,3},{3,2},{4,5},{5,4},{6,7},{7,6},{8,9},{9,8},{10,11... | collective-permute-start | bytes 3538952 | tf_op jit(solution)/shard_map/ppermute | solution.py:332
  294.1 33.1 %collective-permute-start.16 = (bf16[288,2176]{1,0:T(8,128)(2,1)S(1)}, bf16[288,2176]{1,0:T(8,128)(2,1)S(1)}, u32[]{:S(2)}, u32[]{:S(2)}) collective-permute-start(bf16[288,2176]{1,0:T(8,128)(2,1)S(1)} %collective-permute-done.14.refs_0_), channel_id=1, source_target_pairs={{0,4},{1,3},{4,8},{5,1},{8,12},{9,5},{12,14},{13,9},{14,10},{15,13... | collective-permute-start | bytes 3760136 | tf_op jit(solution)/shard_map/ppermute | solution.py:309
  294.6 25.6 %collective-permute-start.35 = (bf16[288,1024]{1,0:T(8,128)(2,1)S(1)}, bf16[288,1024]{1,0:T(8,128)(2,1)S(1)}, u32[]{:S(2)}, u32[]{:S(2)}) collective-permute-start(bf16[288,1024]{1,0:T(8,128)(2,1)S(1)} %add_terms.24), channel_id=1, source_target_pairs={{0,4},{1,3},{4,8},{5,1},{8,12},{9,5},{12,14},{13,9},{14,10},{15,13... | collective-permute-start | bytes 1769480 | tf_op jit(solution)/shard_map/ppermute | solution.py:341
  300.4 31.6 %collective-permute-start.22 = (bf16[288,2176]{1,0:T(8,128)(2,1)S(1)}, bf16[288,2176]{1,0:T(8,128)(2,1)S(1)}, u32[]{:S(2)}, u32[]{:S(2)}) collective-permute-start(bf16[288,2176]{1,0:T(8,128)(2,1)S(1)} %collective-permute-done.12.refs_0_), channel_id=1, source_target_pairs={{0,1},{1,0},{2,3},{3,2},{4,5},{5,4},{6,7},{7,6},{8,9},{9,8},{10,11... | collective-permute-start | bytes 3760136 | tf_op jit(solution)/shard_map/ppermute | solution.py:305
  304.7 35.6 %collective-permute-start.25 = (bf16[288,2048]{1,0:T(8,128)(2,1)S(1)}, bf16[288,2048]{1,0:T(8,128)(2,1)S(1)}, u32[]{:S(2)}, u32[]{:S(2)}) collective-permute-start(bf16[288,2048]{1,0:T(8,128)(2,1)S(1)} %get-tuple-element.122), channel_id=1, source_target_pairs={{0,1},{1,0},{2,3},{3,2},{4,5},{5,4},{6,7},{7,6},{8,9},{9,8},{10,11... | collective-permute-start | bytes 3538952 | tf_op jit(solution)/shard_map/ppermute | solution.py:332
  305.5 27.1 %collective-permute-start.29 = (bf16[288,1024]{1,0:T(8,128)(2,1)S(1)}, bf16[288,1024]{1,0:T(8,128)(2,1)S(1)}, u32[]{:S(2)}, u32[]{:S(2)}) collective-permute-start(bf16[288,1024]{1,0:T(8,128)(2,1)S(1)} %add_terms.17), channel_id=1, source_target_pairs={{0,4},{1,3},{4,8},{5,1},{8,12},{9,5},{12,14},{13,9},{14,10},{15,13... | collective-permute-start | bytes 1769480 | tf_op jit(solution)/shard_map/ppermute | solution.py:341
  320.2 26.1 %collective-permute-start.20 = (bf16[288,2176]{1,0:T(8,128)(2,1)S(1)}, bf16[288,2176]{1,0:T(8,128)(2,1)S(1)}, u32[]{:S(2)}, u32[]{:S(2)}) collective-permute-start(bf16[288,2176]{1,0:T(8,128)(2,1)S(1)} %collective-permute-done.14.refs_0_), channel_id=1, source_target_pairs={{0,1},{1,0},{2,3},{3,2},{4,5},{5,4},{6,7},{7,6},{8,9},{9,8},{10,11... | collective-permute-start | bytes 3760136 | tf_op jit(solution)/shard_map/ppermute | solution.py:305
  331.5 22.8 %collective-permute-start.24 = (bf16[288,2048]{1,0:T(8,128)(2,1)S(1)}, bf16[288,2048]{1,0:T(8,128)(2,1)S(1)}, u32[]{:S(2)}, u32[]{:S(2)}) collective-permute-start(bf16[288,2048]{1,0:T(8,128)(2,1)S(1)} %get-tuple-element.118), channel_id=1, source_target_pairs={{0,1},{1,0},{2,3},{3,2},{4,5},{5,4},{6,7},{7,6},{8,9},{9,8},{10,11... | collective-permute-start | bytes 3538952 | tf_op jit(solution)/shard_map/ppermute | solution.py:332
  332.0 13.5 %collective-permute-start.36 = (bf16[288,1024]{1,0:T(8,128)(2,1)S(1)}, bf16[288,1024]{1,0:T(8,128)(2,1)S(1)}, u32[]{:S(2)}, u32[]{:S(2)}) collective-permute-start(bf16[288,1024]{1,0:T(8,128)(2,1)S(1)} %add_terms.25), channel_id=1, source_target_pairs={{0,4},{1,3},{4,8},{5,1},{8,12},{9,5},{12,14},{13,9},{14,10},{15,13... | collective-permute-start | bytes 1769480 | tf_op jit(solution)/shard_map/ppermute | solution.py:341
  332.6 29.7 %collective-permute-start.18 = (bf16[288,2176]{1,0:T(8,128)(2,1)S(1)}, bf16[288,2176]{1,0:T(8,128)(2,1)S(1)}, u32[]{:S(2)}, u32[]{:S(2)}) collective-permute-start(bf16[288,2176]{1,0:T(8,128)(2,1)S(1)} %collective-permute-done.16.refs_0_), channel_id=1, source_target_pairs={{0,1},{1,0},{2,3},{3,2},{4,5},{5,4},{6,7},{7,6},{8,9},{9,8},{10,11... | collective-permute-start | bytes 3760136 | tf_op jit(solution)/shard_map/ppermute | solution.py:305
  340.5 13.7 %collective-permute-start.30 = (bf16[288,1024]{1,0:T(8,128)(2,1)S(1)}, bf16[288,1024]{1,0:T(8,128)(2,1)S(1)}, u32[]{:S(2)}, u32[]{:S(2)}) collective-permute-start(bf16[288,1024]{1,0:T(8,128)(2,1)S(1)} %add_terms.18), channel_id=1, source_target_pairs={{0,4},{1,3},{4,8},{5,1},{8,12},{9,5},{12,14},{13,9},{14,10},{15,13... | collective-permute-start | bytes 1769480 | tf_op jit(solution)/shard_map/ppermute | solution.py:341
  345.6 23.5 %collective-permute-start.23 = (bf16[288,2048]{1,0:T(8,128)(2,1)S(1)}, bf16[288,2048]{1,0:T(8,128)(2,1)S(1)}, u32[]{:S(2)}, u32[]{:S(2)}) collective-permute-start(bf16[288,2048]{1,0:T(8,128)(2,1)S(1)} %get-tuple-element.114), channel_id=1, source_target_pairs={{0,1},{1,0},{2,3},{3,2},{4,5},{5,4},{6,7},{7,6},{8,9},{9,8},{10,11... | collective-permute-start | bytes 3538952 | tf_op jit(solution)/shard_map/ppermute | solution.py:332
  346.3 14.2 %collective-permute-start.37 = (bf16[288,1024]{1,0:T(8,128)(2,1)S(1)}, bf16[288,1024]{1,0:T(8,128)(2,1)S(1)}, u32[]{:S(2)}, u32[]{:S(2)}) collective-permute-start(bf16[288,1024]{1,0:T(8,128)(2,1)S(1)} %add_terms.26), channel_id=1, source_target_pairs={{0,4},{1,3},{4,8},{5,1},{8,12},{9,5},{12,14},{13,9},{14,10},{15,13... | collective-permute-start | bytes 1769480 | tf_op jit(solution)/shard_map/ppermute | solution.py:341
  354.4 14.6 %collective-permute-start.31 = (bf16[288,1024]{1,0:T(8,128)(2,1)S(1)}, bf16[288,1024]{1,0:T(8,128)(2,1)S(1)}, u32[]{:S(2)}, u32[]{:S(2)}) collective-permute-start(bf16[288,1024]{1,0:T(8,128)(2,1)S(1)} %add_terms.19), channel_id=1, source_target_pairs={{0,4},{1,3},{4,8},{5,1},{8,12},{9,5},{12,14},{13,9},{14,10},{15,13... | collective-permute-start | bytes 1769480 | tf_op jit(solution)/shard_map/ppermute | solution.py:341
  360.4 20.0 %collective-permute-start.21 = (bf16[288,2048]{1,0:T(8,128)(2,1)S(1)}, bf16[288,2048]{1,0:T(8,128)(2,1)S(1)}, u32[]{:S(2)}, u32[]{:S(2)}) collective-permute-start(bf16[288,2048]{1,0:T(8,128)(2,1)S(1)} %get-tuple-element.110), channel_id=1, source_target_pairs={{0,1},{1,0},{2,3},{3,2},{4,5},{5,4},{6,7},{7,6},{8,9},{9,8},{10,11... | collective-permute-start | bytes 3538952 | tf_op jit(solution)/shard_map/ppermute | solution.py:332
  360.7 13.7 %collective-permute-start.38 = (bf16[288,1024]{1,0:T(8,128)(2,1)S(1)}, bf16[288,1024]{1,0:T(8,128)(2,1)S(1)}, u32[]{:S(2)}, u32[]{:S(2)}) collective-permute-start(bf16[288,1024]{1,0:T(8,128)(2,1)S(1)} %add_terms.27), channel_id=1, source_target_pairs={{0,4},{1,3},{4,8},{5,1},{8,12},{9,5},{12,14},{13,9},{14,10},{15,13... | collective-permute-start | bytes 1769480 | tf_op jit(solution)/shard_map/ppermute | solution.py:341
  369.3 11.1 %collective-permute-start.32 = (bf16[288,1024]{1,0:T(8,128)(2,1)S(1)}, bf16[288,1024]{1,0:T(8,128)(2,1)S(1)}, u32[]{:S(2)}, u32[]{:S(2)}) collective-permute-start(bf16[288,1024]{1,0:T(8,128)(2,1)S(1)} %add_terms.20), channel_id=1, source_target_pairs={{0,4},{1,3},{4,8},{5,1},{8,12},{9,5},{12,14},{13,9},{14,10},{15,13... | collective-permute-start | bytes 1769480 | tf_op jit(solution)/shard_map/ppermute | solution.py:341
  374.3 12.2 %collective-permute-start.19 = (bf16[288,2048]{1,0:T(8,128)(2,1)S(1)}, bf16[288,2048]{1,0:T(8,128)(2,1)S(1)}, u32[]{:S(2)}, u32[]{:S(2)}) collective-permute-start(bf16[288,2048]{1,0:T(8,128)(2,1)S(1)} %get-tuple-element.106), channel_id=1, source_target_pairs={{0,1},{1,0},{2,3},{3,2},{4,5},{5,4},{6,7},{7,6},{8,9},{9,8},{10,11... | collective-permute-start | bytes 3538952 | tf_op jit(solution)/shard_map/ppermute | solution.py:332
  374.6 10.9 %collective-permute-start.39 = (bf16[288,1024]{1,0:T(8,128)(2,1)S(1)}, bf16[288,1024]{1,0:T(8,128)(2,1)S(1)}, u32[]{:S(2)}, u32[]{:S(2)}) collective-permute-start(bf16[288,1024]{1,0:T(8,128)(2,1)S(1)} %add_terms.28), channel_id=1, source_target_pairs={{0,4},{1,3},{4,8},{5,1},{8,12},{9,5},{12,14},{13,9},{14,10},{15,13... | collective-permute-start | bytes 1769480 | tf_op jit(solution)/shard_map/ppermute | solution.py:341
  380.6 11.2 %collective-permute-start.33 = (bf16[288,1024]{1,0:T(8,128)(2,1)S(1)}, bf16[288,1024]{1,0:T(8,128)(2,1)S(1)}, u32[]{:S(2)}, u32[]{:S(2)}) collective-permute-start(bf16[288,1024]{1,0:T(8,128)(2,1)S(1)} %add_terms.21), channel_id=1, source_target_pairs={{0,4},{1,3},{4,8},{5,1},{8,12},{9,5},{12,14},{13,9},{14,10},{15,13... | collective-permute-start | bytes 1769480 | tf_op jit(solution)/shard_map/ppermute | solution.py:341
  381.3 18.0 %collective-permute-start.10 = (bf16[288,2048]{1,0:T(8,128)(2,1)S(1)}, bf16[288,2048]{1,0:T(8,128)(2,1)S(1)}, u32[]{:S(2)}, u32[]{:S(2)}) collective-permute-start(bf16[288,2048]{1,0:T(8,128)(2,1)S(1)} %get-tuple-element.89), channel_id=1, source_target_pairs={{0,1},{1,0},{2,3},{3,2},{4,5},{5,4},{6,7},{7,6},{8,9},{9,8},{10,11... | collective-permute-start | bytes 3538952 | tf_op jit(solution)/shard_map/ppermute | solution.py:332
  385.8 12.4 %collective-permute-start.40 = (bf16[288,1024]{1,0:T(8,128)(2,1)S(1)}, bf16[288,1024]{1,0:T(8,128)(2,1)S(1)}, u32[]{:S(2)}, u32[]{:S(2)}) collective-permute-start(bf16[288,1024]{1,0:T(8,128)(2,1)S(1)} %add_terms.29), channel_id=1, source_target_pairs={{0,4},{1,3},{4,8},{5,1},{8,12},{9,5},{12,14},{13,9},{14,10},{15,13... | collective-permute-start | bytes 1769480 | tf_op jit(solution)/shard_map/ppermute | solution.py:341
  392.1 12.4 %collective-permute-start.34 = (bf16[288,1024]{1,0:T(8,128)(2,1)S(1)}, bf16[288,1024]{1,0:T(8,128)(2,1)S(1)}, u32[]{:S(2)}, u32[]{:S(2)}) collective-permute-start(bf16[288,1024]{1,0:T(8,128)(2,1)S(1)} %add_terms.22), channel_id=1, source_target_pairs={{0,4},{1,3},{4,8},{5,1},{8,12},{9,5},{12,14},{13,9},{14,10},{15,13... | collective-permute-start | bytes 1769480 | tf_op jit(solution)/shard_map/ppermute | solution.py:341
  398.4 12.4 %collective-permute-start.41 = (bf16[288,1024]{1,0:T(8,128)(2,1)S(1)}, bf16[288,1024]{1,0:T(8,128)(2,1)S(1)}, u32[]{:S(2)}, u32[]{:S(2)}) collective-permute-start(bf16[288,1024]{1,0:T(8,128)(2,1)S(1)} %add_terms.30), channel_id=1, source_target_pairs={{0,4},{1,3},{4,8},{5,1},{8,12},{9,5},{12,14},{13,9},{14,10},{15,13... | collective-permute-start | bytes 1769480 | tf_op jit(solution)/shard_map/ppermute | solution.py:341
  411.1 2.1 collective-permute-start.42
  (13 other events, 58.1 us)

commit v3 on v2

--- a/solution.py
+++ b/solution.py
@@ -87,7 +87,7 @@
         out_specs=pl.BlockSpec((count, width), lambda i: (0, 0)),
         out_shape=jax.ShapeDtypeStruct((count, width), jnp.float32),
         scratch_shapes=[pltpu.VMEM((count, width), jnp.bfloat16)],
-        compiler_params=pltpu.CompilerParams(vmem_limit_bytes=48 * 1024 * 1024),
+        compiler_params=pltpu.CompilerParams(vmem_limit_bytes=38 * 1024 * 1024),
         cost_estimate=pl.CostEstimate(
             flops=8 * count * width * units + 4 * PLEN * PLEN * units,
             bytes_accessed=8 * width * units + 6 * count * width,
@@ -135,7 +135,7 @@
         in_specs=[pl.BlockSpec(memory_space=pltpu.SMEM)] + [vmem] * (2 + len(weights)),
         out_specs=[vmem] * 2,
         out_shape=[out, out],
-        compiler_params=pltpu.CompilerParams(vmem_limit_bytes=16 * 1024 * 1024),
+        compiler_params=pltpu.CompilerParams(vmem_limit_bytes=8 * 1024 * 1024),
         cost_estimate=pl.CostEstimate(
             flops=8 * count * width * hidden,
             bytes_accessed=4 * count * (width + hidden) + 4 * width * hidden,
@@ -174,7 +174,7 @@
         in_specs=[vmem] * (2 + len(weights)),
         out_specs=[vmem] * 2,
         out_shape=[out, out],
-        compiler_params=pltpu.CompilerParams(vmem_limit_bytes=16 * 1024 * 1024),
+        compiler_params=pltpu.CompilerParams(vmem_limit_bytes=8 * 1024 * 1024),
         cost_estimate=pl.CostEstimate(
             flops=4 * count * width * hidden,
             bytes_accessed=4 * count * (width + hidden) + 2 * width * hidden,
@@ -200,7 +200,7 @@
         in_specs=[vmem] * len(terms),
         out_specs=vmem,
         out_shape=jax.ShapeDtypeStruct((keep.shape[0], columns), jnp.bfloat16),
-        compiler_params=pltpu.CompilerParams(vmem_limit_bytes=16 * 1024 * 1024),
+        compiler_params=pltpu.CompilerParams(vmem_limit_bytes=8 * 1024 * 1024),
         cost_estimate=pl.CostEstimate(
             flops=2 * keep.shape[0] * columns,
             bytes_accessed=8 * keep.shape[0] * columns,
@@ -275,11 +275,11 @@
         sent = rows_of(lax.rem(me_kv + turn, kv)).astype(jnp.bfloat16)
         sent = lax.ppermute(sent, "kv", [(i, (i + turn) % kv) for i in range(kv)])
         resid = resid + sent.astype(jnp.float32)
+    resid, up, down = lax.optimization_barrier((resid, up, down))
+    ups = over_kv(up)
+    down = over_experts(down)
     moe_in = rms_scale(resid, moe_gain).astype(jnp.bfloat16)
     moe_in = jnp.concatenate([moe_in, factor], axis=1)
-    moe_in, up, down = lax.optimization_barrier((moe_in, up, down))
-    ups = over_kv(up)
-    down = over_experts(down)
 
     cores = 2
     order = chip_ring(ex // cores)
@@ -298,7 +298,8 @@
     got = lax.ppermute(half_of(moe_in, 1 - core), "ex", swap)
     held = jnp.concatenate([half_of(moe_in, core), got], axis=0)
     first_weights = [gate, up]
-    due = {3: [0], 4: [1], 5: [2], 6: [3], 7: [4]}
+    due = {3: [0, 1], 4: [2, 3], 5: [4], 6: [5], 7: [6]}
+    held, gates = lax.optimization_barrier((held, gates))
     blocks, hiddens = [held], {}
 
     def hidden_of(step):
@@ -307,19 +308,17 @@
 
     for step in range(1, chips):
         held = lax.ppermute(held, "ex", ring)
-        if step == 1:
-            held, gates = lax.optimization_barrier((held, gates))
         if step == 2:
             held, ups, down = lax.optimization_barrier((held, ups, down))
             downs = over_kv(down)
             for pair in zip(gates, ups):
                 first_weights += pair
-        if step == min(4, chips - 1):
-            held, downs = lax.optimization_barrier((held, downs))
         blocks.append(held)
         for early in due.get(step, []):
             hiddens[early] = hidden_of(early)
             held, hiddens[early] = lax.optimization_barrier((held, hiddens[early]))
+        if step == min(4, chips - 1):
+            held, downs = lax.optimization_barrier((held, downs))
         blocks[step] = held
     for step in range(chips):
         if step not in hiddens:

time: 424 us -> 411 us (0.969)
  waiting for transfers between devices: 193 us -> 162 us
  starting transfers between devices: 73.5 us -> 80.3 us
  other arithmetic: 9.4 us -> 14.3 us
    ppermute x3, waiting for transfers between devices: 98.3 us -> 25.2 us  [over_kv(): lax.ppermute(part, 'kv', [(i, (i + turn) % kv) for i in range(kv)])]
    ppermute x7, waiting for transfers between devices: 11 us -> 43.5 us  [on_device(): held = lax.ppermute(held, 'ex', ring)]
    ppermute x14, waiting for transfers between devices: 44.5 us -> 52.6 us  [on_device(): running = lax.ppermute(running, 'ex', ring)]
    ppermute x7, starting transfers between devices: 18.3 us -> 25.6 us  [on_device(): held = lax.ppermute(held, 'ex', ring)]
    pallas_call x8, Pallas kernels: 55.1 us -> 60.8 us  [expert_hidden(): pl.pallas_call(functools.partial(hidden_kernel, experts, width), in_specs...]
    add x0 -> x1, other arithmetic: none -> 4.37 us  [on_device(): resid = resid + sent.astype(jnp.float32)]
  transfers between devices with their start and end apart: 46 -> 46, of which waited for: 18 -> 25; matrix products, arithmetic and copies ran while one was open for 4% -> 6% of each run, Pallas kernels for 28% -> 30%
where the time goes in v3:
time: 411 us; the launch traced here: 403 us
  waiting for transfers between devices  162 us (39%)
  Pallas kernels  122 us (30%)
  starting transfers between devices  80.3 us (20%)
  local copies, waits for them, and re-layouts  23.7 us (6%)
  other arithmetic  14.3 us (3%)
    pallas_call x8, Pallas kernels, expert_hidden(): pl.pallas_call(functools.partial(hidden_kernel, experts, width), in_specs...  60.8 us
    ppermute x14, waiting for transfers between devices, on_device(): running = lax.ppermute(running, 'ex', ring)  52.6 us
    ppermute x7, waiting for transfers between devices, on_device(): held = lax.ppermute(held, 'ex', ring)  43.5 us
    pallas_call x8, Pallas kernels, expert_down(): pl.pallas_call(down_kernel, in_specs=[vmem] * (2 + len(weights)), out_spe...  33.8 us
    all_to_all x3, starting transfers between devices, over_experts(): return lax.all_to_all(part, 'ex', split_axis=0, concat_axis=0, tiled=True)  29.9 us
    ppermute x7, starting transfers between devices, on_device(): held = lax.ppermute(held, 'ex', ring)  25.6 us
    ppermute x3, waiting for transfers between devices, over_kv(): lax.ppermute(part, 'kv', [(i, (i + turn) % kv) for i in range(kv)])  25.2 us
    ppermute x1, waiting for transfers between devices, on_device(): sent = lax.ppermute(sent, 'kv', [(i, (i + turn) % kv) for i in range(kv)])  24.2 us
  transfers between devices with their start and end apart: 46, of which 25 were waited for; matrix products, arithmetic and copies ran while one was open for 6% of the time, Pallas kernels for 30%

profile of v3, /device:TPU:0, one launch (start us, length us, event | category | flops | bytes accessed | tf_op | source)
XLA Modules:
  0.0 402.8 jit_solution(4100647281574705654)
XLA Ops:
  0.0 3.8 fusion
  3.8 7.4 %all-to-all-start = ((bf16[16,128,512]{2,1,0:T(8,128)(2,1)}), bf16[16,128,512]{2,1,0:T(8,128)(2,1)S(1)}, u32[]{:S(2)}, u32[]{:S(2)}) async-start(bf16[16,128,512]{2,1,0:T(8,128)(2,1)} %fusion), calls=%async_computation | async-start | bytes 4194304 | tf_op jit(solution)/shard_map/all_to_all | solution.py:242
  11.2 6.3 %slice_bitcast_fusion = (bf16[16,128,512]{2,1,0:T(8,128)(2,1)}, bf16[16,128,512]{2,1,0:T(8,128)(2,1)}) fusion(f32[16,3,128,512]{3,2,1,0:T(8,128)} %param.17), kind=kLoop, calls=%fused_computation.8 | loop fusion | bytes 8388608 | tf_op jit(solution)/shard_map/convert_element_type | solution.py:261
  19.8 23.9 %attention.1 = f32[576,2048]{1,0:T(8,128)S(1)} custom-call(s32[2]{0:T(128)S(1)} %copy-done.8, bf16[576,2048]{1,0:T(8,128)(2,1)S(1)} %bitcast.22, f32[1,2048]{1,0:T(1,128)S(1)} %bitcast.23, bf16[3,2048,1024]{2,1,0:T(8,128)(2,1)} %bitcast.25, bf16[2,2,512,1024]{3,2,1,0:T(8,128)(2,1)S(1)} %copy-done.2, bf16[1024,2048]{1,0:T(8,128)(2,1)S(1)} %copy-done.3), custom_call_target="tpu_custom_call" | custom-call | flops 10737418240 | bytes 23855104 | tf_op jit(solution)/shard_map/attention/pallas_call | solution.py:76
  45.7 6.6 %all-to-all-done.refs_2_ = bf16[16,128,512]{2,1,0:T(8,128)(2,1)S(1)} async-done(((bf16[16,128,512]{2,1,0:T(8,128)(2,1)}), bf16[16,128,512]{2,1,0:T(8,128)(2,1)S(1)}, u32[]{:S(2)}, u32[]{:S(2)}) %all-to-all-start) | async-done | bytes 2097184 | tf_op jit(solution)/shard_map/all_to_all | solution.py:242
  52.3 11.3 %all-to-all-start.1 = ((bf16[16,128,512]{2,1,0:T(8,128)(2,1)}), bf16[16,128,512]{2,1,0:T(8,128)(2,1)}, u32[]{:S(2)}, u32[]{:S(2)}) async-start(bf16[16,128,512]{2,1,0:T(8,128)(2,1)} %get-tuple-element.77), calls=%async_computation.1 | async-start | bytes 4194304 | tf_op jit(solution)/shard_map/all_to_all | solution.py:242
  70.2 24.2 %collective-permute-done = bf16[288,2048]{1,0:T(8,128)(2,1)} collective-permute-done((bf16[288,2048]{1,0:T(8,128)(2,1)S(1)}, bf16[288,2048]{1,0:T(8,128)(2,1)}, u32[]{:S(2)}, u32[]{:S(2)}) %collective-permute-start) | collective-permute-done | bytes 1179680 | tf_op jit(solution)/shard_map/ppermute | solution.py:276
  94.4 4.4 %bitcast_add_fusion = f32[288,2048]{1,0:T(8,128)} fusion(bf16[288,2048]{1,0:T(8,128)(2,1)} %collective-permute-done, f32[2,288,2048]{2,1,0:T(8,128)} %bitcast.21, s32[]{:T(128)S(6)} %select_n.29, bf16[1,576,2048]{2,1,0:T(8,128)(2,1)} %param.10, s32[]{:T(128)S(6)} %select_n.28), kind=kLoop, calls=%fused_computation.2 | loop fusion | flops 2359296 | bytes 7077896 | tf_op jit(solution)/shard_map/add | solution.py:277
  98.8 6.0 %all-to-all-done.1.refs_3_ = bf16[16,128,512]{2,1,0:T(8,128)(2,1)} async-done(((bf16[16,128,512]{2,1,0:T(8,128)(2,1)}), bf16[16,128,512]{2,1,0:T(8,128)(2,1)}, u32[]{:S(2)}, u32[]{:S(2)}) %all-to-all-start.1) | async-done | bytes 2097184 | tf_op jit(solution)/shard_map/all_to_all | solution.py:242
  106.6 11.3 %all-to-all-start.2 = ((bf16[16,128,512]{2,1,0:T(8,128)(2,1)}), bf16[16,128,512]{2,1,0:T(8,128)(2,1)}, u32[]{:S(2)}, u32[]{:S(2)}) async-start(bf16[16,128,512]{2,1,0:T(8,128)(2,1)} %get-tuple-element.83), calls=%async_computation.2 | async-start | bytes 4194304 | tf_op jit(solution)/shard_map/all_to_all | solution.py:242
  117.9 2.9 multiply_convert_fusion
  125.5 13.3 %collective-permute-done.2.refs_4_ = bf16[16,128,512]{2,1,0:T(8,128)(2,1)} collective-permute-done((bf16[16,128,512]{2,1,0:T(8,128)(2,1)S(1)}, bf16[16,128,512]{2,1,0:T(8,128)(2,1)}, u32[]{:S(2)}, u32[]{:S(2)}) %collective-permute-start.2) | collective-permute-done | bytes 2097184 | tf_op jit(solution)/shard_map/ppermute | solution.py:246
  142.0 24.3 %collective-permute-done.3.refs_0_ = bf16[288,2176]{1,0:T(8,128)(2,1)} collective-permute-done((bf16[288,2176]{1,0:T(8,128)(2,1)S(1)}, bf16[288,2176]{1,0:T(8,128)(2,1)}, u32[]{:S(2)}, u32[]{:S(2)}) %collective-permute-start.3) | collective-permute-done | bytes 1253408 | tf_op jit(solution)/shard_map/ppermute | solution.py:310
  166.2 12.9 %collective-permute-start.4 = (bf16[288,2176]{1,0:T(8,128)(2,1)}, bf16[288,2176]{1,0:T(8,128)(2,1)}, u32[]{:S(2)}, u32[]{:S(2)}) collective-permute-start(bf16[288,2176]{1,0:T(8,128)(2,1)} %collective-permute-done.3.refs_0_), channel_id=1, source_target_pairs={{0,4},{1,3},{4,8},{5,1},{8,12},{9,5},{12,14},{13,9},{14,10},{15,13... | collective-permute-start | bytes 3760136 | tf_op jit(solution)/shard_map/ppermute | solution.py:310
  179.6 7.6 %collective-permute-done.5.refs_5_ = bf16[16,128,512]{2,1,0:T(8,128)(2,1)S(1)} collective-permute-done((bf16[16,128,512]{2,1,0:T(8,128)(2,1)}, bf16[16,128,512]{2,1,0:T(8,128)(2,1)S(1)}, u32[]{:S(2)}, u32[]{:S(2)}) %collective-permute-start.5) | collective-permute-done | bytes 2097184 | tf_op jit(solution)/shard_map/ppermute | solution.py:246
  188.5 5.4 %collective-permute-done.4.refs_0_ = bf16[288,2176]{1,0:T(8,128)(2,1)} collective-permute-done((bf16[288,2176]{1,0:T(8,128)(2,1)}, bf16[288,2176]{1,0:T(8,128)(2,1)}, u32[]{:S(2)}, u32[]{:S(2)}) %collective-permute-start.4) | collective-permute-done | bytes 1253408 | tf_op jit(solution)/shard_map/ppermute | solution.py:310
  199.9 8.2 %expert_hidden.9 = (bf16[288,1024]{1,0:T(8,128)(2,1)S(1)}, bf16[288,1024]{1,0:T(8,128)(2,1)S(1)}) custom-call(s32[1]{0:T(128)} %bitcast.11.me_ref, bf16[288,2176]{1,0:T(8,128)(2,1)} %collective-permute-done.3.refs_0_, bf16[288,2176]{1,0:T(8,128)(2,1)} %collective-permute-done.8.refs_1_, bf16[16,128,512]{2,1,0:T(8,128)(2,1)S(1)} %all-to-all-done.refs_2_, ...), custom_call_target="tpu_custom_call" | custom-call | flops 4831838208 | bytes 11927552 | tf_op jit(solution)/shard_map/expert_hidden/pallas_call | solution.py:133
  208.1 7.8 %expert_hidden.8 = (bf16[288,1024]{1,0:T(8,128)(2,1)S(1)}, bf16[288,1024]{1,0:T(8,128)(2,1)S(1)}) custom-call(s32[1]{0:T(128)} %bitcast.11.me_ref, bf16[288,2176]{1,0:T(8,128)(2,1)S(1)} %pad_maximum_fusion.refs_0_, bf16[288,2176]{1,0:T(8,128)(2,1)} %collective-permute-done.7.refs_1_, bf16[16,128,512]{2,1,0:T(8,128)(2,1)S(1)} %all-to-all-done.refs_2_, ...), custom_call_target="tpu_custom_call" | custom-call | flops 4831838208 | bytes 11927552 | tf_op jit(solution)/shard_map/expert_hidden/pallas_call | solution.py:133
  215.9 2.8 collective-permute-start.9
  218.7 7.8 %expert_hidden.10 = (bf16[288,1024]{1,0:T(8,128)(2,1)S(1)}, bf16[288,1024]{1,0:T(8,128)(2,1)S(1)}) custom-call(s32[1]{0:T(128)} %bitcast.11.me_ref, bf16[288,2176]{1,0:T(8,128)(2,1)} %collective-permute-done.4.refs_0_, bf16[288,2176]{1,0:T(8,128)(2,1)S(1)} %collective-permute-done.10.refs_1_, bf16[16,128,512]{2,1,0:T(8,128)(2,1)S(1)} %all-to-all-done.refs_2_, ...), custom_call_target="tpu_custom_call" | custom-call | flops 4831838208 | bytes 11927552 | tf_op jit(solution)/shard_map/expert_hidden/pallas_call | solution.py:133
  226.5 6.7 %collective-permute-done.9.refs_0_ = bf16[288,2176]{1,0:T(8,128)(2,1)S(1)} collective-permute-done((bf16[288,2176]{1,0:T(8,128)(2,1)S(1)}, bf16[288,2176]{1,0:T(8,128)(2,1)S(1)}, u32[]{:S(2)}, u32[]{:S(2)}) %collective-permute-start.9) | collective-permute-done | bytes 1253408 | tf_op jit(solution)/shard_map/ppermute | solution.py:310
  233.2 7.4 %expert_hidden.11 = (bf16[288,1024]{1,0:T(8,128)(2,1)S(1)}, bf16[288,1024]{1,0:T(8,128)(2,1)S(1)}) custom-call(s32[1]{0:T(128)} %bitcast.11.me_ref, bf16[288,2176]{1,0:T(8,128)(2,1)S(1)} %collective-permute-done.6.refs_0_, bf16[288,2176]{1,0:T(8,128)(2,1)S(1)} %collective-permute-done.11.refs_1_, bf16[16,128,512]{2,1,0:T(8,128)(2,1)S(1)} %all-to-all-done.refs_2_, ...), custom_call_target="tpu_custom_call" | custom-call | flops 4831838208 | bytes 11927552 | tf_op jit(solution)/shard_map/expert_hidden/pallas_call | solution.py:133
  240.6 4.4 %collective-permute-done.12.refs_3_ = bf16[16,128,512]{2,1,0:T(8,128)(2,1)S(1)} collective-permute-done((bf16[16,128,512]{2,1,0:T(8,128)(2,1)}, bf16[16,128,512]{2,1,0:T(8,128)(2,1)S(1)}, u32[]{:S(2)}, u32[]{:S(2)}) %collective-permute-start.12) | collective-permute-done | bytes 2097184 | tf_op jit(solution)/shard_map/ppermute | solution.py:246
  245.0 2.9 collective-permute-start.14
  248.0 7.4 %expert_hidden.12 = (bf16[288,1024]{1,0:T(8,128)(2,1)S(1)}, bf16[288,1024]{1,0:T(8,128)(2,1)S(1)}) custom-call(s32[1]{0:T(128)} %bitcast.11.me_ref, bf16[288,2176]{1,0:T(8,128)(2,1)S(1)} %collective-permute-done.9.refs_0_, bf16[288,2176]{1,0:T(8,128)(2,1)S(1)} %collective-permute-done.15.refs_1_, bf16[16,128,512]{2,1,0:T(8,128)(2,1)S(1)} %all-to-all-done.refs_2_, ...), custom_call_target="tpu_custom_call" | custom-call | flops 4831838208 | bytes 11927552 | tf_op jit(solution)/shard_map/expert_hidden/pallas_call | solution.py:133
  255.4 7.1 %collective-permute-done.14.refs_0_ = bf16[288,2176]{1,0:T(8,128)(2,1)S(1)} collective-permute-done((bf16[288,2176]{1,0:T(8,128)(2,1)S(1)}, bf16[288,2176]{1,0:T(8,128)(2,1)S(1)}, u32[]{:S(2)}, u32[]{:S(2)}) %collective-permute-start.14) | collective-permute-done | bytes 1253408 | tf_op jit(solution)/shard_map/ppermute | solution.py:310
  262.6 4.2 %expert_down.15 = (bf16[288,2048]{1,0:T(8,128)(2,1)S(1)}, bf16[288,2048]{1,0:T(8,128)(2,1)S(1)}) custom-call(bf16[288,1024]{1,0:T(8,128)(2,1)S(1)} %get-tuple-element.139.refs_0_, bf16[288,1024]{1,0:T(8,128)(2,1)S(1)} %get-tuple-element.140.refs_1_, bf16[16,128,512]{2,1,0:T(8,128)(2,1)} %all-to-all-done.2.refs_2_, ...), custom_call_target="tpu_custom_call" | custom-call | flops 2415919104 | bytes 7733248 | tf_op jit(solution)/shard_map/expert_down/pallas_call | solution.py:172
  269.7 4.2 %expert_down.14 = (bf16[288,2048]{1,0:T(8,128)(2,1)S(1)}, bf16[288,2048]{1,0:T(8,128)(2,1)S(1)}) custom-call(bf16[288,1024]{1,0:T(8,128)(2,1)S(1)} %get-tuple-element.135.refs_0_, bf16[288,1024]{1,0:T(8,128)(2,1)S(1)} %get-tuple-element.136.refs_1_, bf16[16,128,512]{2,1,0:T(8,128)(2,1)} %all-to-all-done.2.refs_2_, ...), custom_call_target="tpu_custom_call" | custom-call | flops 2415919104 | bytes 7733248 | tf_op jit(solution)/shard_map/expert_down/pallas_call | solution.py:172
  274.0 4.2 %expert_down.13 = (bf16[288,2048]{1,0:T(8,128)(2,1)S(1)}, bf16[288,2048]{1,0:T(8,128)(2,1)S(1)}) custom-call(bf16[288,1024]{1,0:T(8,128)(2,1)S(1)} %get-tuple-element.131.refs_0_, bf16[288,1024]{1,0:T(8,128)(2,1)S(1)} %get-tuple-element.132.refs_1_, bf16[16,128,512]{2,1,0:T(8,128)(2,1)} %all-to-all-done.2.refs_2_, ...), custom_call_target="tpu_custom_call" | custom-call | flops 2415919104 | bytes 7733248 | tf_op jit(solution)/shard_map/expert_down/pallas_call | solution.py:172
  280.4 7.4 %expert_hidden.13 = (bf16[288,1024]{1,0:T(8,128)(2,1)S(1)}, bf16[288,1024]{1,0:T(8,128)(2,1)S(1)}) custom-call(s32[1]{0:T(128)} %bitcast.11.me_ref, bf16[288,2176]{1,0:T(8,128)(2,1)S(1)} %collective-permute-done.14.refs_0_, bf16[288,2176]{1,0:T(8,128)(2,1)S(1)} %collective-permute-done.17.refs_1_, bf16[16,128,512]{2,1,0:T(8,128)(2,1)S(1)} %all-to-all-done.refs_2_, ...), custom_call_target="tpu_custom_call" | custom-call | flops 4831838208 | bytes 11927552 | tf_op jit(solution)/shard_map/expert_hidden/pallas_call | solution.py:133
  293.4 4.2 %expert_down.12 = (bf16[288,2048]{1,0:T(8,128)(2,1)S(1)}, bf16[288,2048]{1,0:T(8,128)(2,1)S(1)}) custom-call(bf16[288,1024]{1,0:T(8,128)(2,1)S(1)} %get-tuple-element.127.refs_0_, bf16[288,1024]{1,0:T(8,128)(2,1)S(1)} %get-tuple-element.128.refs_1_, bf16[16,128,512]{2,1,0:T(8,128)(2,1)} %all-to-all-done.2.refs_2_, ...), custom_call_target="tpu_custom_call" | custom-call | flops 2415919104 | bytes 7733248 | tf_op jit(solution)/shard_map/expert_down/pallas_call | solution.py:172
  299.6 4.7 %collective-permute-done.29.refs_2_ = bf16[288,1024]{1,0:T(8,128)(2,1)S(1)} collective-permute-done((bf16[288,1024]{1,0:T(8,128)(2,1)S(1)}, bf16[288,1024]{1,0:T(8,128)(2,1)S(1)}, u32[]{:S(2)}, u32[]{:S(2)}) %collective-permute-start.29) | collective-permute-done | bytes 589856 | tf_op jit(solution)/shard_map/ppermute | solution.py:340
  306.0 4.2 %expert_down.11 = (bf16[288,2048]{1,0:T(8,128)(2,1)S(1)}, bf16[288,2048]{1,0:T(8,128)(2,1)S(1)}) custom-call(bf16[288,1024]{1,0:T(8,128)(2,1)S(1)} %get-tuple-element.123.refs_0_, bf16[288,1024]{1,0:T(8,128)(2,1)S(1)} %get-tuple-element.124.refs_1_, bf16[16,128,512]{2,1,0:T(8,128)(2,1)} %all-to-all-done.2.refs_2_, ...), custom_call_target="tpu_custom_call" | custom-call | flops 2415919104 | bytes 7733248 | tf_op jit(solution)/shard_map/expert_down/pallas_call | solution.py:172
  310.3 7.4 %expert_hidden.14 = (bf16[288,1024]{1,0:T(8,128)(2,1)S(1)}, bf16[288,1024]{1,0:T(8,128)(2,1)S(1)}) custom-call(s32[1]{0:T(128)} %bitcast.11.me_ref, bf16[288,2176]{1,0:T(8,128)(2,1)S(1)} %collective-permute-done.16.refs_0_, bf16[288,2176]{1,0:T(8,128)(2,1)S(1)} %collective-permute-done.19.refs_1_, bf16[16,128,512]{2,1,0:T(8,128)(2,1)S(1)} %all-to-all-done.refs_2_, ...), custom_call_target="tpu_custom_call" | custom-call | flops 4831838208 | bytes 11927552 | tf_op jit(solution)/shard_map/expert_hidden/pallas_call | solution.py:133
  318.3 5.8 %collective-permute-done.36.refs_2_ = bf16[288,1024]{1,0:T(8,128)(2,1)S(1)} collective-permute-done((bf16[288,1024]{1,0:T(8,128)(2,1)S(1)}, bf16[288,1024]{1,0:T(8,128)(2,1)S(1)}, u32[]{:S(2)}, u32[]{:S(2)}) %collective-permute-start.36) | collective-permute-done | bytes 589856 | tf_op jit(solution)/shard_map/ppermute | solution.py:340
  325.7 4.7 %collective-permute-done.30.refs_2_ = bf16[288,1024]{1,0:T(8,128)(2,1)S(1)} collective-permute-done((bf16[288,1024]{1,0:T(8,128)(2,1)S(1)}, bf16[288,1024]{1,0:T(8,128)(2,1)S(1)}, u32[]{:S(2)}, u32[]{:S(2)}) %collective-permute-start.30) | collective-permute-done | bytes 589856 | tf_op jit(solution)/shard_map/ppermute | solution.py:340
  332.0 4.7 %collective-permute-done.37.refs_2_ = bf16[288,1024]{1,0:T(8,128)(2,1)S(1)} collective-permute-done((bf16[288,1024]{1,0:T(8,128)(2,1)S(1)}, bf16[288,1024]{1,0:T(8,128)(2,1)S(1)}, u32[]{:S(2)}, u32[]{:S(2)}) %collective-permute-start.37) | collective-permute-done | bytes 589856 | tf_op jit(solution)/shard_map/ppermute | solution.py:340
  338.3 4.7 %collective-permute-done.31.refs_2_ = bf16[288,1024]{1,0:T(8,128)(2,1)S(1)} collective-permute-done((bf16[288,1024]{1,0:T(8,128)(2,1)S(1)}, bf16[288,1024]{1,0:T(8,128)(2,1)S(1)}, u32[]{:S(2)}, u32[]{:S(2)}) %collective-permute-start.31) | collective-permute-done | bytes 589856 | tf_op jit(solution)/shard_map/ppermute | solution.py:340
  344.9 4.2 %expert_down.10 = (bf16[288,2048]{1,0:T(8,128)(2,1)S(1)}, bf16[288,2048]{1,0:T(8,128)(2,1)S(1)}) custom-call(bf16[288,1024]{1,0:T(8,128)(2,1)S(1)} %get-tuple-element.119.refs_0_, bf16[288,1024]{1,0:T(8,128)(2,1)S(1)} %get-tuple-element.120.refs_1_, bf16[16,128,512]{2,1,0:T(8,128)(2,1)} %all-to-all-done.2.refs_2_, ...), custom_call_target="tpu_custom_call" | custom-call | flops 2415919104 | bytes 7733248 | tf_op jit(solution)/shard_map/expert_down/pallas_call | solution.py:172
  349.2 7.4 %expert_hidden.15 = (bf16[288,1024]{1,0:T(8,128)(2,1)S(1)}, bf16[288,1024]{1,0:T(8,128)(2,1)S(1)}) custom-call(s32[1]{0:T(128)} %bitcast.11.me_ref, bf16[288,2176]{1,0:T(8,128)(2,1)S(1)} %collective-permute-done.18.refs_0_, bf16[288,2176]{1,0:T(8,128)(2,1)S(1)} %collective-permute-done.20.refs_1_, bf16[16,128,512]{2,1,0:T(8,128)(2,1)S(1)} %all-to-all-done.refs_2_, ...), custom_call_target="tpu_custom_call" | custom-call | flops 4831838208 | bytes 11927552 | tf_op jit(solution)/shard_map/expert_hidden/pallas_call | solution.py:133
  356.6 4.2 %expert_down.9 = (bf16[288,2048]{1,0:T(8,128)(2,1)S(1)}, bf16[288,2048]{1,0:T(8,128)(2,1)S(1)}) custom-call(bf16[288,1024]{1,0:T(8,128)(2,1)S(1)} %get-tuple-element.115.refs_0_, bf16[288,1024]{1,0:T(8,128)(2,1)S(1)} %get-tuple-element.116.refs_1_, bf16[16,128,512]{2,1,0:T(8,128)(2,1)} %all-to-all-done.2.refs_2_, ...), custom_call_target="tpu_custom_call" | custom-call | flops 2415919104 | bytes 7733248 | tf_op jit(solution)/shard_map/expert_down/pallas_call | solution.py:172
  362.1 4.2 %expert_down.8 = (bf16[288,2048]{1,0:T(8,128)(2,1)S(1)}, bf16[288,2048]{1,0:T(8,128)(2,1)S(1)}) custom-call(bf16[288,1024]{1,0:T(8,128)(2,1)S(1)} %get-tuple-element.89.refs_0_, bf16[288,1024]{1,0:T(8,128)(2,1)S(1)} %get-tuple-element.90.refs_1_, bf16[16,128,512]{2,1,0:T(8,128)(2,1)} %all-to-all-done.2.refs_2_, ...), custom_call_target="tpu_custom_call" | custom-call | flops 2415919104 | bytes 7733248 | tf_op jit(solution)/shard_map/expert_down/pallas_call | solution.py:172
  368.5 3.0 collective-permute-done.39.refs_2_
  372.3 5.6 %collective-permute-done.33.refs_2_ = bf16[288,1024]{1,0:T(8,128)(2,1)S(1)} collective-permute-done((bf16[288,1024]{1,0:T(8,128)(2,1)S(1)}, bf16[288,1024]{1,0:T(8,128)(2,1)S(1)}, u32[]{:S(2)}, u32[]{:S(2)}) %collective-permute-start.33) | collective-permute-done | bytes 589856 | tf_op jit(solution)/shard_map/ppermute | solution.py:340
  378.7 5.5 %collective-permute-done.40.refs_2_ = bf16[288,1024]{1,0:T(8,128)(2,1)S(1)} collective-permute-done((bf16[288,1024]{1,0:T(8,128)(2,1)S(1)}, bf16[288,1024]{1,0:T(8,128)(2,1)S(1)}, u32[]{:S(2)}, u32[]{:S(2)}) %collective-permute-start.40) | collective-permute-done | bytes 589856 | tf_op jit(solution)/shard_map/ppermute | solution.py:340
  385.0 5.5 %collective-permute-done.34.refs_2_ = bf16[288,1024]{1,0:T(8,128)(2,1)S(1)} collective-permute-done((bf16[288,1024]{1,0:T(8,128)(2,1)S(1)}, bf16[288,1024]{1,0:T(8,128)(2,1)S(1)}, u32[]{:S(2)}, u32[]{:S(2)}) %collective-permute-start.34) | collective-permute-done | bytes 589856 | tf_op jit(solution)/shard_map/ppermute | solution.py:340
  390.7 6.1 %collective-permute-done.41.refs_2_ = bf16[288,1024]{1,0:T(8,128)(2,1)S(1)} collective-permute-done((bf16[288,1024]{1,0:T(8,128)(2,1)S(1)}, bf16[288,1024]{1,0:T(8,128)(2,1)S(1)}, u32[]{:S(2)}, u32[]{:S(2)}) %collective-permute-start.41) | collective-permute-done | bytes 589856 | tf_op jit(solution)/shard_map/ppermute | solution.py:340
  399.2 3.2 fusion.2
  (122 shorter events, 58.5 us)
Async XLA Ops:
  3.8 48.5 %all-to-all-start = ((bf16[16,128,512]{2,1,0:T(8,128)(2,1)}), bf16[16,128,512]{2,1,0:T(8,128)(2,1)S(1)}, u32[]{:S(2)}, u32[]{:S(2)}) async-start(bf16[16,128,512]{2,1,0:T(8,128)(2,1)} %fusion), calls=%async_computation | async-start | bytes 4194304 | tf_op jit(solution)/shard_map/all_to_all | solution.py:242
  11.2 6.4 %copy-start.1 = (bf16[1,576,2048]{2,1,0:T(8,128)(2,1)S(1)}, bf16[1,576,2048]{2,1,0:T(8,128)(2,1)}, u32[]{:S(2)}) copy-start(bf16[1,576,2048]{2,1,0:T(8,128)(2,1)} %param.10) | copy-start | bytes 7077892
  52.3 52.4 %all-to-all-start.1 = ((bf16[16,128,512]{2,1,0:T(8,128)(2,1)}), bf16[16,128,512]{2,1,0:T(8,128)(2,1)}, u32[]{:S(2)}, u32[]{:S(2)}) async-start(bf16[16,128,512]{2,1,0:T(8,128)(2,1)} %get-tuple-element.77), calls=%async_computation.1 | async-start | bytes 4194304 | tf_op jit(solution)/shard_map/all_to_all | solution.py:242
  65.4 29.0 %collective-permute-start = (bf16[288,2048]{1,0:T(8,128)(2,1)S(1)}, bf16[288,2048]{1,0:T(8,128)(2,1)}, u32[]{:S(2)}, u32[]{:S(2)}) collective-permute-start(bf16[288,2048]{1,0:T(8,128)(2,1)S(1)} %fusion.1), channel_id=1, source_target_pairs={{0,16},{16,0},{1,17},{17,1},{2,18},{18,2},{3,19},{19,3},{4,20},{20... | collective-permute-start | bytes 3538952 | tf_op jit(solution)/shard_map/ppermute | solution.py:276
  69.7 69.1 %collective-permute-start.2 = (bf16[16,128,512]{2,1,0:T(8,128)(2,1)S(1)}, bf16[16,128,512]{2,1,0:T(8,128)(2,1)}, u32[]{:S(2)}, u32[]{:S(2)}) collective-permute-start(bf16[16,128,512]{2,1,0:T(8,128)(2,1)S(1)} %all-to-all-done.refs_2_), channel_id=1, source_target_pairs={{0,16},{16,0},{1,17},{17,1},{2,18},{18,2},{3,19},{19,3},{4,20},{20... | collective-permute-start | bytes 6291464 | tf_op jit(solution)/shard_map/ppermute | solution.py:246
  106.6 11.3 %copy-start.11 = (f32[2048]{0:T(1024)S(1)}, f32[2048]{0:T(1024)}, u32[]{:S(2)}) copy-start(f32[2048]{0:T(1024)} %param.16) | copy-start | bytes 24580
  106.6 87.3 %all-to-all-start.2 = ((bf16[16,128,512]{2,1,0:T(8,128)(2,1)}), bf16[16,128,512]{2,1,0:T(8,128)(2,1)}, u32[]{:S(2)}, u32[]{:S(2)}) async-start(bf16[16,128,512]{2,1,0:T(8,128)(2,1)} %get-tuple-element.83), calls=%async_computation.2 | async-start | bytes 4194304 | tf_op jit(solution)/shard_map/all_to_all | solution.py:242
  123.3 2.1 collective-permute-start.1
  138.8 27.5 %collective-permute-start.3 = (bf16[288,2176]{1,0:T(8,128)(2,1)S(1)}, bf16[288,2176]{1,0:T(8,128)(2,1)}, u32[]{:S(2)}, u32[]{:S(2)}) collective-permute-start(bf16[288,2176]{1,0:T(8,128)(2,1)S(1)} %pad_maximum_fusion.refs_0_), channel_id=1, source_target_pairs={{0,4},{1,3},{4,8},{5,1},{8,12},{9,5},{12,14},{13,9},{14,10},{15,13... | collective-permute-start | bytes 3760136 | tf_op jit(solution)/shard_map/ppermute | solution.py:310
  140.4 46.8 %collective-permute-start.5 = (bf16[16,128,512]{2,1,0:T(8,128)(2,1)}, bf16[16,128,512]{2,1,0:T(8,128)(2,1)S(1)}, u32[]{:S(2)}, u32[]{:S(2)}) collective-permute-start(bf16[16,128,512]{2,1,0:T(8,128)(2,1)} %all-to-all-done.1.refs_3_), channel_id=1, source_target_pairs={{0,16},{16,0},{1,17},{17,1},{2,18},{18,2},{3,19},{19,3},{4,20},{20... | collective-permute-start | bytes 6291464 | tf_op jit(solution)/shard_map/ppermute | solution.py:246
  166.2 27.7 %collective-permute-start.4 = (bf16[288,2176]{1,0:T(8,128)(2,1)}, bf16[288,2176]{1,0:T(8,128)(2,1)}, u32[]{:S(2)}, u32[]{:S(2)}) collective-permute-start(bf16[288,2176]{1,0:T(8,128)(2,1)} %collective-permute-done.3.refs_0_), channel_id=1, source_target_pairs={{0,4},{1,3},{4,8},{5,1},{8,12},{9,5},{12,14},{13,9},{14,10},{15,13... | collective-permute-start | bytes 3760136 | tf_op jit(solution)/shard_map/ppermute | solution.py:310
  179.1 19.1 %collective-permute-start.8 = (bf16[288,2176]{1,0:T(8,128)(2,1)}, bf16[288,2176]{1,0:T(8,128)(2,1)}, u32[]{:S(2)}, u32[]{:S(2)}) collective-permute-start(bf16[288,2176]{1,0:T(8,128)(2,1)} %collective-permute-done.3.refs_0_), channel_id=1, source_target_pairs={{0,1},{1,0},{2,3},{3,2},{4,5},{5,4},{6,7},{7,6},{8,9},{9,8},{10,11... | collective-permute-start | bytes 3760136 | tf_op jit(solution)/shard_map/ppermute | solution.py:306
  179.1 28.9 %collective-permute-start.7 = (bf16[288,2176]{1,0:T(8,128)(2,1)S(1)}, bf16[288,2176]{1,0:T(8,128)(2,1)}, u32[]{:S(2)}, u32[]{:S(2)}) collective-permute-start(bf16[288,2176]{1,0:T(8,128)(2,1)S(1)} %pad_maximum_fusion.refs_0_), channel_id=1, source_target_pairs={{0,1},{1,0},{2,3},{3,2},{4,5},{5,4},{6,7},{7,6},{8,9},{9,8},{10,11... | collective-permute-start | bytes 3760136 | tf_op jit(solution)/shard_map/ppermute | solution.py:306
  194.0 21.9 %collective-permute-start.6 = (bf16[288,2176]{1,0:T(8,128)(2,1)}, bf16[288,2176]{1,0:T(8,128)(2,1)S(1)}, u32[]{:S(2)}, u32[]{:S(2)}) collective-permute-start(bf16[288,2176]{1,0:T(8,128)(2,1)} %collective-permute-done.4.refs_0_), channel_id=1, source_target_pairs={{0,4},{1,3},{4,8},{5,1},{8,12},{9,5},{12,14},{13,9},{14,10},{15,13... | collective-permute-start | bytes 3760136 | tf_op jit(solution)/shard_map/ppermute | solution.py:310
  196.7 21.9 %collective-permute-start.10 = (bf16[288,2176]{1,0:T(8,128)(2,1)}, bf16[288,2176]{1,0:T(8,128)(2,1)S(1)}, u32[]{:S(2)}, u32[]{:S(2)}) collective-permute-start(bf16[288,2176]{1,0:T(8,128)(2,1)} %collective-permute-done.4.refs_0_), channel_id=1, source_target_pairs={{0,1},{1,0},{2,3},{3,2},{4,5},{5,4},{6,7},{7,6},{8,9},{9,8},{10,11... | collective-permute-start | bytes 3760136 | tf_op jit(solution)/shard_map/ppermute | solution.py:306
  196.7 48.3 %collective-permute-start.12 = (bf16[16,128,512]{2,1,0:T(8,128)(2,1)}, bf16[16,128,512]{2,1,0:T(8,128)(2,1)S(1)}, u32[]{:S(2)}, u32[]{:S(2)}) collective-permute-start(bf16[16,128,512]{2,1,0:T(8,128)(2,1)} %all-to-all-done.2.refs_2_), channel_id=1, source_target_pairs={{0,16},{16,0},{1,17},{17,1},{2,18},{18,2},{3,19},{19,3},{4,20},{20... | collective-permute-start | bytes 6291464 | tf_op jit(solution)/shard_map/ppermute | solution.py:246
  215.9 17.3 %collective-permute-start.9 = (bf16[288,2176]{1,0:T(8,128)(2,1)S(1)}, bf16[288,2176]{1,0:T(8,128)(2,1)S(1)}, u32[]{:S(2)}, u32[]{:S(2)}) collective-permute-start(bf16[288,2176]{1,0:T(8,128)(2,1)S(1)} %collective-permute-done.6.refs_0_), channel_id=1, source_target_pairs={{0,4},{1,3},{4,8},{5,1},{8,12},{9,5},{12,14},{13,9},{14,10},{15,13... | collective-permute-start | bytes 3760136 | tf_op jit(solution)/shard_map/ppermute | solution.py:310
  218.7 14.5 %collective-permute-start.11 = (bf16[288,2176]{1,0:T(8,128)(2,1)S(1)}, bf16[288,2176]{1,0:T(8,128)(2,1)S(1)}, u32[]{:S(2)}, u32[]{:S(2)}) collective-permute-start(bf16[288,2176]{1,0:T(8,128)(2,1)S(1)} %collective-permute-done.6.refs_0_), channel_id=1, source_target_pairs={{0,1},{1,0},{2,3},{3,2},{4,5},{5,4},{6,7},{7,6},{8,9},{9,8},{10,11... | collective-permute-start | bytes 3760136 | tf_op jit(solution)/shard_map/ppermute | solution.py:306
  245.0 3.0 collective-permute-start.15
  245.0 17.4 %collective-permute-start.14 = (bf16[288,2176]{1,0:T(8,128)(2,1)S(1)}, bf16[288,2176]{1,0:T(8,128)(2,1)S(1)}, u32[]{:S(2)}, u32[]{:S(2)}) collective-permute-start(bf16[288,2176]{1,0:T(8,128)(2,1)S(1)} %collective-permute-done.9.refs_0_), channel_id=1, source_target_pairs={{0,4},{1,3},{4,8},{5,1},{8,12},{9,5},{12,14},{13,9},{14,10},{15,13... | collective-permute-start | bytes 3760136 | tf_op jit(solution)/shard_map/ppermute | solution.py:310
  262.4 16.9 %collective-permute-start.17 = (bf16[288,2176]{1,0:T(8,128)(2,1)S(1)}, bf16[288,2176]{1,0:T(8,128)(2,1)S(1)}, u32[]{:S(2)}, u32[]{:S(2)}) collective-permute-start(bf16[288,2176]{1,0:T(8,128)(2,1)S(1)} %collective-permute-done.14.refs_0_), channel_id=1, source_target_pairs={{0,1},{1,0},{2,3},{3,2},{4,5},{5,4},{6,7},{7,6},{8,9},{9,8},{10,11... | collective-permute-start | bytes 3760136 | tf_op jit(solution)/shard_map/ppermute | solution.py:306
  266.8 12.0 %collective-permute-start.27 = (bf16[288,2048]{1,0:T(8,128)(2,1)S(1)}, bf16[288,2048]{1,0:T(8,128)(2,1)S(1)}, u32[]{:S(2)}, u32[]{:S(2)}) collective-permute-start(bf16[288,2048]{1,0:T(8,128)(2,1)S(1)} %get-tuple-element.142), channel_id=1, source_target_pairs={{0,1},{1,0},{2,3},{3,2},{4,5},{5,4},{6,7},{7,6},{8,9},{9,8},{10,11... | collective-permute-start | bytes 3538952 | tf_op jit(solution)/shard_map/ppermute | solution.py:331
  267.2 20.6 %collective-permute-start.16 = (bf16[288,2176]{1,0:T(8,128)(2,1)S(1)}, bf16[288,2176]{1,0:T(8,128)(2,1)S(1)}, u32[]{:S(2)}, u32[]{:S(2)}) collective-permute-start(bf16[288,2176]{1,0:T(8,128)(2,1)S(1)} %collective-permute-done.14.refs_0_), channel_id=1, source_target_pairs={{0,4},{1,3},{4,8},{5,1},{8,12},{9,5},{12,14},{13,9},{14,10},{15,13... | collective-permute-start | bytes 3760136 | tf_op jit(solution)/shard_map/ppermute | solution.py:310
  274.0 14.7 %collective-permute-start.26 = (bf16[288,2048]{1,0:T(8,128)(2,1)S(1)}, bf16[288,2048]{1,0:T(8,128)(2,1)S(1)}, u32[]{:S(2)}, u32[]{:S(2)}) collective-permute-start(bf16[288,2048]{1,0:T(8,128)(2,1)S(1)} %get-tuple-element.138), channel_id=1, source_target_pairs={{0,1},{1,0},{2,3},{3,2},{4,5},{5,4},{6,7},{7,6},{8,9},{9,8},{10,11... | collective-permute-start | bytes 3538952 | tf_op jit(solution)/shard_map/ppermute | solution.py:331
  278.3 20.0 %collective-permute-start.25 = (bf16[288,2048]{1,0:T(8,128)(2,1)S(1)}, bf16[288,2048]{1,0:T(8,128)(2,1)S(1)}, u32[]{:S(2)}, u32[]{:S(2)}) collective-permute-start(bf16[288,2048]{1,0:T(8,128)(2,1)S(1)} %get-tuple-element.134), channel_id=1, source_target_pairs={{0,1},{1,0},{2,3},{3,2},{4,5},{5,4},{6,7},{7,6},{8,9},{9,8},{10,11... | collective-permute-start | bytes 3538952 | tf_op jit(solution)/shard_map/ppermute | solution.py:331
  279.0 11.6 %collective-permute-start.28 = (bf16[288,1024]{1,0:T(8,128)(2,1)S(1)}, bf16[288,1024]{1,0:T(8,128)(2,1)S(1)}, u32[]{:S(2)}, u32[]{:S(2)}) collective-permute-start(bf16[288,1024]{1,0:T(8,128)(2,1)S(1)} %add_terms.16), channel_id=1, source_target_pairs={{0,4},{1,3},{4,8},{5,1},{8,12},{9,5},{12,14},{13,9},{14,10},{15,13... | collective-permute-start | bytes 1769480 | tf_op jit(solution)/shard_map/ppermute | solution.py:340
  287.8 22.3 %collective-permute-start.19 = (bf16[288,2176]{1,0:T(8,128)(2,1)S(1)}, bf16[288,2176]{1,0:T(8,128)(2,1)S(1)}, u32[]{:S(2)}, u32[]{:S(2)}) collective-permute-start(bf16[288,2176]{1,0:T(8,128)(2,1)S(1)} %collective-permute-done.16.refs_0_), channel_id=1, source_target_pairs={{0,1},{1,0},{2,3},{3,2},{4,5},{5,4},{6,7},{7,6},{8,9},{9,8},{10,11... | collective-permute-start | bytes 3760136 | tf_op jit(solution)/shard_map/ppermute | solution.py:306
  288.1 9.9 %collective-permute-start.35 = (bf16[288,1024]{1,0:T(8,128)(2,1)S(1)}, bf16[288,1024]{1,0:T(8,128)(2,1)S(1)}, u32[]{:S(2)}, u32[]{:S(2)}) collective-permute-start(bf16[288,1024]{1,0:T(8,128)(2,1)S(1)} %add_terms.24), channel_id=1, source_target_pairs={{0,4},{1,3},{4,8},{5,1},{8,12},{9,5},{12,14},{13,9},{14,10},{15,13... | collective-permute-start | bytes 1769480 | tf_op jit(solution)/shard_map/ppermute | solution.py:340
  290.8 13.6 %collective-permute-start.29 = (bf16[288,1024]{1,0:T(8,128)(2,1)S(1)}, bf16[288,1024]{1,0:T(8,128)(2,1)S(1)}, u32[]{:S(2)}, u32[]{:S(2)}) collective-permute-start(bf16[288,1024]{1,0:T(8,128)(2,1)S(1)} %add_terms.17), channel_id=1, source_target_pairs={{0,4},{1,3},{4,8},{5,1},{8,12},{9,5},{12,14},{13,9},{14,10},{15,13... | collective-permute-start | bytes 1769480 | tf_op jit(solution)/shard_map/ppermute | solution.py:340
  293.3 24.4 %collective-permute-start.18 = (bf16[288,2176]{1,0:T(8,128)(2,1)S(1)}, bf16[288,2176]{1,0:T(8,128)(2,1)S(1)}, u32[]{:S(2)}, u32[]{:S(2)}) collective-permute-start(bf16[288,2176]{1,0:T(8,128)(2,1)S(1)} %collective-permute-done.16.refs_0_), channel_id=1, source_target_pairs={{0,4},{1,3},{4,8},{5,1},{8,12},{9,5},{12,14},{13,9},{14,10},{15,13... | collective-permute-start | bytes 3760136 | tf_op jit(solution)/shard_map/ppermute | solution.py:310
  298.0 27.7 %collective-permute-start.24 = (bf16[288,2048]{1,0:T(8,128)(2,1)S(1)}, bf16[288,2048]{1,0:T(8,128)(2,1)S(1)}, u32[]{:S(2)}, u32[]{:S(2)}) collective-permute-start(bf16[288,2048]{1,0:T(8,128)(2,1)S(1)} %get-tuple-element.130), channel_id=1, source_target_pairs={{0,1},{1,0},{2,3},{3,2},{4,5},{5,4},{6,7},{7,6},{8,9},{9,8},{10,11... | collective-permute-start | bytes 3538952 | tf_op jit(solution)/shard_map/ppermute | solution.py:331
  298.2 25.8 %collective-permute-start.36 = (bf16[288,1024]{1,0:T(8,128)(2,1)S(1)}, bf16[288,1024]{1,0:T(8,128)(2,1)S(1)}, u32[]{:S(2)}, u32[]{:S(2)}) collective-permute-start(bf16[288,1024]{1,0:T(8,128)(2,1)S(1)} %add_terms.25), channel_id=1, source_target_pairs={{0,4},{1,3},{4,8},{5,1},{8,12},{9,5},{12,14},{13,9},{14,10},{15,13... | collective-permute-start | bytes 1769480 | tf_op jit(solution)/shard_map/ppermute | solution.py:340
  304.5 25.9 %collective-permute-start.30 = (bf16[288,1024]{1,0:T(8,128)(2,1)S(1)}, bf16[288,1024]{1,0:T(8,128)(2,1)S(1)}, u32[]{:S(2)}, u32[]{:S(2)}) collective-permute-start(bf16[288,1024]{1,0:T(8,128)(2,1)S(1)} %add_terms.18), channel_id=1, source_target_pairs={{0,4},{1,3},{4,8},{5,1},{8,12},{9,5},{12,14},{13,9},{14,10},{15,13... | collective-permute-start | bytes 1769480 | tf_op jit(solution)/shard_map/ppermute | solution.py:340
  310.2 32.8 %collective-permute-start.23 = (bf16[288,2048]{1,0:T(8,128)(2,1)S(1)}, bf16[288,2048]{1,0:T(8,128)(2,1)S(1)}, u32[]{:S(2)}, u32[]{:S(2)}) collective-permute-start(bf16[288,2048]{1,0:T(8,128)(2,1)S(1)} %get-tuple-element.126), channel_id=1, source_target_pairs={{0,1},{1,0},{2,3},{3,2},{4,5},{5,4},{6,7},{7,6},{8,9},{9,8},{10,11... | collective-permute-start | bytes 3538952 | tf_op jit(solution)/shard_map/ppermute | solution.py:331
  317.8 31.4 %collective-permute-start.20 = (bf16[288,2176]{1,0:T(8,128)(2,1)S(1)}, bf16[288,2176]{1,0:T(8,128)(2,1)S(1)}, u32[]{:S(2)}, u32[]{:S(2)}) collective-permute-start(bf16[288,2176]{1,0:T(8,128)(2,1)S(1)} %collective-permute-done.18.refs_0_), channel_id=1, source_target_pairs={{0,1},{1,0},{2,3},{3,2},{4,5},{5,4},{6,7},{7,6},{8,9},{9,8},{10,11... | collective-permute-start | bytes 3760136 | tf_op jit(solution)/shard_map/ppermute | solution.py:306
  324.3 12.4 %collective-permute-start.37 = (bf16[288,1024]{1,0:T(8,128)(2,1)S(1)}, bf16[288,1024]{1,0:T(8,128)(2,1)S(1)}, u32[]{:S(2)}, u32[]{:S(2)}) collective-permute-start(bf16[288,1024]{1,0:T(8,128)(2,1)S(1)} %add_terms.26), channel_id=1, source_target_pairs={{0,4},{1,3},{4,8},{5,1},{8,12},{9,5},{12,14},{13,9},{14,10},{15,13... | collective-permute-start | bytes 1769480 | tf_op jit(solution)/shard_map/ppermute | solution.py:340
  330.6 12.4 %collective-permute-start.31 = (bf16[288,1024]{1,0:T(8,128)(2,1)S(1)}, bf16[288,1024]{1,0:T(8,128)(2,1)S(1)}, u32[]{:S(2)}, u32[]{:S(2)}) collective-permute-start(bf16[288,1024]{1,0:T(8,128)(2,1)S(1)} %add_terms.19), channel_id=1, source_target_pairs={{0,4},{1,3},{4,8},{5,1},{8,12},{9,5},{12,14},{13,9},{14,10},{15,13... | collective-permute-start | bytes 1769480 | tf_op jit(solution)/shard_map/ppermute | solution.py:340
  336.9 24.5 %collective-permute-start.38 = (bf16[288,1024]{1,0:T(8,128)(2,1)S(1)}, bf16[288,1024]{1,0:T(8,128)(2,1)S(1)}, u32[]{:S(2)}, u32[]{:S(2)}) collective-permute-start(bf16[288,1024]{1,0:T(8,128)(2,1)S(1)} %add_terms.27), channel_id=1, source_target_pairs={{0,4},{1,3},{4,8},{5,1},{8,12},{9,5},{12,14},{13,9},{14,10},{15,13... | collective-permute-start | bytes 1769480 | tf_op jit(solution)/shard_map/ppermute | solution.py:340
  343.3 23.1 %collective-permute-start.32 = (bf16[288,1024]{1,0:T(8,128)(2,1)S(1)}, bf16[288,1024]{1,0:T(8,128)(2,1)S(1)}, u32[]{:S(2)}, u32[]{:S(2)}) collective-permute-start(bf16[288,1024]{1,0:T(8,128)(2,1)S(1)} %add_terms.20), channel_id=1, source_target_pairs={{0,4},{1,3},{4,8},{5,1},{8,12},{9,5},{12,14},{13,9},{14,10},{15,13... | collective-permute-start | bytes 1769480 | tf_op jit(solution)/shard_map/ppermute | solution.py:340
  349.1 17.2 %collective-permute-start.22 = (bf16[288,2048]{1,0:T(8,128)(2,1)S(1)}, bf16[288,2048]{1,0:T(8,128)(2,1)S(1)}, u32[]{:S(2)}, u32[]{:S(2)}) collective-permute-start(bf16[288,2048]{1,0:T(8,128)(2,1)S(1)} %get-tuple-element.122), channel_id=1, source_target_pairs={{0,1},{1,0},{2,3},{3,2},{4,5},{5,4},{6,7},{7,6},{8,9},{9,8},{10,11... | collective-permute-start | bytes 3538952 | tf_op jit(solution)/shard_map/ppermute | solution.py:331
  360.9 17.0 %collective-permute-start.21 = (bf16[288,2048]{1,0:T(8,128)(2,1)S(1)}, bf16[288,2048]{1,0:T(8,128)(2,1)S(1)}, u32[]{:S(2)}, u32[]{:S(2)}) collective-permute-start(bf16[288,2048]{1,0:T(8,128)(2,1)S(1)} %get-tuple-element.118), channel_id=1, source_target_pairs={{0,1},{1,0},{2,3},{3,2},{4,5},{5,4},{6,7},{7,6},{8,9},{9,8},{10,11... | collective-permute-start | bytes 3538952 | tf_op jit(solution)/shard_map/ppermute | solution.py:331
  361.6 9.9 %collective-permute-start.39 = (bf16[288,1024]{1,0:T(8,128)(2,1)S(1)}, bf16[288,1024]{1,0:T(8,128)(2,1)S(1)}, u32[]{:S(2)}, u32[]{:S(2)}) collective-permute-start(bf16[288,1024]{1,0:T(8,128)(2,1)S(1)} %add_terms.28), channel_id=1, source_target_pairs={{0,4},{1,3},{4,8},{5,1},{8,12},{9,5},{12,14},{13,9},{14,10},{15,13... | collective-permute-start | bytes 1769480 | tf_op jit(solution)/shard_map/ppermute | solution.py:340
  366.6 11.3 %collective-permute-start.33 = (bf16[288,1024]{1,0:T(8,128)(2,1)S(1)}, bf16[288,1024]{1,0:T(8,128)(2,1)S(1)}, u32[]{:S(2)}, u32[]{:S(2)}) collective-permute-start(bf16[288,1024]{1,0:T(8,128)(2,1)S(1)} %add_terms.21), channel_id=1, source_target_pairs={{0,4},{1,3},{4,8},{5,1},{8,12},{9,5},{12,14},{13,9},{14,10},{15,13... | collective-permute-start | bytes 1769480 | tf_op jit(solution)/shard_map/ppermute | solution.py:340
  368.5 16.5 %collective-permute-start.13 = (bf16[288,2048]{1,0:T(8,128)(2,1)S(1)}, bf16[288,2048]{1,0:T(8,128)(2,1)S(1)}, u32[]{:S(2)}, u32[]{:S(2)}) collective-permute-start(bf16[288,2048]{1,0:T(8,128)(2,1)S(1)} %get-tuple-element.104), channel_id=1, source_target_pairs={{0,1},{1,0},{2,3},{3,2},{4,5},{5,4},{6,7},{7,6},{8,9},{9,8},{10,11... | collective-permute-start | bytes 3538952 | tf_op jit(solution)/shard_map/ppermute | solution.py:331
  371.8 12.4 %collective-permute-start.40 = (bf16[288,1024]{1,0:T(8,128)(2,1)S(1)}, bf16[288,1024]{1,0:T(8,128)(2,1)S(1)}, u32[]{:S(2)}, u32[]{:S(2)}) collective-permute-start(bf16[288,1024]{1,0:T(8,128)(2,1)S(1)} %add_terms.29), channel_id=1, source_target_pairs={{0,4},{1,3},{4,8},{5,1},{8,12},{9,5},{12,14},{13,9},{14,10},{15,13... | collective-permute-start | bytes 1769480 | tf_op jit(solution)/shard_map/ppermute | solution.py:340
  378.1 12.4 %collective-permute-start.34 = (bf16[288,1024]{1,0:T(8,128)(2,1)S(1)}, bf16[288,1024]{1,0:T(8,128)(2,1)S(1)}, u32[]{:S(2)}, u32[]{:S(2)}) collective-permute-start(bf16[288,1024]{1,0:T(8,128)(2,1)S(1)} %add_terms.22), channel_id=1, source_target_pairs={{0,4},{1,3},{4,8},{5,1},{8,12},{9,5},{12,14},{13,9},{14,10},{15,13... | collective-permute-start | bytes 1769480 | tf_op jit(solution)/shard_map/ppermute | solution.py:340
  384.4 12.4 %collective-permute-start.41 = (bf16[288,1024]{1,0:T(8,128)(2,1)S(1)}, bf16[288,1024]{1,0:T(8,128)(2,1)S(1)}, u32[]{:S(2)}, u32[]{:S(2)}) collective-permute-start(bf16[288,1024]{1,0:T(8,128)(2,1)S(1)} %add_terms.30), channel_id=1, source_target_pairs={{0,4},{1,3},{4,8},{5,1},{8,12},{9,5},{12,14},{13,9},{14,10},{15,13... | collective-permute-start | bytes 1769480 | tf_op jit(solution)/shard_map/ppermute | solution.py:340
  397.2 2.1 collective-permute-start.42
  (10 other events, 34.8 us)

commit v4 on v3

--- a/solution.py
+++ b/solution.py
@@ -298,8 +298,9 @@
     got = lax.ppermute(half_of(moe_in, 1 - core), "ex", swap)
     held = jnp.concatenate([half_of(moe_in, core), got], axis=0)
     first_weights = [gate, up]
-    due = {3: [0, 1], 4: [2, 3], 5: [4], 6: [5], 7: [6]}
-    held, gates = lax.optimization_barrier((held, gates))
+    due = {2: [0], 3: [1, 2], 4: [3], 5: [4], 6: [5], 7: [6]}
+    held, gates, down = lax.optimization_barrier((held, gates, down))
+    downs = over_kv(down)
     blocks, hiddens = [held], {}
 
     def hidden_of(step):
@@ -308,16 +309,15 @@
 
     for step in range(1, chips):
         held = lax.ppermute(held, "ex", ring)
-        if step == 2:
-            held, ups, down = lax.optimization_barrier((held, ups, down))
-            downs = over_kv(down)
+        if step == 1:
+            held, ups = lax.optimization_barrier((held, ups))
             for pair in zip(gates, ups):
                 first_weights += pair
         blocks.append(held)
         for early in due.get(step, []):
             hiddens[early] = hidden_of(early)
             held, hiddens[early] = lax.optimization_barrier((held, hiddens[early]))
-        if step == min(4, chips - 1):
+        if step == min(3, chips - 1):
             held, downs = lax.optimization_barrier((held, downs))
         blocks[step] = held
     for step in range(chips):

time: 411 us -> 436 us (1.061)
  waiting for transfers between devices: 162 us -> 205 us
  starting transfers between devices: 80.3 us -> 66.4 us
  local copies, waits for them, and re-layouts: 23.7 us -> 19 us
    ppermute x3, waiting for transfers between devices: 25.2 us -> 88.1 us  [over_kv(): lax.ppermute(part, 'kv', [(i, (i + turn) % kv) for i in range(kv)])]
    ppermute x7, waiting for transfers between devices: 43.5 us -> 22.4 us  [on_device(): held = lax.ppermute(held, 'ex', ring)]
    ppermute x7, starting transfers between devices: 25.6 us -> 9.05 us  [on_device(): held = lax.ppermute(held, 'ex', ring)]
  transfers between devices with their start and end apart: 46 -> 46, of which waited for: 25 -> 25; matrix products, arithmetic and copies ran while one was open for 6% -> 4% of each run, Pallas kernels for 30% -> 29%
where the time goes in v4:
time: 436 us; the launch traced here: 428 us
  waiting for transfers between devices  205 us (47%)
  Pallas kernels  125 us (29%)
  starting transfers between devices  66.4 us (15%)
  local copies, waits for them, and re-layouts  19 us (4%)
  other arithmetic  11.6 us (3%)
    ppermute x3, waiting for transfers between devices, over_kv(): lax.ppermute(part, 'kv', [(i, (i + turn) % kv) for i in range(kv)])  88.1 us
    pallas_call x8, Pallas kernels, expert_hidden(): pl.pallas_call(functools.partial(hidden_kernel, experts, width), in_specs...  64.4 us
    ppermute x14, waiting for transfers between devices, on_device(): running = lax.ppermute(running, 'ex', ring)  49.5 us
    pallas_call x8, Pallas kernels, expert_down(): pl.pallas_call(down_kernel, in_specs=[vmem] * (2 + len(weights)), out_spe...  33.8 us
    all_to_all x3, starting transfers between devices, over_experts(): return lax.all_to_all(part, 'ex', split_axis=0, concat_axis=0, tiled=True)  29.9 us
    ppermute x1, waiting for transfers between devices, on_device(): sent = lax.ppermute(sent, 'kv', [(i, (i + turn) % kv) for i in range(kv)])  26.8 us
    pallas_call x1, Pallas kernels, attention(): pl.pallas_call(functools.partial(attention_kernel, 1.0 / math.sqrt(HD)),...  23.9 us
    ppermute x7, waiting for transfers between devices, on_device(): held = lax.ppermute(held, 'ex', ring)  22.4 us
  transfers between devices with their start and end apart: 46, of which 25 were waited for; matrix products, arithmetic and copies ran while one was open for 4% of the time, Pallas kernels for 29%

profile of v4, /device:TPU:0, one launch (start us, length us, event | category | flops | bytes accessed | tf_op | source)
XLA Modules:
  0.0 428.4 jit_solution(6770976452575509089)
XLA Ops:
  0.0 3.8 fusion
  3.8 7.4 %all-to-all-start = ((bf16[16,128,512]{2,1,0:T(8,128)(2,1)}), bf16[16,128,512]{2,1,0:T(8,128)(2,1)S(1)}, u32[]{:S(2)}, u32[]{:S(2)}) async-start(bf16[16,128,512]{2,1,0:T(8,128)(2,1)} %fusion), calls=%async_computation | async-start | bytes 4194304 | tf_op jit(solution)/shard_map/all_to_all | solution.py:242
  11.2 6.3 %slice_bitcast_fusion = (bf16[16,128,512]{2,1,0:T(8,128)(2,1)}, bf16[16,128,512]{2,1,0:T(8,128)(2,1)}) fusion(f32[16,3,128,512]{3,2,1,0:T(8,128)} %param.17), kind=kLoop, calls=%fused_computation.8 | loop fusion | bytes 8388608 | tf_op jit(solution)/shard_map/convert_element_type | solution.py:261
  17.5 2.2 copy-done.3
  19.7 23.9 %attention.1 = f32[576,2048]{1,0:T(8,128)S(1)} custom-call(s32[2]{0:T(128)S(1)} %copy-done.5, bf16[576,2048]{1,0:T(8,128)(2,1)S(1)} %bitcast.22, f32[1,2048]{1,0:T(1,128)S(1)} %bitcast.23, bf16[3,2048,1024]{2,1,0:T(8,128)(2,1)} %bitcast.25, bf16[2,2,512,1024]{3,2,1,0:T(8,128)(2,1)S(1)} %copy-done.2, bf16[1024,2048]{1,0:T(8,128)(2,1)S(1)} %copy-done.3), custom_call_target="tpu_custom_call" | custom-call | flops 10737418240 | bytes 23855104 | tf_op jit(solution)/shard_map/attention/pallas_call | solution.py:76
  43.6 2.2 copy-done
  45.7 6.5 %all-to-all-done.refs_2_ = bf16[16,128,512]{2,1,0:T(8,128)(2,1)S(1)} async-done(((bf16[16,128,512]{2,1,0:T(8,128)(2,1)}), bf16[16,128,512]{2,1,0:T(8,128)(2,1)S(1)}, u32[]{:S(2)}, u32[]{:S(2)}) %all-to-all-start) | async-done | bytes 2097184 | tf_op jit(solution)/shard_map/all_to_all | solution.py:242
  52.2 11.3 %all-to-all-start.1 = ((bf16[16,128,512]{2,1,0:T(8,128)(2,1)}), bf16[16,128,512]{2,1,0:T(8,128)(2,1)}, u32[]{:S(2)}, u32[]{:S(2)}) async-start(bf16[16,128,512]{2,1,0:T(8,128)(2,1)} %get-tuple-element.77), calls=%async_computation.1 | async-start | bytes 4194304 | tf_op jit(solution)/shard_map/all_to_all | solution.py:242
  67.0 26.8 %collective-permute-done = bf16[288,2048]{1,0:T(8,128)(2,1)} collective-permute-done((bf16[288,2048]{1,0:T(8,128)(2,1)S(1)}, bf16[288,2048]{1,0:T(8,128)(2,1)}, u32[]{:S(2)}, u32[]{:S(2)}) %collective-permute-start) | collective-permute-done | bytes 1179680 | tf_op jit(solution)/shard_map/ppermute | solution.py:276
  93.8 4.3 %bitcast_add_fusion = f32[288,2048]{1,0:T(8,128)} fusion(bf16[288,2048]{1,0:T(8,128)(2,1)} %collective-permute-done, f32[2,288,2048]{2,1,0:T(8,128)} %bitcast.21, s32[]{:T(128)S(6)} %select_n.29, bf16[1,576,2048]{2,1,0:T(8,128)(2,1)} %param.10, s32[]{:T(128)S(6)} %select_n.28), kind=kLoop, calls=%fused_computation.2 | loop fusion | flops 2359296 | bytes 7077896 | tf_op jit(solution)/shard_map/add | solution.py:277
  98.1 6.6 %all-to-all-done.1.refs_3_ = bf16[16,128,512]{2,1,0:T(8,128)(2,1)} async-done(((bf16[16,128,512]{2,1,0:T(8,128)(2,1)}), bf16[16,128,512]{2,1,0:T(8,128)(2,1)}, u32[]{:S(2)}, u32[]{:S(2)}) %all-to-all-start.1) | async-done | bytes 2097184 | tf_op jit(solution)/shard_map/all_to_all | solution.py:242
  104.7 11.3 %all-to-all-start.2 = ((bf16[16,128,512]{2,1,0:T(8,128)(2,1)}), bf16[16,128,512]{2,1,0:T(8,128)(2,1)}, u32[]{:S(2)}, u32[]{:S(2)}) async-start(bf16[16,128,512]{2,1,0:T(8,128)(2,1)} %get-tuple-element.81), calls=%async_computation.2 | async-start | bytes 4194304 | tf_op jit(solution)/shard_map/all_to_all | solution.py:242
  121.8 2.2 concatenate.15
  126.4 39.2 %collective-permute-done.2.refs_4_ = bf16[16,128,512]{2,1,0:T(8,128)(2,1)} collective-permute-done((bf16[16,128,512]{2,1,0:T(8,128)(2,1)S(1)}, bf16[16,128,512]{2,1,0:T(8,128)(2,1)}, u32[]{:S(2)}, u32[]{:S(2)}) %collective-permute-start.2) | collective-permute-done | bytes 2097184 | tf_op jit(solution)/shard_map/ppermute | solution.py:246
  167.5 42.5 %collective-permute-done.4.refs_5_ = bf16[16,128,512]{2,1,0:T(8,128)(2,1)} collective-permute-done((bf16[16,128,512]{2,1,0:T(8,128)(2,1)}, bf16[16,128,512]{2,1,0:T(8,128)(2,1)}, u32[]{:S(2)}, u32[]{:S(2)}) %collective-permute-start.4) | collective-permute-done | bytes 2097184 | tf_op jit(solution)/shard_map/ppermute | solution.py:246
  213.4 8.0 %expert_hidden.8 = (bf16[288,1024]{1,0:T(8,128)(2,1)S(1)}, bf16[288,1024]{1,0:T(8,128)(2,1)S(1)}) custom-call(s32[1]{0:T(128)} %bitcast.11.me_ref, bf16[288,2176]{1,0:T(8,128)(2,1)S(1)} %pad_maximum_fusion.refs_0_, bf16[288,2176]{1,0:T(8,128)(2,1)S(1)} %collective-permute-done.6.refs_1_, bf16[16,128,512]{2,1,0:T(8,128)(2,1)S(1)} %all-to-all-done.refs_2_, ...), custom_call_target="tpu_custom_call" | custom-call | flops 4831838208 | bytes 11927552 | tf_op jit(solution)/shard_map/expert_hidden/pallas_call | solution.py:133
  221.4 5.8 %collective-permute-done.5.refs_0_ = bf16[288,2176]{1,0:T(8,128)(2,1)S(1)} collective-permute-done((bf16[288,2176]{1,0:T(8,128)(2,1)S(1)}, bf16[288,2176]{1,0:T(8,128)(2,1)S(1)}, u32[]{:S(2)}, u32[]{:S(2)}) %collective-permute-start.5) | collective-permute-done | bytes 1253408 | tf_op jit(solution)/shard_map/ppermute | solution.py:311
  228.9 8.1 %expert_hidden.9 = (bf16[288,1024]{1,0:T(8,128)(2,1)S(1)}, bf16[288,1024]{1,0:T(8,128)(2,1)S(1)}) custom-call(s32[1]{0:T(128)} %bitcast.11.me_ref, bf16[288,2176]{1,0:T(8,128)(2,1)S(1)} %collective-permute-done.3.refs_0_, bf16[288,2176]{1,0:T(8,128)(2,1)S(1)} %collective-permute-done.8.refs_1_, bf16[16,128,512]{2,1,0:T(8,128)(2,1)S(1)} %all-to-all-done.refs_2_, ...), custom_call_target="tpu_custom_call" | custom-call | flops 4831838208 | bytes 11927552 | tf_op jit(solution)/shard_map/expert_hidden/pallas_call | solution.py:133
  236.9 7.3 %collective-permute-done.7.refs_0_ = bf16[288,2176]{1,0:T(8,128)(2,1)S(1)} collective-permute-done((bf16[288,2176]{1,0:T(8,128)(2,1)S(1)}, bf16[288,2176]{1,0:T(8,128)(2,1)S(1)}, u32[]{:S(2)}, u32[]{:S(2)}) %collective-permute-start.7) | collective-permute-done | bytes 1253408 | tf_op jit(solution)/shard_map/ppermute | solution.py:311
  244.2 8.0 %expert_hidden.10 = (bf16[288,1024]{1,0:T(8,128)(2,1)S(1)}, bf16[288,1024]{1,0:T(8,128)(2,1)S(1)}) custom-call(s32[1]{0:T(128)} %bitcast.11.me_ref, bf16[288,2176]{1,0:T(8,128)(2,1)S(1)} %collective-permute-done.5.refs_0_, bf16[288,2176]{1,0:T(8,128)(2,1)S(1)} %collective-permute-done.9.refs_1_, bf16[16,128,512]{2,1,0:T(8,128)(2,1)S(1)} %all-to-all-done.refs_2_, ...), custom_call_target="tpu_custom_call" | custom-call | flops 4831838208 | bytes 11927552 | tf_op jit(solution)/shard_map/expert_hidden/pallas_call | solution.py:133
  252.2 6.4 %collective-permute-done.10.refs_3_ = bf16[16,128,512]{2,1,0:T(8,128)(2,1)S(1)} collective-permute-done((bf16[16,128,512]{2,1,0:T(8,128)(2,1)}, bf16[16,128,512]{2,1,0:T(8,128)(2,1)S(1)}, u32[]{:S(2)}, u32[]{:S(2)}) %collective-permute-start.10) | collective-permute-done | bytes 2097184 | tf_op jit(solution)/shard_map/ppermute | solution.py:246
  261.6 8.1 %expert_hidden.11 = (bf16[288,1024]{1,0:T(8,128)(2,1)S(1)}, bf16[288,1024]{1,0:T(8,128)(2,1)S(1)}) custom-call(s32[1]{0:T(128)} %bitcast.11.me_ref, bf16[288,2176]{1,0:T(8,128)(2,1)S(1)} %collective-permute-done.7.refs_0_, bf16[288,2176]{1,0:T(8,128)(2,1)S(1)} %collective-permute-done.13.refs_1_, bf16[16,128,512]{2,1,0:T(8,128)(2,1)S(1)} %all-to-all-done.refs_2_, ...), custom_call_target="tpu_custom_call" | custom-call | flops 4831838208 | bytes 11927552 | tf_op jit(solution)/shard_map/expert_hidden/pallas_call | solution.py:133
  269.7 6.4 %collective-permute-done.12.refs_0_ = bf16[288,2176]{1,0:T(8,128)(2,1)S(1)} collective-permute-done((bf16[288,2176]{1,0:T(8,128)(2,1)S(1)}, bf16[288,2176]{1,0:T(8,128)(2,1)S(1)}, u32[]{:S(2)}, u32[]{:S(2)}) %collective-permute-start.12) | collective-permute-done | bytes 1253408 | tf_op jit(solution)/shard_map/ppermute | solution.py:311
  276.7 4.2 expert_down.15
  282.1 8.0 %expert_hidden.12 = (bf16[288,1024]{1,0:T(8,128)(2,1)S(1)}, bf16[288,1024]{1,0:T(8,128)(2,1)S(1)}) custom-call(s32[1]{0:T(128)} %bitcast.11.me_ref, bf16[288,2176]{1,0:T(8,128)(2,1)S(1)} %collective-permute-done.12.refs_0_, bf16[288,2176]{1,0:T(8,128)(2,1)S(1)} %collective-permute-done.15.refs_1_, bf16[16,128,512]{2,1,0:T(8,128)(2,1)S(1)} %all-to-all-done.refs_2_, ...), custom_call_target="tpu_custom_call" | custom-call | flops 4831838208 | bytes 11927552 | tf_op jit(solution)/shard_map/expert_hidden/pallas_call | solution.py:133
  290.1 3.0 collective-permute-done.14.refs_0_
  293.7 4.2 expert_down.14
  300.0 4.2 expert_down.13
  305.0 8.1 %expert_hidden.13 = (bf16[288,1024]{1,0:T(8,128)(2,1)S(1)}, bf16[288,1024]{1,0:T(8,128)(2,1)S(1)}) custom-call(s32[1]{0:T(128)} %bitcast.11.me_ref, bf16[288,2176]{1,0:T(8,128)(2,1)S(1)} %collective-permute-done.14.refs_0_, bf16[288,2176]{1,0:T(8,128)(2,1)S(1)} %collective-permute-done.17.refs_1_, bf16[16,128,512]{2,1,0:T(8,128)(2,1)S(1)} %all-to-all-done.refs_2_, ...), custom_call_target="tpu_custom_call" | custom-call | flops 4831838208 | bytes 11927552 | tf_op jit(solution)/shard_map/expert_hidden/pallas_call | solution.py:133
  314.4 2.0 collective-permute-done.28.refs_2_
  318.7 4.2 expert_down.12
  323.4 6.1 %collective-permute-done.29.refs_2_ = bf16[288,1024]{1,0:T(8,128)(2,1)S(1)} collective-permute-done((bf16[288,1024]{1,0:T(8,128)(2,1)S(1)}, bf16[288,1024]{1,0:T(8,128)(2,1)S(1)}, u32[]{:S(2)}, u32[]{:S(2)}) %collective-permute-start.29) | collective-permute-done | bytes 589856 | tf_op jit(solution)/shard_map/ppermute | solution.py:340
  332.3 4.2 expert_down.11
  336.7 8.1 %expert_hidden.14 = (bf16[288,1024]{1,0:T(8,128)(2,1)S(1)}, bf16[288,1024]{1,0:T(8,128)(2,1)S(1)}) custom-call(s32[1]{0:T(128)} %bitcast.11.me_ref, bf16[288,2176]{1,0:T(8,128)(2,1)S(1)} %collective-permute-done.16.refs_0_, bf16[288,2176]{1,0:T(8,128)(2,1)S(1)} %collective-permute-done.19.refs_1_, bf16[16,128,512]{2,1,0:T(8,128)(2,1)S(1)} %all-to-all-done.refs_2_, ...), custom_call_target="tpu_custom_call" | custom-call | flops 4831838208 | bytes 11927552 | tf_op jit(solution)/shard_map/expert_hidden/pallas_call | solution.py:133
  345.3 4.0 collective-permute-done.36.refs_2_
  350.6 5.0 %collective-permute-done.30.refs_2_ = bf16[288,1024]{1,0:T(8,128)(2,1)S(1)} collective-permute-done((bf16[288,1024]{1,0:T(8,128)(2,1)S(1)}, bf16[288,1024]{1,0:T(8,128)(2,1)S(1)}, u32[]{:S(2)}, u32[]{:S(2)}) %collective-permute-start.30) | collective-permute-done | bytes 589856 | tf_op jit(solution)/shard_map/ppermute | solution.py:340
  357.0 4.9 %collective-permute-done.37.refs_2_ = bf16[288,1024]{1,0:T(8,128)(2,1)S(1)} collective-permute-done((bf16[288,1024]{1,0:T(8,128)(2,1)S(1)}, bf16[288,1024]{1,0:T(8,128)(2,1)S(1)}, u32[]{:S(2)}, u32[]{:S(2)}) %collective-permute-start.37) | collective-permute-done | bytes 589856 | tf_op jit(solution)/shard_map/ppermute | solution.py:340
  363.3 5.0 %collective-permute-done.31.refs_2_ = bf16[288,1024]{1,0:T(8,128)(2,1)S(1)} collective-permute-done((bf16[288,1024]{1,0:T(8,128)(2,1)S(1)}, bf16[288,1024]{1,0:T(8,128)(2,1)S(1)}, u32[]{:S(2)}, u32[]{:S(2)}) %collective-permute-start.31) | collective-permute-done | bytes 589856 | tf_op jit(solution)/shard_map/ppermute | solution.py:340
  369.8 4.2 expert_down.10
  374.1 8.0 %expert_hidden.15 = (bf16[288,1024]{1,0:T(8,128)(2,1)S(1)}, bf16[288,1024]{1,0:T(8,128)(2,1)S(1)}) custom-call(s32[1]{0:T(128)} %bitcast.11.me_ref, bf16[288,2176]{1,0:T(8,128)(2,1)S(1)} %collective-permute-done.18.refs_0_, bf16[288,2176]{1,0:T(8,128)(2,1)S(1)} %collective-permute-done.20.refs_1_, bf16[16,128,512]{2,1,0:T(8,128)(2,1)S(1)} %all-to-all-done.refs_2_, ...), custom_call_target="tpu_custom_call" | custom-call | flops 4831838208 | bytes 11927552 | tf_op jit(solution)/shard_map/expert_hidden/pallas_call | solution.py:133
  382.2 4.2 expert_down.9
  388.7 4.2 expert_down.8
  394.7 2.4 collective-permute-done.39.refs_2_
  398.8 4.6 %collective-permute-done.33.refs_2_ = bf16[288,1024]{1,0:T(8,128)(2,1)S(1)} collective-permute-done((bf16[288,1024]{1,0:T(8,128)(2,1)S(1)}, bf16[288,1024]{1,0:T(8,128)(2,1)S(1)}, u32[]{:S(2)}, u32[]{:S(2)}) %collective-permute-start.33) | collective-permute-done | bytes 589856 | tf_op jit(solution)/shard_map/ppermute | solution.py:340
  405.2 4.6 %collective-permute-done.40.refs_2_ = bf16[288,1024]{1,0:T(8,128)(2,1)S(1)} collective-permute-done((bf16[288,1024]{1,0:T(8,128)(2,1)S(1)}, bf16[288,1024]{1,0:T(8,128)(2,1)S(1)}, u32[]{:S(2)}, u32[]{:S(2)}) %collective-permute-start.40) | collective-permute-done | bytes 589856 | tf_op jit(solution)/shard_map/ppermute | solution.py:340
  411.5 4.6 %collective-permute-done.34.refs_2_ = bf16[288,1024]{1,0:T(8,128)(2,1)S(1)} collective-permute-done((bf16[288,1024]{1,0:T(8,128)(2,1)S(1)}, bf16[288,1024]{1,0:T(8,128)(2,1)S(1)}, u32[]{:S(2)}, u32[]{:S(2)}) %collective-permute-start.34) | collective-permute-done | bytes 589856 | tf_op jit(solution)/shard_map/ppermute | solution.py:340
  416.3 6.1 %collective-permute-done.41.refs_2_ = bf16[288,1024]{1,0:T(8,128)(2,1)S(1)} collective-permute-done((bf16[288,1024]{1,0:T(8,128)(2,1)S(1)}, bf16[288,1024]{1,0:T(8,128)(2,1)S(1)}, u32[]{:S(2)}, u32[]{:S(2)}) %collective-permute-start.41) | collective-permute-done | bytes 589856 | tf_op jit(solution)/shard_map/ppermute | solution.py:340
  424.8 3.2 fusion.2
  (118 shorter events, 51.8 us)
Async XLA Ops:
  3.8 48.5 %all-to-all-start = ((bf16[16,128,512]{2,1,0:T(8,128)(2,1)}), bf16[16,128,512]{2,1,0:T(8,128)(2,1)S(1)}, u32[]{:S(2)}, u32[]{:S(2)}) async-start(bf16[16,128,512]{2,1,0:T(8,128)(2,1)} %fusion), calls=%async_computation | async-start | bytes 4194304 | tf_op jit(solution)/shard_map/all_to_all | solution.py:242
  52.2 52.4 %all-to-all-start.1 = ((bf16[16,128,512]{2,1,0:T(8,128)(2,1)}), bf16[16,128,512]{2,1,0:T(8,128)(2,1)}, u32[]{:S(2)}, u32[]{:S(2)}) async-start(bf16[16,128,512]{2,1,0:T(8,128)(2,1)} %get-tuple-element.77), calls=%async_computation.1 | async-start | bytes 4194304 | tf_op jit(solution)/shard_map/all_to_all | solution.py:242
  65.4 28.4 %collective-permute-start = (bf16[288,2048]{1,0:T(8,128)(2,1)S(1)}, bf16[288,2048]{1,0:T(8,128)(2,1)}, u32[]{:S(2)}, u32[]{:S(2)}) collective-permute-start(bf16[288,2048]{1,0:T(8,128)(2,1)S(1)} %fusion.1), channel_id=1, source_target_pairs={{0,16},{16,0},{1,17},{17,1},{2,18},{18,2},{3,19},{19,3},{4,20},{20... | collective-permute-start | bytes 3538952 | tf_op jit(solution)/shard_map/ppermute | solution.py:276
  98.1 17.9 %copy-start.7 = (f32[1,288,8]{1,2,0:T(8,128)S(1)}, f32[1,288,8]{1,2,0:T(8,128)}, u32[]{:S(2)}) copy-start(f32[1,288,8]{1,2,0:T(8,128)} %param.19) | copy-start | bytes 27652
  98.1 18.0 %copy-start.8 = (s32[1,288,8]{1,2,0:T(8,128)S(1)}, s32[1,288,8]{1,2,0:T(8,128)}, u32[]{:S(2)}) copy-start(s32[1,288,8]{1,2,0:T(8,128)} %param.18) | copy-start | bytes 27652
  104.7 61.0 %all-to-all-start.2 = ((bf16[16,128,512]{2,1,0:T(8,128)(2,1)}), bf16[16,128,512]{2,1,0:T(8,128)(2,1)}, u32[]{:S(2)}, u32[]{:S(2)}) async-start(bf16[16,128,512]{2,1,0:T(8,128)(2,1)} %get-tuple-element.81), calls=%async_computation.2 | async-start | bytes 4194304 | tf_op jit(solution)/shard_map/all_to_all | solution.py:242
  117.1 48.6 %collective-permute-start.2 = (bf16[16,128,512]{2,1,0:T(8,128)(2,1)S(1)}, bf16[16,128,512]{2,1,0:T(8,128)(2,1)}, u32[]{:S(2)}, u32[]{:S(2)}) collective-permute-start(bf16[16,128,512]{2,1,0:T(8,128)(2,1)S(1)} %all-to-all-done.refs_2_), channel_id=1, source_target_pairs={{0,16},{16,0},{1,17},{17,1},{2,18},{18,2},{3,19},{19,3},{4,20},{20... | collective-permute-start | bytes 6291464 | tf_op jit(solution)/shard_map/ppermute | solution.py:246
  124.2 2.1 collective-permute-start.1
  124.3 85.7 %collective-permute-start.4 = (bf16[16,128,512]{2,1,0:T(8,128)(2,1)}, bf16[16,128,512]{2,1,0:T(8,128)(2,1)}, u32[]{:S(2)}, u32[]{:S(2)}) collective-permute-start(bf16[16,128,512]{2,1,0:T(8,128)(2,1)} %all-to-all-done.1.refs_3_), channel_id=1, source_target_pairs={{0,16},{16,0},{1,17},{17,1},{2,18},{18,2},{3,19},{19,3},{4,20},{20... | collective-permute-start | bytes 6291464 | tf_op jit(solution)/shard_map/ppermute | solution.py:246
  165.6 44.4 %collective-permute-start.3 = (bf16[288,2176]{1,0:T(8,128)(2,1)S(1)}, bf16[288,2176]{1,0:T(8,128)(2,1)S(1)}, u32[]{:S(2)}, u32[]{:S(2)}) collective-permute-start(bf16[288,2176]{1,0:T(8,128)(2,1)S(1)} %pad_maximum_fusion.refs_0_), channel_id=1, source_target_pairs={{0,4},{1,3},{4,8},{5,1},{8,12},{9,5},{12,14},{13,9},{14,10},{15,13... | collective-permute-start | bytes 3760136 | tf_op jit(solution)/shard_map/ppermute | solution.py:311
  167.5 45.9 %collective-permute-start.6 = (bf16[288,2176]{1,0:T(8,128)(2,1)S(1)}, bf16[288,2176]{1,0:T(8,128)(2,1)S(1)}, u32[]{:S(2)}, u32[]{:S(2)}) collective-permute-start(bf16[288,2176]{1,0:T(8,128)(2,1)S(1)} %pad_maximum_fusion.refs_0_), channel_id=1, source_target_pairs={{0,1},{1,0},{2,3},{3,2},{4,5},{5,4},{6,7},{7,6},{8,9},{9,8},{10,11... | collective-permute-start | bytes 3760136 | tf_op jit(solution)/shard_map/ppermute | solution.py:307
  210.0 17.2 %collective-permute-start.5 = (bf16[288,2176]{1,0:T(8,128)(2,1)S(1)}, bf16[288,2176]{1,0:T(8,128)(2,1)S(1)}, u32[]{:S(2)}, u32[]{:S(2)}) collective-permute-start(bf16[288,2176]{1,0:T(8,128)(2,1)S(1)} %collective-permute-done.3.refs_0_), channel_id=1, source_target_pairs={{0,4},{1,3},{4,8},{5,1},{8,12},{9,5},{12,14},{13,9},{14,10},{15,13... | collective-permute-start | bytes 3760136 | tf_op jit(solution)/shard_map/ppermute | solution.py:311
  211.9 46.8 %collective-permute-start.10 = (bf16[16,128,512]{2,1,0:T(8,128)(2,1)}, bf16[16,128,512]{2,1,0:T(8,128)(2,1)S(1)}, u32[]{:S(2)}, u32[]{:S(2)}) collective-permute-start(bf16[16,128,512]{2,1,0:T(8,128)(2,1)} %all-to-all-done.2.refs_2_), channel_id=1, source_target_pairs={{0,16},{16,0},{1,17},{17,1},{2,18},{18,2},{3,19},{19,3},{4,20},{20... | collective-permute-start | bytes 6291464 | tf_op jit(solution)/shard_map/ppermute | solution.py:246
  213.4 15.5 %collective-permute-start.8 = (bf16[288,2176]{1,0:T(8,128)(2,1)S(1)}, bf16[288,2176]{1,0:T(8,128)(2,1)S(1)}, u32[]{:S(2)}, u32[]{:S(2)}) collective-permute-start(bf16[288,2176]{1,0:T(8,128)(2,1)S(1)} %collective-permute-done.3.refs_0_), channel_id=1, source_target_pairs={{0,1},{1,0},{2,3},{3,2},{4,5},{5,4},{6,7},{7,6},{8,9},{9,8},{10,11... | collective-permute-start | bytes 3760136 | tf_op jit(solution)/shard_map/ppermute | solution.py:307
  227.2 17.0 %collective-permute-start.7 = (bf16[288,2176]{1,0:T(8,128)(2,1)S(1)}, bf16[288,2176]{1,0:T(8,128)(2,1)S(1)}, u32[]{:S(2)}, u32[]{:S(2)}) collective-permute-start(bf16[288,2176]{1,0:T(8,128)(2,1)S(1)} %collective-permute-done.5.refs_0_), channel_id=1, source_target_pairs={{0,4},{1,3},{4,8},{5,1},{8,12},{9,5},{12,14},{13,9},{14,10},{15,13... | collective-permute-start | bytes 3760136 | tf_op jit(solution)/shard_map/ppermute | solution.py:311
  228.9 15.3 %collective-permute-start.9 = (bf16[288,2176]{1,0:T(8,128)(2,1)S(1)}, bf16[288,2176]{1,0:T(8,128)(2,1)S(1)}, u32[]{:S(2)}, u32[]{:S(2)}) collective-permute-start(bf16[288,2176]{1,0:T(8,128)(2,1)S(1)} %collective-permute-done.5.refs_0_), channel_id=1, source_target_pairs={{0,1},{1,0},{2,3},{3,2},{4,5},{5,4},{6,7},{7,6},{8,9},{9,8},{10,11... | collective-permute-start | bytes 3760136 | tf_op jit(solution)/shard_map/ppermute | solution.py:307
  258.6 3.0 collective-permute-start.13
  258.7 17.4 %collective-permute-start.12 = (bf16[288,2176]{1,0:T(8,128)(2,1)S(1)}, bf16[288,2176]{1,0:T(8,128)(2,1)S(1)}, u32[]{:S(2)}, u32[]{:S(2)}) collective-permute-start(bf16[288,2176]{1,0:T(8,128)(2,1)S(1)} %collective-permute-done.7.refs_0_), channel_id=1, source_target_pairs={{0,4},{1,3},{4,8},{5,1},{8,12},{9,5},{12,14},{13,9},{14,10},{15,13... | collective-permute-start | bytes 3760136 | tf_op jit(solution)/shard_map/ppermute | solution.py:311
  276.1 6.0 %collective-permute-start.15 = (bf16[288,2176]{1,0:T(8,128)(2,1)S(1)}, bf16[288,2176]{1,0:T(8,128)(2,1)S(1)}, u32[]{:S(2)}, u32[]{:S(2)}) collective-permute-start(bf16[288,2176]{1,0:T(8,128)(2,1)S(1)} %collective-permute-done.12.refs_0_), channel_id=1, source_target_pairs={{0,1},{1,0},{2,3},{3,2},{4,5},{5,4},{6,7},{7,6},{8,9},{9,8},{10,11... | collective-permute-start | bytes 3760136 | tf_op jit(solution)/shard_map/ppermute | solution.py:307
  276.1 17.0 %collective-permute-start.14 = (bf16[288,2176]{1,0:T(8,128)(2,1)S(1)}, bf16[288,2176]{1,0:T(8,128)(2,1)S(1)}, u32[]{:S(2)}, u32[]{:S(2)}) collective-permute-start(bf16[288,2176]{1,0:T(8,128)(2,1)S(1)} %collective-permute-done.12.refs_0_), channel_id=1, source_target_pairs={{0,4},{1,3},{4,8},{5,1},{8,12},{9,5},{12,14},{13,9},{14,10},{15,13... | collective-permute-start | bytes 3760136 | tf_op jit(solution)/shard_map/ppermute | solution.py:311
  280.9 18.2 %collective-permute-start.27 = (bf16[288,2048]{1,0:T(8,128)(2,1)S(1)}, bf16[288,2048]{1,0:T(8,128)(2,1)S(1)}, u32[]{:S(2)}, u32[]{:S(2)}) collective-permute-start(bf16[288,2048]{1,0:T(8,128)(2,1)S(1)} %get-tuple-element.142), channel_id=1, source_target_pairs={{0,1},{1,0},{2,3},{3,2},{4,5},{5,4},{6,7},{7,6},{8,9},{9,8},{10,11... | collective-permute-start | bytes 3538952 | tf_op jit(solution)/shard_map/ppermute | solution.py:331
  293.1 11.9 %collective-permute-start.17 = (bf16[288,2176]{1,0:T(8,128)(2,1)S(1)}, bf16[288,2176]{1,0:T(8,128)(2,1)S(1)}, u32[]{:S(2)}, u32[]{:S(2)}) collective-permute-start(bf16[288,2176]{1,0:T(8,128)(2,1)S(1)} %collective-permute-done.14.refs_0_), channel_id=1, source_target_pairs={{0,1},{1,0},{2,3},{3,2},{4,5},{5,4},{6,7},{7,6},{8,9},{9,8},{10,11... | collective-permute-start | bytes 3760136 | tf_op jit(solution)/shard_map/ppermute | solution.py:307
  293.1 19.9 %collective-permute-start.16 = (bf16[288,2176]{1,0:T(8,128)(2,1)S(1)}, bf16[288,2176]{1,0:T(8,128)(2,1)S(1)}, u32[]{:S(2)}, u32[]{:S(2)}) collective-permute-start(bf16[288,2176]{1,0:T(8,128)(2,1)S(1)} %collective-permute-done.14.refs_0_), channel_id=1, source_target_pairs={{0,4},{1,3},{4,8},{5,1},{8,12},{9,5},{12,14},{13,9},{14,10},{15,13... | collective-permute-start | bytes 3760136 | tf_op jit(solution)/shard_map/ppermute | solution.py:311
  297.9 16.5 %collective-permute-start.26 = (bf16[288,2048]{1,0:T(8,128)(2,1)S(1)}, bf16[288,2048]{1,0:T(8,128)(2,1)S(1)}, u32[]{:S(2)}, u32[]{:S(2)}) collective-permute-start(bf16[288,2048]{1,0:T(8,128)(2,1)S(1)} %get-tuple-element.138), channel_id=1, source_target_pairs={{0,1},{1,0},{2,3},{3,2},{4,5},{5,4},{6,7},{7,6},{8,9},{9,8},{10,11... | collective-permute-start | bytes 3538952 | tf_op jit(solution)/shard_map/ppermute | solution.py:331
  299.2 17.2 %collective-permute-start.28 = (bf16[288,1024]{1,0:T(8,128)(2,1)S(1)}, bf16[288,1024]{1,0:T(8,128)(2,1)S(1)}, u32[]{:S(2)}, u32[]{:S(2)}) collective-permute-start(bf16[288,1024]{1,0:T(8,128)(2,1)S(1)} %add_terms.16), channel_id=1, source_target_pairs={{0,4},{1,3},{4,8},{5,1},{8,12},{9,5},{12,14},{13,9},{14,10},{15,13... | collective-permute-start | bytes 1769480 | tf_op jit(solution)/shard_map/ppermute | solution.py:340
  304.2 26.4 %collective-permute-start.25 = (bf16[288,2048]{1,0:T(8,128)(2,1)S(1)}, bf16[288,2048]{1,0:T(8,128)(2,1)S(1)}, u32[]{:S(2)}, u32[]{:S(2)}) collective-permute-start(bf16[288,2048]{1,0:T(8,128)(2,1)S(1)} %get-tuple-element.134), channel_id=1, source_target_pairs={{0,1},{1,0},{2,3},{3,2},{4,5},{5,4},{6,7},{7,6},{8,9},{9,8},{10,11... | collective-permute-start | bytes 3538952 | tf_op jit(solution)/shard_map/ppermute | solution.py:331
  313.0 23.5 %collective-permute-start.19 = (bf16[288,2176]{1,0:T(8,128)(2,1)S(1)}, bf16[288,2176]{1,0:T(8,128)(2,1)S(1)}, u32[]{:S(2)}, u32[]{:S(2)}) collective-permute-start(bf16[288,2176]{1,0:T(8,128)(2,1)S(1)} %collective-permute-done.16.refs_0_), channel_id=1, source_target_pairs={{0,1},{1,0},{2,3},{3,2},{4,5},{5,4},{6,7},{7,6},{8,9},{9,8},{10,11... | collective-permute-start | bytes 3760136 | tf_op jit(solution)/shard_map/ppermute | solution.py:307
  313.3 9.9 %collective-permute-start.35 = (bf16[288,1024]{1,0:T(8,128)(2,1)S(1)}, bf16[288,1024]{1,0:T(8,128)(2,1)S(1)}, u32[]{:S(2)}, u32[]{:S(2)}) collective-permute-start(bf16[288,1024]{1,0:T(8,128)(2,1)S(1)} %add_terms.24), channel_id=1, source_target_pairs={{0,4},{1,3},{4,8},{5,1},{8,12},{9,5},{12,14},{13,9},{14,10},{15,13... | collective-permute-start | bytes 1769480 | tf_op jit(solution)/shard_map/ppermute | solution.py:340
  316.6 12.9 %collective-permute-start.29 = (bf16[288,1024]{1,0:T(8,128)(2,1)S(1)}, bf16[288,1024]{1,0:T(8,128)(2,1)S(1)}, u32[]{:S(2)}, u32[]{:S(2)}) collective-permute-start(bf16[288,1024]{1,0:T(8,128)(2,1)S(1)} %add_terms.17), channel_id=1, source_target_pairs={{0,4},{1,3},{4,8},{5,1},{8,12},{9,5},{12,14},{13,9},{14,10},{15,13... | collective-permute-start | bytes 1769480 | tf_op jit(solution)/shard_map/ppermute | solution.py:340
  317.3 27.5 %collective-permute-start.18 = (bf16[288,2176]{1,0:T(8,128)(2,1)S(1)}, bf16[288,2176]{1,0:T(8,128)(2,1)S(1)}, u32[]{:S(2)}, u32[]{:S(2)}) collective-permute-start(bf16[288,2176]{1,0:T(8,128)(2,1)S(1)} %collective-permute-done.16.refs_0_), channel_id=1, source_target_pairs={{0,4},{1,3},{4,8},{5,1},{8,12},{9,5},{12,14},{13,9},{14,10},{15,13... | collective-permute-start | bytes 3760136 | tf_op jit(solution)/shard_map/ppermute | solution.py:311
  323.2 32.4 %collective-permute-start.24 = (bf16[288,2048]{1,0:T(8,128)(2,1)S(1)}, bf16[288,2048]{1,0:T(8,128)(2,1)S(1)}, u32[]{:S(2)}, u32[]{:S(2)}) collective-permute-start(bf16[288,2048]{1,0:T(8,128)(2,1)S(1)} %get-tuple-element.130), channel_id=1, source_target_pairs={{0,1},{1,0},{2,3},{3,2},{4,5},{5,4},{6,7},{7,6},{8,9},{9,8},{10,11... | collective-permute-start | bytes 3538952 | tf_op jit(solution)/shard_map/ppermute | solution.py:331
  329.5 19.7 %collective-permute-start.36 = (bf16[288,1024]{1,0:T(8,128)(2,1)S(1)}, bf16[288,1024]{1,0:T(8,128)(2,1)S(1)}, u32[]{:S(2)}, u32[]{:S(2)}) collective-permute-start(bf16[288,1024]{1,0:T(8,128)(2,1)S(1)} %add_terms.25), channel_id=1, source_target_pairs={{0,4},{1,3},{4,8},{5,1},{8,12},{9,5},{12,14},{13,9},{14,10},{15,13... | collective-permute-start | bytes 1769480 | tf_op jit(solution)/shard_map/ppermute | solution.py:340
  330.8 24.8 %collective-permute-start.30 = (bf16[288,1024]{1,0:T(8,128)(2,1)S(1)}, bf16[288,1024]{1,0:T(8,128)(2,1)S(1)}, u32[]{:S(2)}, u32[]{:S(2)}) collective-permute-start(bf16[288,1024]{1,0:T(8,128)(2,1)S(1)} %add_terms.18), channel_id=1, source_target_pairs={{0,4},{1,3},{4,8},{5,1},{8,12},{9,5},{12,14},{13,9},{14,10},{15,13... | collective-permute-start | bytes 1769480 | tf_op jit(solution)/shard_map/ppermute | solution.py:340
  336.6 31.6 %collective-permute-start.23 = (bf16[288,2048]{1,0:T(8,128)(2,1)S(1)}, bf16[288,2048]{1,0:T(8,128)(2,1)S(1)}, u32[]{:S(2)}, u32[]{:S(2)}) collective-permute-start(bf16[288,2048]{1,0:T(8,128)(2,1)S(1)} %get-tuple-element.126), channel_id=1, source_target_pairs={{0,1},{1,0},{2,3},{3,2},{4,5},{5,4},{6,7},{7,6},{8,9},{9,8},{10,11... | collective-permute-start | bytes 3538952 | tf_op jit(solution)/shard_map/ppermute | solution.py:331
  344.7 29.4 %collective-permute-start.20 = (bf16[288,2176]{1,0:T(8,128)(2,1)S(1)}, bf16[288,2176]{1,0:T(8,128)(2,1)S(1)}, u32[]{:S(2)}, u32[]{:S(2)}) collective-permute-start(bf16[288,2176]{1,0:T(8,128)(2,1)S(1)} %collective-permute-done.18.refs_0_), channel_id=1, source_target_pairs={{0,1},{1,0},{2,3},{3,2},{4,5},{5,4},{6,7},{7,6},{8,9},{9,8},{10,11... | collective-permute-start | bytes 3760136 | tf_op jit(solution)/shard_map/ppermute | solution.py:307
  349.5 12.4 %collective-permute-start.37 = (bf16[288,1024]{1,0:T(8,128)(2,1)S(1)}, bf16[288,1024]{1,0:T(8,128)(2,1)S(1)}, u32[]{:S(2)}, u32[]{:S(2)}) collective-permute-start(bf16[288,1024]{1,0:T(8,128)(2,1)S(1)} %add_terms.26), channel_id=1, source_target_pairs={{0,4},{1,3},{4,8},{5,1},{8,12},{9,5},{12,14},{13,9},{14,10},{15,13... | collective-permute-start | bytes 1769480 | tf_op jit(solution)/shard_map/ppermute | solution.py:340
  355.8 12.4 %collective-permute-start.31 = (bf16[288,1024]{1,0:T(8,128)(2,1)S(1)}, bf16[288,1024]{1,0:T(8,128)(2,1)S(1)}, u32[]{:S(2)}, u32[]{:S(2)}) collective-permute-start(bf16[288,1024]{1,0:T(8,128)(2,1)S(1)} %add_terms.19), channel_id=1, source_target_pairs={{0,4},{1,3},{4,8},{5,1},{8,12},{9,5},{12,14},{13,9},{14,10},{15,13... | collective-permute-start | bytes 1769480 | tf_op jit(solution)/shard_map/ppermute | solution.py:340
  362.1 24.8 %collective-permute-start.38 = (bf16[288,1024]{1,0:T(8,128)(2,1)S(1)}, bf16[288,1024]{1,0:T(8,128)(2,1)S(1)}, u32[]{:S(2)}, u32[]{:S(2)}) collective-permute-start(bf16[288,1024]{1,0:T(8,128)(2,1)S(1)} %add_terms.27), channel_id=1, source_target_pairs={{0,4},{1,3},{4,8},{5,1},{8,12},{9,5},{12,14},{13,9},{14,10},{15,13... | collective-permute-start | bytes 1769480 | tf_op jit(solution)/shard_map/ppermute | solution.py:340
  368.4 24.5 %collective-permute-start.32 = (bf16[288,1024]{1,0:T(8,128)(2,1)S(1)}, bf16[288,1024]{1,0:T(8,128)(2,1)S(1)}, u32[]{:S(2)}, u32[]{:S(2)}) collective-permute-start(bf16[288,1024]{1,0:T(8,128)(2,1)S(1)} %add_terms.20), channel_id=1, source_target_pairs={{0,4},{1,3},{4,8},{5,1},{8,12},{9,5},{12,14},{13,9},{14,10},{15,13... | collective-permute-start | bytes 1769480 | tf_op jit(solution)/shard_map/ppermute | solution.py:340
  374.0 18.9 %collective-permute-start.22 = (bf16[288,2048]{1,0:T(8,128)(2,1)S(1)}, bf16[288,2048]{1,0:T(8,128)(2,1)S(1)}, u32[]{:S(2)}, u32[]{:S(2)}) collective-permute-start(bf16[288,2048]{1,0:T(8,128)(2,1)S(1)} %get-tuple-element.122), channel_id=1, source_target_pairs={{0,1},{1,0},{2,3},{3,2},{4,5},{5,4},{6,7},{7,6},{8,9},{9,8},{10,11... | collective-permute-start | bytes 3538952 | tf_op jit(solution)/shard_map/ppermute | solution.py:331
  386.4 17.0 %collective-permute-start.21 = (bf16[288,2048]{1,0:T(8,128)(2,1)S(1)}, bf16[288,2048]{1,0:T(8,128)(2,1)S(1)}, u32[]{:S(2)}, u32[]{:S(2)}) collective-permute-start(bf16[288,2048]{1,0:T(8,128)(2,1)S(1)} %get-tuple-element.118), channel_id=1, source_target_pairs={{0,1},{1,0},{2,3},{3,2},{4,5},{5,4},{6,7},{7,6},{8,9},{9,8},{10,11... | collective-permute-start | bytes 3538952 | tf_op jit(solution)/shard_map/ppermute | solution.py:331
  387.2 9.9 %collective-permute-start.39 = (bf16[288,1024]{1,0:T(8,128)(2,1)S(1)}, bf16[288,1024]{1,0:T(8,128)(2,1)S(1)}, u32[]{:S(2)}, u32[]{:S(2)}) collective-permute-start(bf16[288,1024]{1,0:T(8,128)(2,1)S(1)} %add_terms.28), channel_id=1, source_target_pairs={{0,4},{1,3},{4,8},{5,1},{8,12},{9,5},{12,14},{13,9},{14,10},{15,13... | collective-permute-start | bytes 1769480 | tf_op jit(solution)/shard_map/ppermute | solution.py:340
  393.2 10.3 %collective-permute-start.33 = (bf16[288,1024]{1,0:T(8,128)(2,1)S(1)}, bf16[288,1024]{1,0:T(8,128)(2,1)S(1)}, u32[]{:S(2)}, u32[]{:S(2)}) collective-permute-start(bf16[288,1024]{1,0:T(8,128)(2,1)S(1)} %add_terms.21), channel_id=1, source_target_pairs={{0,4},{1,3},{4,8},{5,1},{8,12},{9,5},{12,14},{13,9},{14,10},{15,13... | collective-permute-start | bytes 1769480 | tf_op jit(solution)/shard_map/ppermute | solution.py:340
  394.7 16.8 %collective-permute-start.11 = (bf16[288,2048]{1,0:T(8,128)(2,1)S(1)}, bf16[288,2048]{1,0:T(8,128)(2,1)S(1)}, u32[]{:S(2)}, u32[]{:S(2)}) collective-permute-start(bf16[288,2048]{1,0:T(8,128)(2,1)S(1)} %get-tuple-element.101), channel_id=1, source_target_pairs={{0,1},{1,0},{2,3},{3,2},{4,5},{5,4},{6,7},{7,6},{8,9},{9,8},{10,11... | collective-permute-start | bytes 3538952 | tf_op jit(solution)/shard_map/ppermute | solution.py:331
  397.3 12.4 %collective-permute-start.40 = (bf16[288,1024]{1,0:T(8,128)(2,1)S(1)}, bf16[288,1024]{1,0:T(8,128)(2,1)S(1)}, u32[]{:S(2)}, u32[]{:S(2)}) collective-permute-start(bf16[288,1024]{1,0:T(8,128)(2,1)S(1)} %add_terms.29), channel_id=1, source_target_pairs={{0,4},{1,3},{4,8},{5,1},{8,12},{9,5},{12,14},{13,9},{14,10},{15,13... | collective-permute-start | bytes 1769480 | tf_op jit(solution)/shard_map/ppermute | solution.py:340
  403.7 12.4 %collective-permute-start.34 = (bf16[288,1024]{1,0:T(8,128)(2,1)S(1)}, bf16[288,1024]{1,0:T(8,128)(2,1)S(1)}, u32[]{:S(2)}, u32[]{:S(2)}) collective-permute-start(bf16[288,1024]{1,0:T(8,128)(2,1)S(1)} %add_terms.22), channel_id=1, source_target_pairs={{0,4},{1,3},{4,8},{5,1},{8,12},{9,5},{12,14},{13,9},{14,10},{15,13... | collective-permute-start | bytes 1769480 | tf_op jit(solution)/shard_map/ppermute | solution.py:340
  410.0 12.4 %collective-permute-start.41 = (bf16[288,1024]{1,0:T(8,128)(2,1)S(1)}, bf16[288,1024]{1,0:T(8,128)(2,1)S(1)}, u32[]{:S(2)}, u32[]{:S(2)}) collective-permute-start(bf16[288,1024]{1,0:T(8,128)(2,1)S(1)} %add_terms.30), channel_id=1, source_target_pairs={{0,4},{1,3},{4,8},{5,1},{8,12},{9,5},{12,14},{13,9},{14,10},{15,13... | collective-permute-start | bytes 1769480 | tf_op jit(solution)/shard_map/ppermute | solution.py:340
  422.7 2.1 collective-permute-start.42
  (8 other events, 37.2 us)
